TPU v7x, 256 devices: a whole 4x4x8 slice. The times are simulated.
256 devices in a mesh: rows: 128 (over x, y, z_hi, core), rep: 2 (over z_lo).
Axes of the slice: x: 4, y: 4, z: 8 (z_hi: 4, z_lo: 2; z = z_hi * 2 + z_lo), core: 2. Of those that a mesh axis runs over, the one named last changes fastest.
Arguments:
- features: bfloat16 [32768, 128], P('rows'), may hold values from -6 to 6
- node_order: int32 [32768], P('rows'), may hold values from 0 to 32767, as said below
- tile_vals: bfloat16 [49152, 128, 128], P(('rows', 'rep')), may hold values from -0.0546875 to 0.0546875
- tile_row: int32 [49152], P(('rows', 'rep')), may hold values from 0 to 255, as said below
- tile_col: int32 [49152], P(('rows', 'rep')), may hold values from 0 to 255, as said below
- tile_count: int32 [256], P(('rows', 'rep')), may hold values from 48 to 192, as said below
- weight: bfloat16 [128, 256], replicated, may hold values from -0.5 to 0.5
- bias: float32 [256], replicated, may hold values from -3 to 3
- cotangent: bfloat16 [32768, 256], P('rows'), may hold values from -6 to 6
Outputs:
- activations: bfloat16 [32768, 256], P('rows')
- weight_grad: float32 [128, 256], replicated
- bias_grad: float32 [256], replicated
Inputs may be any that keep to these rules, and one draw needn't show every extreme that they name: `node_order`: positions c * 256 to c * 256 + 255 hold each of the node numbers c * 256 to c * 256 + 255 once. `tile_row`: slots d * 192 to d * 192 + 191 belong to device d = i * 2 + j (i along rows, j along rep); each of them names a row-block from i * 2 to i * 2 + 1. `tile_col`: A slot of device d = i * 2 + j names a column-block c * 2 + j + e for any node group c and any e from 0 to 0; slots may repeat a pair of row-block and column-block. Only the first tile_count[d] slots of device d are live; some device has exactly 192 and some other exactly 48.
All inputs are finite; a program needn't handle non-finite values.
Results may differ from a plain program's by a relative error of at most 0.0056.
Values may be sent and summed in bfloat16 or wider, within the bound.
No kernel may reach another device: no remote copies, remote signals or barrier semaphores. Data moves between devices by JAX's collectives and lax.ppermute only.
A program may use at most 128 MiB of HBM per device.

v0:
```python
import jax
import jax.numpy as jnp
from jax import lax
from jax.sharding import Mesh
from jax.sharding import PartitionSpec as P

ROWS = ("rows_0", "rows_1", "rows_2", "rows_3")
ROWS_REP = ("rows_0", "rows_1", "rows_2", "rows_3", "rep")


def from_everyone(array, axis):
    copies = jnp.broadcast_to(array, (lax.axis_size(axis), *array.shape))
    return lax.all_to_all(copies, axis, split_axis=0, concat_axis=0, tiled=True)


def laid_out(pieces, dim):
    shape = list(pieces.shape[1:])
    shape[dim] *= pieces.shape[0]
    return jnp.moveaxis(pieces, 0, dim).reshape(shape)


def gathered_by_axis(array, axes, dim):
    far, near = axes
    leading = from_everyone(array, far)
    pieces = jnp.swapaxes(from_everyone(leading, near), 0, 1)
    return laid_out(pieces.reshape(-1, *array.shape), dim)


def of_everyone(array, axis):
    return from_everyone(array, axis).sum(axis=0)


def padded_to(lines, count):
    spare = -len(lines) % count
    return jnp.pad(lines, [(0, spare)] + [(0, 0)] * (lines.ndim - 1))


def in_blocks(array, dim, count):
    shape = array.shape
    pieces = array.reshape(*shape[:dim], count, shape[dim] // count, *shape[dim + 1 :])
    return jnp.moveaxis(pieces, dim, 0)


def summed_on_arrival(array, axis, dim):
    pieces = in_blocks(array, dim, lax.axis_size(axis))
    arrived = lax.all_to_all(pieces, axis, split_axis=0, concat_axis=0, tiled=True)
    return arrived.sum(axis=0)


def summed_rows(array, axes, dim):
    far, near = axes
    pieces = in_blocks(array, dim, lax.axis_size(far))
    nearer = summed_on_arrival(pieces, near, dim + 1)
    arrived = lax.all_to_all(nearer, far, split_axis=0, concat_axis=0, tiled=True)
    return arrived.sum(axis=0)


def total_of(array, axes):
    padded = padded_to(array, lax.axis_size(axes[0]) * lax.axis_size(axes[1]))
    whole = gathered_by_axis(summed_rows(padded, axes, 0), axes, 0)
    return lax.slice_in_dim(whole, 0, len(array)).reshape(array.shape)


def in_one(arrays, axis):
    ends = [0]
    for a in arrays:
        ends.append(ends[-1] + a.size)
    total = total_of(jnp.concatenate([a.ravel() for a in arrays]), axis)
    return tuple((total[b:e].reshape(a.shape) for a, b, e in zip(arrays, ends, ends[1:])))


def silu_slope(pre_act):
    sigma = jax.nn.sigmoid(pre_act)
    return sigma * (1.0 + pre_act * (1.0 - sigma))


def body(features, node_order, tile_vals, tile_row, tile_col, tile_count, weight, bias, cotangent):
    row_index = lax.axis_index(ROWS)
    replica = lax.axis_index("rep")
    replicas = lax.axis_size("rep")
    nodes_dev = features.shape[0]
    feat_width = features.shape[1]
    tile_size = tile_vals.shape[1]
    slot_count = tile_vals.shape[0]
    row_blocks = nodes_dev // tile_size
    half_blocks = row_blocks // replicas
    local_order = node_order - row_index * nodes_dev
    reordered = features[local_order]
    own_half = lax.dynamic_slice_in_dim(
        reordered, replica * half_blocks * tile_size, half_blocks * tile_size, 0
    )
    gathered = gathered_by_axis(own_half, (("rows_0", "rows_1", "rows_2"), "rows_3"), 0)
    sources = gathered.reshape(-1, tile_size, feat_width)
    position = tile_col // row_blocks * half_blocks + tile_col % row_blocks - replica * half_blocks
    picked = sources[position]
    products = jnp.einsum("tij,tjf->tif", tile_vals, picked, preferred_element_type=jnp.float32)
    local_rows = tile_row - row_index * row_blocks
    live_mask = (jnp.arange(slot_count, dtype=jnp.int32) < tile_count[0]).astype(jnp.float32)
    select = (local_rows[:, None] == jnp.arange(row_blocks, dtype=jnp.int32)[None, :]).astype(
        jnp.float32
    )
    select = select * live_mask[:, None]
    partial_value = jnp.einsum("tk,tif->kif", select, products, precision=lax.Precision.HIGHEST)
    partial_value = partial_value.reshape(nodes_dev, feat_width)
    grad_reordered = cotangent[local_order]
    grad_scale = float(nodes_dev * lax.axis_size(ROWS)) ** (-0.5)
    full_total = of_everyone(partial_value, "rep")
    hidden = full_total.astype(jnp.bfloat16)
    pre_act = jnp.dot(hidden, weight, preferred_element_type=jnp.float32) + bias
    activated = jax.nn.silu(pre_act).astype(jnp.bfloat16)
    scaled = (grad_reordered.astype(jnp.float32) * silu_slope(pre_act)).astype(jnp.bfloat16)
    weight_term = lax.dot_general(
        hidden, scaled, (((0,), (0,)), ((), ())), preferred_element_type=jnp.float32
    )
    bias_term = jnp.sum(scaled.astype(jnp.float32), axis=0)
    weight_grad, bias_grad = in_one(
        (weight_term, bias_term), (("rows_0", "rows_1", "rows_2"), "rows_3")
    )
    activations = jnp.zeros_like(activated).at[local_order].set(activated)
    return (activations, weight_grad * grad_scale, bias_grad * grad_scale)


def solution(mesh):
    finer = Mesh(
        mesh.devices.reshape(4, 4, 4, 2, mesh.shape["rep"]),
        ("rows_0", "rows_1", "rows_2", "rows_3", "rep"),
    )
    return jax.shard_map(
        body,
        mesh=finer,
        in_specs=(
            P(ROWS, None),
            P(ROWS),
            P(ROWS_REP, None, None),
            P(ROWS_REP),
            P(ROWS_REP),
            P(ROWS_REP),
            P(),
            P(),
            P(ROWS, None),
        ),
        out_specs=(P(ROWS, None), P(), P()),
        check_vma=False,
    )
```

profile of v0, /device:TPU:1, one launch (start us, length us, event | category | flops | bytes accessed | tf_op | source)
XLA Modules:
  0.0 186.4 jit_solution(13818349121481118274)
XLA Ops:
  0.7 0.7 compare_select_fusion.2
  1.4 1.6 gather_fusion
  3.0 1.9 broadcast_in_dim.32
  4.9 15.1 %all-to-all-start = ((bf16[64,128,128]{2,1,0:T(8,128)(2,1)}), bf16[64,128,128]{2,1,0:T(8,128)(2,1)S(1)}, u32[]{:S(2)}, u32[]{:S(2)}) async-start(bf16[64,128,128]{2,1,0:T(8,128)(2,1)} %broadcast_in_dim.32), calls=%async_computation | async-start | bytes 4194304 | tf_op jit(solution)/shard_map/all_to_all | solution.py:13
  20.7 50.8 %all-to-all-done = bf16[64,128,128]{2,1,0:T(8,128)(2,1)S(1)} async-done(((bf16[64,128,128]{2,1,0:T(8,128)(2,1)}), bf16[64,128,128]{2,1,0:T(8,128)(2,1)S(1)}, u32[]{:S(2)}, u32[]{:S(2)}) %all-to-all-start) | async-done | bytes 2097184 | tf_op jit(solution)/shard_map/all_to_all | solution.py:13
  71.5 1.0 broadcast_in_dim.33
  72.6 10.0 %all_to_all.43 = bf16[2,64,128,128]{3,2,1,0:T(8,128)(2,1)S(1)} all-to-all(bf16[2,64,128,128]{3,2,1,0:T(8,128)(2,1)S(1)} %broadcast_in_dim.33), channel_id=1, replica_groups=mesh['rows_0'=4,'rows_1'=4,'rows_2'=4,'rows_3'=2,'rep'=2] {'rows_3'}, dimensions={0} | all-to-all | bytes 8388608 | tf_op jit(solution)/shard_map/all_to_all | solution.py:13
  82.5 2.2 %copy.24 = bf16[2,64,128,128]{3,2,0,1:T(8,128)(2,1)} copy(bf16[2,64,128,128]{3,2,1,0:T(8,128)(2,1)S(1)} %all_to_all.43) | data formatting | bytes 8388608 | tf_op jit(solution)/shard_map/all_to_all | solution.py:13
  84.8 10.2 %gather_fusion.1 = bf16[192,128,128]{2,1,0:T(8,128)(2,1)} fusion(bf16[128,128,128]{2,1,0:T(8,128)(2,1)} %bitcast.26, s32[1024]{0:T(1024)S(1)} %pad_clamp_fusion), kind=kCustom, calls=%fused_computation.1 | custom fusion | bytes 12583680 | tf_op jit(solution)/shard_map/gather | solution.py:95
  94.9 13.7 %convolution_bitcast_fusion = f32[192,128,128]{1,2,0:T(8,128)} fusion(bf16[192,128,128]{2,1,0:T(8,128)(2,1)} %gather_fusion.1, bf16[192,128,128]{2,1,0:T(8,128)(2,1)} %param.11), kind=kOutput, calls=%fused_computation.4 | convolution fusion | flops 805306368 | bytes 25165824 | tf_op jit(solution)/shard_map/tij,tjf->tif/dot_general | solution.py:96
  108.7 12.7 %copy.26 = f32[192,128,128]{2,0,1:T(8,128)} copy(f32[192,128,128]{1,2,0:T(8,128)} %convolution_bitcast_fusion) | data formatting | bytes 25165824 | tf_op jit(solution)/shard_map/tij,tjf->tif/dot_general | solution.py:96
  121.3 8.9 %fusion.5 = f32[2,128,128]{2,0,1:T(2,128)S(1)} fusion(f32[192,128,128]{2,0,1:T(8,128)} %copy.26, f32[192]{0:T(256)S(1)} %compare_convert_fusion, s32[192]{0:T(256)S(1)} %broadcast_subtract_fusion), kind=kOutput, calls=%fused_computation.24 | convolution fusion | flops 75498240 | bytes 12715520 | tf_op jit(solution)/shard_map/tk,tif->kif/dot_general | solution.py:103
  130.3 0.7 broadcast_in_dim.35
  131.0 3.4 %all-to-all-start.2 = ((f32[2,256,128]{2,1,0:T(8,128)}), f32[2,256,128]{2,1,0:T(8,128)S(1)}, u32[]{:S(2)}, u32[]{:S(2)}) async-start(f32[2,256,128]{2,1,0:T(8,128)} %broadcast_in_dim.35), calls=%async_computation.2 | async-start | bytes 524288 | tf_op jit(solution)/shard_map/all_to_all | solution.py:13
  134.4 1.2 gather_fusion.2
  135.6 3.7 %all-to-all-done.2 = f32[2,256,128]{2,1,0:T(8,128)S(1)} async-done(((f32[2,256,128]{2,1,0:T(8,128)}), f32[2,256,128]{2,1,0:T(8,128)S(1)}, u32[]{:S(2)}, u32[]{:S(2)}) %all-to-all-start.2) | async-done | bytes 262176 | tf_op jit(solution)/shard_map/all_to_all | solution.py:13
  140.3 4.7 %all_to_all.44 = f32[2,64,258]{2,1,0:T(8,128)S(1)} all-to-all(f32[2,64,258]{2,1,0:T(8,128)S(1)} %copy.28), channel_id=1, replica_groups=mesh['rows_0'=4,'rows_1'=4,'rows_2'=4,'rows_3'=2,'rep'=2] {'rows_3'}, dimensions={0} | all-to-all | bytes 264192 | tf_op jit(solution)/shard_map/all_to_all | solution.py:46
  145.1 16.2 %all_to_all.45 = f32[64,1,258]{2,1,0:T(1,128)S(1)} all-to-all(f32[64,1,258]{2,1,0:T(1,128)S(1)} %all_to_all.31), channel_id=1, replica_groups=mesh['rows_0'=4,'rows_1'=4,'rows_2'=4,'rows_3'=2,'rep'=2] {'rows_0','row..., dimensions={0} | all-to-all | bytes 132096 | tf_op jit(solution)/shard_map/all_to_all | solution.py:54
  161.4 0.7 broadcast_in_dim.36
  162.1 4.6 %all-to-all-start.5 = ((f32[64,1,258]{2,1,0:T(1,128)}), f32[64,1,258]{2,1,0:T(1,128)S(1)}, u32[]{:S(2)}, u32[]{:S(2)}) async-start(f32[64,1,258]{2,1,0:T(1,128)} %broadcast_in_dim.36), calls=%async_computation.5 | async-start | bytes 196608 | tf_op jit(solution)/shard_map/all_to_all | solution.py:13
  166.7 2.1 %scatter_custom_fusion = bf16[256,256]{1,0:T(8,128)(2,1)} fusion(s32[256]{0:T(256)S(1)} %compare_select_fusion.2, f32[256,256]{1,0:T(8,128)S(1)} %get-tuple-element.5, f32[]{:T(128)} %constant.68.clone.1, bf16[]{:T(256)} %constant.53.clone.1), kind=kCustom, calls=%fused_computation.13 | custom fusion | flops 327680 | bytes 393222 | tf_op jit(solution)/shard_map/scatter | solution.py:119
  168.9 9.1 %all-to-all-done.5 = f32[64,1,258]{2,1,0:T(1,128)S(1)} async-done(((f32[64,1,258]{2,1,0:T(1,128)}), f32[64,1,258]{2,1,0:T(1,128)S(1)}, u32[]{:S(2)}, u32[]{:S(2)}) %all-to-all-start.5) | async-done | bytes 66080 | tf_op jit(solution)/shard_map/all_to_all | solution.py:13
  178.1 6.3 %all_to_all.46 = f32[2,64,258]{2,1,0:T(8,128)S(1)} all-to-all(f32[2,64,258]{2,1,0:T(8,128)S(1)} %broadcast_in_dim.37), channel_id=1, replica_groups=mesh['rows_0'=4,'rows_1'=4,'rows_2'=4,'rows_3'=2,'rep'=2] {'rows_3'}, dimensions={0} | all-to-all | bytes 264192 | tf_op jit(solution)/shard_map/all_to_all | solution.py:13
  185.1 0.7 slice_multiply_fusion
  (33 shorter events, 2.5 us)
Async XLA Ops:
  0.6 133.8 %copy-start = (bf16[256,256]{1,0:T(8,128)(2,1)S(1)}, bf16[256,256]{1,0:T(8,128)(2,1)}, u32[]{:S(2)}) copy-start(bf16[256,256]{1,0:T(8,128)(2,1)} %param.17) | copy-start | bytes 393220
  0.6 20.0 %copy-start.1 = (s32[192]{0:T(256)S(1)}, s32[192]{0:T(256)}, u32[]{:S(2)}) copy-start(s32[192]{0:T(256)} %param.13) | copy-start | bytes 2308
  0.7 20.0 %copy-start.2 = (s32[192]{0:T(256)S(1)}, s32[192]{0:T(256)}, u32[]{:S(2)}) copy-start(s32[192]{0:T(256)} %param.12) | copy-start | bytes 2308
  4.9 66.7 %all-to-all-start = ((bf16[64,128,128]{2,1,0:T(8,128)(2,1)}), bf16[64,128,128]{2,1,0:T(8,128)(2,1)S(1)}, u32[]{:S(2)}, u32[]{:S(2)}) async-start(bf16[64,128,128]{2,1,0:T(8,128)(2,1)} %broadcast_in_dim.32), calls=%async_computation | async-start | bytes 4194304 | tf_op jit(solution)/shard_map/all_to_all | solution.py:13
  121.3 18.0 %copy-start.3 = (bf16[128,256]{1,0:T(8,128)(2,1)S(1)}, bf16[128,256]{1,0:T(8,128)(2,1)}, u32[]{:S(2)}) copy-start(bf16[128,256]{1,0:T(8,128)(2,1)} %param.15) | copy-start | bytes 196612
  121.3 18.0 %copy-start.4 = (f32[256]{0:T(256)S(1)}, f32[256]{0:T(256)}, u32[]{:S(2)}) copy-start(f32[256]{0:T(256)} %param.16) | copy-start | bytes 3076
  131.0 8.3 %all-to-all-start.2 = ((f32[2,256,128]{2,1,0:T(8,128)}), f32[2,256,128]{2,1,0:T(8,128)S(1)}, u32[]{:S(2)}, u32[]{:S(2)}) async-start(f32[2,256,128]{2,1,0:T(8,128)} %broadcast_in_dim.35), calls=%async_computation.2 | async-start | bytes 524288 | tf_op jit(solution)/shard_map/all_to_all | solution.py:13
  162.1 15.9 %all-to-all-start.5 = ((f32[64,1,258]{2,1,0:T(1,128)}), f32[64,1,258]{2,1,0:T(1,128)S(1)}, u32[]{:S(2)}, u32[]{:S(2)}) async-start(f32[64,1,258]{2,1,0:T(1,128)} %broadcast_in_dim.36), calls=%async_computation.5 | async-start | bytes 196608 | tf_op jit(solution)/shard_map/all_to_all | solution.py:13
where the time goes:
time: 187 us; the launch traced here: 186 us
  waiting for transfers between devices  63.7 us (34%)
  blocking collectives  37.2 us (20%)
  local copies, waits for them, and re-layouts  33.4 us (18%)
  starting transfers between devices  23.2 us (12%)
  matrix products  23.1 us (12%)
  other arithmetic  4.27 us (2%)
    all_to_all x3, waiting for transfers between devices, from_everyone(): return lax.all_to_all(copies, axis, split_axis=0, concat_axis=0, tiled=True)  63.7 us
    all_to_all x3, starting transfers between devices, from_everyone(): return lax.all_to_all(copies, axis, split_axis=0, concat_axis=0, tiled=True)  23.2 us
    all_to_all x2, blocking collectives, from_everyone(): return lax.all_to_all(copies, axis, split_axis=0, concat_axis=0, tiled=True)  16.3 us
    all_to_all x1, blocking collectives, summed_rows(): lax.all_to_all(nearer, far, split_axis=0, concat_axis=0, tiled=True)  16.2 us
    dot_general x1, matrix products, body(): jnp.einsum('tij,tjf->tif', tile_vals, picked, preferred_element_type=jnp....  13.7 us
    dot_general x1, local copies, waits for them, and re-layouts, body(): jnp.einsum('tij,tjf->tif', tile_vals, picked, preferred_element_type=jnp....  12.7 us
    gather x1, local copies, waits for them, and re-layouts, body(): picked = sources[position]  10.2 us
    dot_general x1, matrix products, body(): jnp.einsum('tk,tif->kif', select, products, precision=lax.Precision.HIGHEST)  8.92 us
  transfers between devices with their start and end apart: 3, of which 3 were waited for; matrix products, arithmetic and copies ran while one was open for 2% of the time, Pallas kernels for 0%

commit v1 on v0

v1 whole, which is shorter than its diff:
```python
import itertools

import jax
import jax.numpy as jnp
from jax import lax
from jax.experimental import pallas as pl
from jax.experimental.pallas import tpu as pltpu
from jax.sharding import Mesh
from jax.sharding import PartitionSpec as P

ROWS = ("x", "y", "z", "c")
ROWS_REP = ("x", "y", "z", "c", "rep")
GROUP = 4

SMEM = pl.BlockSpec(memory_space=pltpu.SMEM)
VMEM = pl.BlockSpec(memory_space=pltpu.VMEM)


def swap(value, axis, step):
    n = lax.axis_size(axis)
    return lax.ppermute(value, axis, [(i, i ^ step) for i in range(n)])


def swap_plane(value, step, last):
    nx, ny = lax.axis_size("x"), lax.axis_size("y")
    pairs = []
    for x, y, c in itertools.product(range(nx), range(ny), range(2)):
        along_x = (c == 1) != last
        x2, y2 = (x ^ step, y) if along_x else (x, y ^ step)
        pairs.append(((x * ny + y) * 2 + c, (x2 * ny + y2) * 2 + c))
    return lax.ppermute(value, ("x", "y", "c"), pairs)


def reorder_kernel(place, order, features, own):
    half = own.shape[0]
    nodes = features.shape[0]
    wanted = order[pl.ds(place[1], 1), :] & (nodes - 1)
    pick = (lax.broadcasted_iota(jnp.int32, (nodes, half), 0) == wanted).astype(jnp.bfloat16)
    own[...] = lax.dot_general(
        pick, features[...], (((0,), (0,)), ((), ())), preferred_element_type=jnp.float32
    ).astype(jnp.bfloat16)


def tiles_kernel(position, row, count, tiles, *refs):
    pieces, (out, sources) = refs[:-2], refs[-2:]
    size = tiles.shape[1]
    live = count[0]
    blocks = pieces[0].shape[0]

    def place_block(b, _):
        for k, piece in enumerate(pieces):
            sources[k * blocks + b] = piece[b]
        return 0

    lax.fori_loop(0, blocks, place_block, 0)

    def step(g, total):
        lefts, rights = [], []
        for k in range(GROUP):
            t = g * GROUP + k
            block = sources[position[t]]
            zero = jnp.zeros_like(block)
            first = jnp.where((row[t] == 0) & (t < live), block, zero)
            second = jnp.where((row[t] == 1) & (t < live), block, zero)
            lefts.append(tiles[t])
            rights.append(jnp.concatenate([first, second], axis=1))
        return total + jnp.dot(
            jnp.concatenate(lefts, axis=1),
            jnp.concatenate(rights, axis=0),
            preferred_element_type=jnp.float32,
        )

    total = lax.fori_loop(
        0, (live + GROUP - 1) // GROUP, step, jnp.zeros((size, 2 * size), jnp.float32)
    )
    out[:size] = total[:, :size]
    out[size:] = total[:, size:]


def dense_kernel(place, order, mine, theirs, weight, bias, cotangent, act, keep, send):
    nodes = mine.shape[0]
    half = weight.shape[1] // 2
    part = weight.shape[0] // 2
    hidden = (mine[...] + theirs[...]).astype(jnp.bfloat16)
    where = jnp.concatenate([order[0:1], order[1:2]], axis=1) & (nodes - 1)
    put = (lax.broadcasted_iota(jnp.int32, (nodes, nodes), 0) == where).astype(jnp.bfloat16)
    hidden = jnp.dot(put, hidden, preferred_element_type=jnp.float32).astype(jnp.bfloat16)
    pre_act = jnp.dot(hidden, weight[...], preferred_element_type=jnp.float32) + bias[...]
    sigma = 1.0 / (1.0 + jnp.exp(-pre_act))
    act[...] = (pre_act * sigma).astype(jnp.bfloat16)
    slope = sigma * (1.0 + pre_act * (1.0 - sigma))
    scaled = (cotangent[...].astype(jnp.float32) * slope).astype(jnp.bfloat16)
    total = lax.dot_general(
        hidden, scaled, (((0,), (0,)), ((), ())), preferred_element_type=jnp.float32
    )
    column = jnp.sum(scaled.astype(jnp.float32), axis=0, keepdims=True)
    upper = place[1] == 1
    total = jnp.where(upper, total[:, half:], total[:, :half])
    column = jnp.where(upper, column[:, half:], column[:, :half])
    lower = place[0] == 0
    keep[:part] = jnp.where(lower, total[:part], total[part:])
    send[:part] = jnp.where(lower, total[part:], total[:part])
    keep[part:] = jnp.broadcast_to(column, (8, half))
    send[part:] = jnp.broadcast_to(column, (8, half))


def finish_kernel(scale, place, own, core, rep, both, weight_grad, bias_grad):
    part = own.shape[0] - 8
    half = own.shape[1]
    c, j = place[0], place[1]
    for piece, c2, j2 in ((own, c, j), (core, 1 - c, j), (rep, c, 1 - j), (both, 1 - c, 1 - j)):
        rows = pl.ds(pl.multiple_of(c2 * part, part), part)
        columns = pl.ds(pl.multiple_of(j2 * half, half), half)
        weight_grad[rows, columns] = piece[:part] * scale
    for piece, j2 in ((own, j), (rep, 1 - j)):
        columns = pl.ds(pl.multiple_of(j2 * half, half), half)
        bias_grad[:, columns] = piece[part : part + 1] * scale


def gathered(own):
    v = own[None]
    v = jnp.concatenate([v, swap(v, "z", 1)])
    v = jnp.concatenate([v, swap(v, "z", 3)])
    v = jnp.concatenate([v] + [swap_plane(v, s, False) for s in (1, 2, 3)])
    pieces = [v] + [swap_plane(v, s, True) for s in (1, 2, 3)]
    return pieces + [swap(p, "c", 1) for p in pieces]


def positions(tile_col, me):
    source = tile_col >> 1
    away = source ^ me
    x, y, z, c = (away >> 5) & 3, (away >> 3) & 3, (away >> 1) & 3, away & 1
    flip = (source & 1) == 1
    last, plane = jnp.where(flip, y, x), jnp.where(flip, x, y)
    return c * 64 + last * 16 + plane * 4 + (z ^ (z >> 1))


def body(features, node_order, tile_vals, tile_row, tile_col, tile_count, weight, bias, cotangent):
    nodes, width = features.shape
    slots, size, _ = tile_vals.shape
    hid = weight.shape[1]
    half, part = hid // 2, width // 2
    me = lax.axis_index(ROWS)
    place = jnp.stack([lax.axis_index("c"), lax.axis_index("rep")]).astype(jnp.int32)
    order = node_order.reshape(2, nodes // 2)
    own = pl.pallas_call(
        reorder_kernel,
        out_shape=jax.ShapeDtypeStruct((nodes // 2, width), jnp.bfloat16),
        in_specs=[SMEM, VMEM, VMEM],
        out_specs=VMEM,
        compiler_params=pltpu.CompilerParams(vmem_limit_bytes=4 * 2**20),
    )(place, order, features)
    pieces = gathered(own)
    blocks = len(pieces) * pieces[0].shape[0]
    mine = pl.pallas_call(
        tiles_kernel,
        out_shape=jax.ShapeDtypeStruct((nodes, width), jnp.float32),
        in_specs=[SMEM] * 3 + [VMEM] * (1 + len(pieces)),
        out_specs=VMEM,
        scratch_shapes=[pltpu.VMEM((blocks, size, width), jnp.bfloat16)],
        compiler_params=pltpu.CompilerParams(vmem_limit_bytes=32 * 2**20),
    )(positions(tile_col, me), tile_row & 1, tile_count, tile_vals, *pieces)
    theirs = swap(mine, "rep", 1)
    act, keep, send = pl.pallas_call(
        dense_kernel,
        out_shape=(
            jax.ShapeDtypeStruct((nodes, hid), jnp.bfloat16),
            jax.ShapeDtypeStruct((part + 8, half), jnp.float32),
            jax.ShapeDtypeStruct((part + 8, half), jnp.float32),
        ),
        in_specs=[SMEM] + [VMEM] * 6,
        out_specs=(VMEM,) * 3,
        compiler_params=pltpu.CompilerParams(vmem_limit_bytes=16 * 2**20),
    )(place, order, mine, theirs, weight, bias.reshape(1, hid), cotangent)
    total = keep + swap(send, "c", 1)
    for axis in ("z", "y", "x"):
        for step in (1, 3):
            total = total + swap(total, axis, step)
    scale = float(nodes * lax.axis_size(ROWS)) ** -0.5
    weight_grad, bias_grad = pl.pallas_call(
        lambda *refs: finish_kernel(scale, *refs),
        out_shape=(
            jax.ShapeDtypeStruct((width, hid), jnp.float32),
            jax.ShapeDtypeStruct((1, hid), jnp.float32),
        ),
        in_specs=[SMEM] + [VMEM] * 4,
        out_specs=(VMEM,) * 2,
        compiler_params=pltpu.CompilerParams(vmem_limit_bytes=4 * 2**20),
    )(
        place,
        total,
        swap(total, "c", 1),
        swap(total, "rep", 1),
        swap(total, ("c", "rep"), 3),
    )
    return act, weight_grad, bias_grad.reshape(hid)


def solution(mesh):
    finer = Mesh(mesh.devices.reshape(4, 4, 4, 2, mesh.shape["rep"]), ROWS_REP)
    return jax.shard_map(
        body,
        mesh=finer,
        in_specs=(
            P(ROWS, None),
            P(ROWS),
            P(ROWS_REP, None, None),
            P(ROWS_REP),
            P(ROWS_REP),
            P(ROWS_REP),
            P(),
            P(),
            P(ROWS, None),
        ),
        out_specs=(P(ROWS, None), P(), P()),
        check_vma=False,
    )
```

time: 187 us -> 104 us (0.56)
  blocking collectives: 37.2 us -> 0 us
  local copies, waits for them, and re-layouts: 33.4 us -> 4.4 us
  starting transfers between devices: 23.2 us -> 48.8 us
  waiting for transfers between devices: 63.7 us -> 40.1 us
  matrix products: 23.1 us -> 0 us
  Pallas kernels: 0 us -> 8.91 us
  other arithmetic: 4.27 us -> 0.85 us
    all_to_all x3 -> x0, waiting for transfers between devices: 63.7 us -> none  [from_everyone(): return lax.all_to_all(copies, axis, split_axis=0, concat_axis=0, tiled=True)]
    ppermute x0 -> x23, starting transfers between devices: none -> 48.8 us  [the longest x17 41.5 us: swap(): return lax.ppermute(value, axis, [(i, i ^ step) for i in range(n)])]
    ppermute x0 -> x23, waiting for transfers between devices: none -> 40.1 us  [the longest x17 28.9 us: swap(): return lax.ppermute(value, axis, [(i, i ^ step) for i in range(n)])]
    all_to_all x4 -> x0, blocking collectives: 37.2 us -> none  [the longest x2 16.3 us: from_everyone(): return lax.all_to_all(copies, axis, split_axis=0, concat_axis=0, tiled=True)]
    all_to_all x3 -> x0, starting transfers between devices: 23.2 us -> none  [from_everyone(): return lax.all_to_all(copies, axis, split_axis=0, concat_axis=0, tiled=True)]
    dot_general x4 -> x0, matrix products: 23.1 us -> none  [the longest x1 13.7 us: body(): jnp.einsum('tij,tjf->tif', tile_vals, picked, preferred_element_type=jnp....]
    gather x3 -> x0, local copies, waits for them, and re-layouts: 12.9 us -> none  [the longest x1 10.2 us: body(): picked = sources[position]]
    dot_general x2 -> x0, local copies, waits for them, and re-layouts: 12.7 us -> none  [the longest x1 12.7 us: body(): jnp.einsum('tij,tjf->tif', tile_vals, picked, preferred_element_type=jnp....]
  transfers between devices with their start and end apart: 3 -> 23, of which waited for: 3 -> 16; matrix products, arithmetic and copies ran while one was open for 2% -> 1% of each run, Pallas kernels for 0% -> 0%
where the time goes in v1:
time: 104 us
  starting transfers between devices  48.8 us (47%)
  waiting for transfers between devices  40.1 us (39%)
  Pallas kernels  8.91 us (9%)
  local copies, waits for them, and re-layouts  4.4 us (4%)
  between operations  1.41 us (1%)
    ppermute x17, starting transfers between devices, swap(): return lax.ppermute(value, axis, [(i, i ^ step) for i in range(n)])  41.5 us
    ppermute x17, waiting for transfers between devices, swap(): return lax.ppermute(value, axis, [(i, i ^ step) for i in range(n)])  28.9 us
    ppermute x6, waiting for transfers between devices, swap_plane(): return lax.ppermute(value, ('x', 'y', 'c'), pairs)  11.2 us
    ppermute x6, starting transfers between devices, swap_plane(): return lax.ppermute(value, ('x', 'y', 'c'), pairs)  7.34 us
    pallas_call x1, Pallas kernels, body(): pl.pallas_call(tiles_kernel, out_shape=jax.ShapeDtypeStruct((nodes, width...  5.36 us
    unnamed x19, local copies, waits for them, and re-layouts  4.38 us
  transfers between devices with their start and end apart: 23, of which 16 were waited for; matrix products, arithmetic and copies ran while one was open for 1% of the time, Pallas kernels for 0%

profile of v1, /device:TPU:1, one launch (start us, length us, event | category | flops | bytes accessed | tf_op | source)
XLA Modules:
  0.0 104.5 jit_solution(14360777049020728067)
XLA Ops:
  3.0 3.9 %collective-permute-start = (bf16[1,128,128]{2,1,0:T(8,128)(2,1)S(1)}, bf16[1,128,128]{2,1,0:T(8,128)(2,1)S(1)}, u32[]{:S(2)}, u32[]{:S(2)}) collective-permute-start(bf16[1,128,128]{2,1,0:T(8,128)(2,1)S(1)} %bitcast.7), channel_id=1, source_target_pairs={{0,4},{4,0},{8,12},{12,8},{1,5},{5,1},{9,13},{13,9},{2,6},{6,2},{1... | collective-permute-start | bytes 98312 | tf_op jit(solution)/shard_map/ppermute | solution.py:21
  8.2 5.5 %collective-permute-start.1 = (bf16[2,128,128]{2,1,0:T(8,128)(2,1)S(1)}, bf16[2,128,128]{2,1,0:T(8,128)(2,1)S(1)}, u32[]{:S(2)}, u32[]{:S(2)}) collective-permute-start(bf16[2,128,128]{2,1,0:T(8,128)(2,1)S(1)} %pad_maximum_fusion.1), channel_id=1, source_target_pairs={{0,12},{4,8},{8,4},{12,0},{1,13},{5,9},{9,5},{13,1},{2,14},{6,10},... | collective-permute-start | bytes 196616 | tf_op jit(solution)/shard_map/ppermute | solution.py:21
  13.7 1.8 %collective-permute-done.1 = bf16[2,128,128]{2,1,0:T(8,128)(2,1)S(1)} collective-permute-done((bf16[2,128,128]{2,1,0:T(8,128)(2,1)S(1)}, bf16[2,128,128]{2,1,0:T(8,128)(2,1)S(1)}, u32[]{:S(2)}, u32[]{:S(2)}) %collective-permute-start.1) | collective-permute-done | bytes 65568 | tf_op jit(solution)/shard_map/ppermute | solution.py:21
  16.8 1.8 %collective-permute-start.4 = (bf16[4,128,128]{2,1,0:T(8,128)(2,1)S(1)}, bf16[4,128,128]{2,1,0:T(8,128)(2,1)S(1)}, u32[]{:S(2)}, u32[]{:S(2)}) collective-permute-start(bf16[4,128,128]{2,1,0:T(8,128)(2,1)S(1)} %pad_maximum_fusion), channel_id=1, source_target_pairs={{0,48},{2,194},{16,32},{18,210},{32,16},{34,226},{48,0},{50,242},{... | collective-permute-start | bytes 393224 | tf_op jit(solution)/shard_map/ppermute | solution.py:31
  19.4 4.5 %collective-permute-done.3 = bf16[4,128,128]{2,1,0:T(8,128)(2,1)S(1)} collective-permute-done((bf16[4,128,128]{2,1,0:T(8,128)(2,1)S(1)}, bf16[4,128,128]{2,1,0:T(8,128)(2,1)S(1)}, u32[]{:S(2)}, u32[]{:S(2)}) %collective-permute-start.3) | collective-permute-done | bytes 131104 | tf_op jit(solution)/shard_map/ppermute | solution.py:31
  24.0 2.8 %collective-permute-start.7 = (bf16[16,128,128]{2,1,0:T(8,128)(2,1)S(1)}, bf16[16,128,128]{2,1,0:T(8,128)(2,1)S(1)}, u32[]{:S(2)}, u32[]{:S(2)}) collective-permute-start(bf16[16,128,128]{2,1,0:T(8,128)(2,1)S(1)} %constant_dynamic-update-slice_fusion.refs_0_), channel_id=1, source_target_pairs={{0,192},{2,50},{16,208},{18,34},{32,224},{34,18},{48,240},{50,2},{... | collective-permute-start | bytes 1572872 | tf_op jit(solution)/shard_map/ppermute | solution.py:31
  27.5 5.3 %collective-permute-start.8 = (bf16[16,128,128]{2,1,0:T(8,128)(2,1)S(1)}, bf16[16,128,128]{2,1,0:T(8,128)(2,1)S(1)}, u32[]{:S(2)}, u32[]{:S(2)}) collective-permute-start(bf16[16,128,128]{2,1,0:T(8,128)(2,1)S(1)} %constant_dynamic-update-slice_fusion.refs_0_), channel_id=1, source_target_pairs={{0,2},{2,0},{1,3},{3,1},{4,6},{6,4},{5,7},{7,5},{8,10},{10,8},{9,1... | collective-permute-start | bytes 1572872 | tf_op jit(solution)/shard_map/ppermute | solution.py:21
  32.7 6.6 %collective-permute-done.7.refs_3_ = bf16[16,128,128]{2,1,0:T(8,128)(2,1)S(1)} collective-permute-done((bf16[16,128,128]{2,1,0:T(8,128)(2,1)S(1)}, bf16[16,128,128]{2,1,0:T(8,128)(2,1)S(1)}, u32[]{:S(2)}, u32[]{:S(2)}) %collective-permute-start.7) | collective-permute-done | bytes 524320 | tf_op jit(solution)/shard_map/ppermute | solution.py:31
  39.3 5.3 %collective-permute-start.11 = (bf16[16,128,128]{2,1,0:T(8,128)(2,1)S(1)}, bf16[16,128,128]{2,1,0:T(8,128)(2,1)S(1)}, u32[]{:S(2)}, u32[]{:S(2)}) collective-permute-start(bf16[16,128,128]{2,1,0:T(8,128)(2,1)S(1)} %collective-permute-done.7.refs_3_), channel_id=1, source_target_pairs={{0,2},{2,0},{1,3},{3,1},{4,6},{6,4},{5,7},{7,5},{8,10},{10,8},{9,1... | collective-permute-start | bytes 1572872 | tf_op jit(solution)/shard_map/ppermute | solution.py:21
  47.8 2.8 %copy-done = bf16[192,128,128]{2,1,0:T(8,128)(2,1)S(1)} copy-done((bf16[192,128,128]{2,1,0:T(8,128)(2,1)S(1)}, bf16[192,128,128]{2,1,0:T(8,128)(2,1)}, u32[]{:S(2)}) %copy-start) | copy-done | bytes 6291480
  50.6 5.4 %shard_map.113.mine = f32[256,128]{1,0:T(8,128)S(1)} custom-call(s32[192]{0:T(256)S(1)} %get-tuple-element.13.position, s32[192]{0:T(256)S(1)} %get-tuple-element.14.row, s32[1]{0:T(128)S(6)} %copy.17.count, bf16[192,128,128]{2,1,0:T(8,128)(2,1)S(1)} %copy-done, bf16[16,128,128]{2,1,0:T(8,128)(2,1)S(1)} %constant_dynamic-update-slice_fusion.refs_0_, ...), custom_call_target="tpu_custom_call" | custom-call | tf_op jit(solution)/shard_map/pallas_call | solution.py:155
  56.0 4.1 %collective-permute-start.12 = (f32[256,128]{1,0:T(8,128)S(1)}, f32[256,128]{1,0:T(8,128)S(1)}, u32[]{:S(2)}, u32[]{:S(2)}) collective-permute-start(f32[256,128]{1,0:T(8,128)S(1)} %shard_map.113.mine), channel_id=1, source_target_pairs={{0,1},{1,0},{2,3},{3,2},{4,5},{5,4},{6,7},{7,6},{8,9},{9,8},{10,11... | collective-permute-start | bytes 393224 | tf_op jit(solution)/shard_map/ppermute | solution.py:21
  60.0 2.4 %collective-permute-done.12.theirs = f32[256,128]{1,0:T(8,128)S(1)} collective-permute-done((f32[256,128]{1,0:T(8,128)S(1)}, f32[256,128]{1,0:T(8,128)S(1)}, u32[]{:S(2)}, u32[]{:S(2)}) %collective-permute-start.12) | collective-permute-done | bytes 131104 | tf_op jit(solution)/shard_map/ppermute | solution.py:21
  62.4 1.6 %shard_map.114 = (bf16[256,256]{1,0:T(8,128)(2,1)}, f32[72,128]{1,0:T(8,128)S(1)}, f32[72,128]{1,0:T(8,128)S(1)}) custom-call(s32[2]{0:T(128)S(1)} %pad_add_fusion.place.refs_0_, s32[2,128]{1,0:T(2,128)S(1)} %bitcast.11, f32[256,128]{1,0:T(8,128)S(1)} %shard_map.113.mine, f32[256,128]{1,0:T(8,128)S(1)} %collective-permute-done.12.theirs, ...), custom_call_target="tpu_custom_call" | custom-call | tf_op jit(solution)/shard_map/pallas_call | solution.py:164
  64.0 4.7 %collective-permute-start.13 = (f32[72,128]{1,0:T(8,128)S(1)}, f32[72,128]{1,0:T(8,128)S(1)}, u32[]{:S(2)}, u32[]{:S(2)}) collective-permute-start(f32[72,128]{1,0:T(8,128)S(1)} %get-tuple-element.10), channel_id=1, source_target_pairs={{0,2},{2,0},{1,3},{3,1},{4,6},{6,4},{5,7},{7,5},{8,10},{10,8},{9,1... | collective-permute-start | bytes 110600 | tf_op jit(solution)/shard_map/ppermute | solution.py:21
  70.8 3.3 %collective-permute-done.14 = f32[72,128]{1,0:T(8,128)S(1)} collective-permute-done((f32[72,128]{1,0:T(8,128)S(1)}, f32[72,128]{1,0:T(8,128)S(1)}, u32[]{:S(2)}, u32[]{:S(2)}) %collective-permute-start.14) | collective-permute-done | bytes 36896 | tf_op jit(solution)/shard_map/ppermute | solution.py:21
  74.1 1.8 %collective-permute-start.15 = (f32[72,128]{1,0:T(8,128)S(1)}, f32[72,128]{1,0:T(8,128)S(1)}, u32[]{:S(2)}, u32[]{:S(2)}) collective-permute-start(f32[72,128]{1,0:T(8,128)S(1)} %add.46), channel_id=1, source_target_pairs={{0,12},{4,8},{8,4},{12,0},{1,13},{5,9},{9,5},{13,1},{2,14},{6,10},... | collective-permute-start | bytes 110600 | tf_op jit(solution)/shard_map/ppermute | solution.py:21
  75.9 3.2 %collective-permute-done.15 = f32[72,128]{1,0:T(8,128)S(1)} collective-permute-done((f32[72,128]{1,0:T(8,128)S(1)}, f32[72,128]{1,0:T(8,128)S(1)}, u32[]{:S(2)}, u32[]{:S(2)}) %collective-permute-start.15) | collective-permute-done | bytes 36896 | tf_op jit(solution)/shard_map/ppermute | solution.py:21
  79.1 2.8 %collective-permute-done.16 = f32[72,128]{1,0:T(8,128)S(1)} collective-permute-done((f32[72,128]{1,0:T(8,128)S(1)}, f32[72,128]{1,0:T(8,128)S(1)}, u32[]{:S(2)}, u32[]{:S(2)}) %collective-permute-start.16) | collective-permute-done | bytes 36896 | tf_op jit(solution)/shard_map/ppermute | solution.py:21
  81.9 4.0 %collective-permute-done.17 = f32[72,128]{1,0:T(8,128)S(1)} collective-permute-done((f32[72,128]{1,0:T(8,128)S(1)}, f32[72,128]{1,0:T(8,128)S(1)}, u32[]{:S(2)}, u32[]{:S(2)}) %collective-permute-start.17) | collective-permute-done | bytes 36896 | tf_op jit(solution)/shard_map/ppermute | solution.py:21
  85.9 2.8 %collective-permute-done.18 = f32[72,128]{1,0:T(8,128)S(1)} collective-permute-done((f32[72,128]{1,0:T(8,128)S(1)}, f32[72,128]{1,0:T(8,128)S(1)}, u32[]{:S(2)}, u32[]{:S(2)}) %collective-permute-start.18) | collective-permute-done | bytes 36896 | tf_op jit(solution)/shard_map/ppermute | solution.py:21
  89.8 2.9 %collective-permute-done.19 = f32[72,128]{1,0:T(8,128)S(1)} collective-permute-done((f32[72,128]{1,0:T(8,128)S(1)}, f32[72,128]{1,0:T(8,128)S(1)}, u32[]{:S(2)}, u32[]{:S(2)}) %collective-permute-start.19) | collective-permute-done | bytes 36896 | tf_op jit(solution)/shard_map/ppermute | solution.py:21
  92.8 7.0 %collective-permute-start.22 = (f32[72,128]{1,0:T(8,128)S(1)}, f32[72,128]{1,0:T(8,128)S(1)}, u32[]{:S(2)}, u32[]{:S(2)}) collective-permute-start(f32[72,128]{1,0:T(8,128)S(1)} %add.51.refs_1_), channel_id=1, source_target_pairs={{0,3},{1,2},{2,1},{3,0},{4,7},{5,6},{6,5},{7,4},{8,11},{9,10},{10,... | collective-permute-start | bytes 110600 | tf_op jit(solution)/shard_map/ppermute | solution.py:21
  101.4 1.8 %collective-permute-done.21.refs_3_ = f32[72,128]{1,0:T(8,128)S(1)} collective-permute-done((f32[72,128]{1,0:T(8,128)S(1)}, f32[72,128]{1,0:T(8,128)S(1)}, u32[]{:S(2)}, u32[]{:S(2)}) %collective-permute-start.21) | collective-permute-done | bytes 36896 | tf_op jit(solution)/shard_map/ppermute | solution.py:21
  (57 shorter events, 15.1 us)
Async XLA Ops:
  0.6 61.8 %copy-start.1 = (bf16[256,256]{1,0:T(8,128)(2,1)S(1)}, bf16[256,256]{1,0:T(8,128)(2,1)}, u32[]{:S(2)}) copy-start(bf16[256,256]{1,0:T(8,128)(2,1)} %cotangent.1) | copy-start | bytes 393220
  3.0 5.2 %collective-permute-start = (bf16[1,128,128]{2,1,0:T(8,128)(2,1)S(1)}, bf16[1,128,128]{2,1,0:T(8,128)(2,1)S(1)}, u32[]{:S(2)}, u32[]{:S(2)}) collective-permute-start(bf16[1,128,128]{2,1,0:T(8,128)(2,1)S(1)} %bitcast.7), channel_id=1, source_target_pairs={{0,4},{4,0},{8,12},{12,8},{1,5},{5,1},{9,13},{13,9},{2,6},{6,2},{1... | collective-permute-start | bytes 98312 | tf_op jit(solution)/shard_map/ppermute | solution.py:21
  8.2 7.2 %collective-permute-start.1 = (bf16[2,128,128]{2,1,0:T(8,128)(2,1)S(1)}, bf16[2,128,128]{2,1,0:T(8,128)(2,1)S(1)}, u32[]{:S(2)}, u32[]{:S(2)}) collective-permute-start(bf16[2,128,128]{2,1,0:T(8,128)(2,1)S(1)} %pad_maximum_fusion.1), channel_id=1, source_target_pairs={{0,12},{4,8},{8,4},{12,0},{1,13},{5,9},{9,5},{13,1},{2,14},{6,10},... | collective-permute-start | bytes 196616 | tf_op jit(solution)/shard_map/ppermute | solution.py:21
  15.5 3.9 %collective-permute-start.2 = (bf16[4,128,128]{2,1,0:T(8,128)(2,1)S(1)}, bf16[4,128,128]{2,1,0:T(8,128)(2,1)S(1)}, u32[]{:S(2)}, u32[]{:S(2)}) collective-permute-start(bf16[4,128,128]{2,1,0:T(8,128)(2,1)S(1)} %pad_maximum_fusion), channel_id=1, source_target_pairs={{0,16},{2,66},{16,0},{18,82},{32,48},{34,98},{48,32},{50,114},{64,... | collective-permute-start | bytes 393224 | tf_op jit(solution)/shard_map/ppermute | solution.py:31
  16.8 7.2 %collective-permute-start.4 = (bf16[4,128,128]{2,1,0:T(8,128)(2,1)S(1)}, bf16[4,128,128]{2,1,0:T(8,128)(2,1)S(1)}, u32[]{:S(2)}, u32[]{:S(2)}) collective-permute-start(bf16[4,128,128]{2,1,0:T(8,128)(2,1)S(1)} %pad_maximum_fusion), channel_id=1, source_target_pairs={{0,48},{2,194},{16,32},{18,210},{32,16},{34,226},{48,0},{50,242},{... | collective-permute-start | bytes 393224 | tf_op jit(solution)/shard_map/ppermute | solution.py:31
  18.6 5.3 %collective-permute-start.3 = (bf16[4,128,128]{2,1,0:T(8,128)(2,1)S(1)}, bf16[4,128,128]{2,1,0:T(8,128)(2,1)S(1)}, u32[]{:S(2)}, u32[]{:S(2)}) collective-permute-start(bf16[4,128,128]{2,1,0:T(8,128)(2,1)S(1)} %pad_maximum_fusion), channel_id=1, source_target_pairs={{0,32},{2,130},{16,48},{18,146},{32,0},{34,162},{48,16},{50,178},{... | collective-permute-start | bytes 393224 | tf_op jit(solution)/shard_map/ppermute | solution.py:31
  24.0 15.4 %collective-permute-start.7 = (bf16[16,128,128]{2,1,0:T(8,128)(2,1)S(1)}, bf16[16,128,128]{2,1,0:T(8,128)(2,1)S(1)}, u32[]{:S(2)}, u32[]{:S(2)}) collective-permute-start(bf16[16,128,128]{2,1,0:T(8,128)(2,1)S(1)} %constant_dynamic-update-slice_fusion.refs_0_), channel_id=1, source_target_pairs={{0,192},{2,50},{16,208},{18,34},{32,224},{34,18},{48,240},{50,2},{... | collective-permute-start | bytes 1572872 | tf_op jit(solution)/shard_map/ppermute | solution.py:31
  26.8 17.9 %collective-permute-start.6 = (bf16[16,128,128]{2,1,0:T(8,128)(2,1)S(1)}, bf16[16,128,128]{2,1,0:T(8,128)(2,1)S(1)}, u32[]{:S(2)}, u32[]{:S(2)}) collective-permute-start(bf16[16,128,128]{2,1,0:T(8,128)(2,1)S(1)} %constant_dynamic-update-slice_fusion.refs_0_), channel_id=1, source_target_pairs={{0,128},{2,34},{16,144},{18,50},{32,160},{34,2},{48,176},{50,18},{... | collective-permute-start | bytes 1572872 | tf_op jit(solution)/shard_map/ppermute | solution.py:31
  27.1 17.5 %collective-permute-start.5 = (bf16[16,128,128]{2,1,0:T(8,128)(2,1)S(1)}, bf16[16,128,128]{2,1,0:T(8,128)(2,1)S(1)}, u32[]{:S(2)}, u32[]{:S(2)}) collective-permute-start(bf16[16,128,128]{2,1,0:T(8,128)(2,1)S(1)} %constant_dynamic-update-slice_fusion.refs_0_), channel_id=1, source_target_pairs={{0,64},{2,18},{16,80},{18,2},{32,96},{34,50},{48,112},{50,34},{64,... | collective-permute-start | bytes 1572872 | tf_op jit(solution)/shard_map/ppermute | solution.py:31
  27.5 19.4 %collective-permute-start.8 = (bf16[16,128,128]{2,1,0:T(8,128)(2,1)S(1)}, bf16[16,128,128]{2,1,0:T(8,128)(2,1)S(1)}, u32[]{:S(2)}, u32[]{:S(2)}) collective-permute-start(bf16[16,128,128]{2,1,0:T(8,128)(2,1)S(1)} %constant_dynamic-update-slice_fusion.refs_0_), channel_id=1, source_target_pairs={{0,2},{2,0},{1,3},{3,1},{4,6},{6,4},{5,7},{7,5},{8,10},{10,8},{9,1... | collective-permute-start | bytes 1572872 | tf_op jit(solution)/shard_map/ppermute | solution.py:21
  39.3 7.6 %collective-permute-start.11 = (bf16[16,128,128]{2,1,0:T(8,128)(2,1)S(1)}, bf16[16,128,128]{2,1,0:T(8,128)(2,1)S(1)}, u32[]{:S(2)}, u32[]{:S(2)}) collective-permute-start(bf16[16,128,128]{2,1,0:T(8,128)(2,1)S(1)} %collective-permute-done.7.refs_3_), channel_id=1, source_target_pairs={{0,2},{2,0},{1,3},{3,1},{4,6},{6,4},{5,7},{7,5},{8,10},{10,8},{9,1... | collective-permute-start | bytes 1572872 | tf_op jit(solution)/shard_map/ppermute | solution.py:21
  44.6 2.4 %collective-permute-start.10 = (bf16[16,128,128]{2,1,0:T(8,128)(2,1)S(1)}, bf16[16,128,128]{2,1,0:T(8,128)(2,1)}, u32[]{:S(2)}, u32[]{:S(2)}) collective-permute-start(bf16[16,128,128]{2,1,0:T(8,128)(2,1)S(1)} %collective-permute-done.6.refs_2_), channel_id=1, source_target_pairs={{0,2},{2,0},{1,3},{3,1},{4,6},{6,4},{5,7},{7,5},{8,10},{10,8},{9,1... | collective-permute-start | bytes 1572872 | tf_op jit(solution)/shard_map/ppermute | solution.py:21
  44.7 3.2 %collective-permute-start.9 = (bf16[16,128,128]{2,1,0:T(8,128)(2,1)S(1)}, bf16[16,128,128]{2,1,0:T(8,128)(2,1)}, u32[]{:S(2)}, u32[]{:S(2)}) collective-permute-start(bf16[16,128,128]{2,1,0:T(8,128)(2,1)S(1)} %collective-permute-done.5.refs_1_), channel_id=1, source_target_pairs={{0,2},{2,0},{1,3},{3,1},{4,6},{6,4},{5,7},{7,5},{8,10},{10,8},{9,1... | collective-permute-start | bytes 1572872 | tf_op jit(solution)/shard_map/ppermute | solution.py:21
  56.0 6.4 %collective-permute-start.12 = (f32[256,128]{1,0:T(8,128)S(1)}, f32[256,128]{1,0:T(8,128)S(1)}, u32[]{:S(2)}, u32[]{:S(2)}) collective-permute-start(f32[256,128]{1,0:T(8,128)S(1)} %shard_map.113.mine), channel_id=1, source_target_pairs={{0,1},{1,0},{2,3},{3,2},{4,5},{5,4},{6,7},{7,6},{8,9},{9,8},{10,11... | collective-permute-start | bytes 393224 | tf_op jit(solution)/shard_map/ppermute | solution.py:21
  64.0 5.5 %collective-permute-start.13 = (f32[72,128]{1,0:T(8,128)S(1)}, f32[72,128]{1,0:T(8,128)S(1)}, u32[]{:S(2)}, u32[]{:S(2)}) collective-permute-start(f32[72,128]{1,0:T(8,128)S(1)} %get-tuple-element.10), channel_id=1, source_target_pairs={{0,2},{2,0},{1,3},{3,1},{4,6},{6,4},{5,7},{7,5},{8,10},{10,8},{9,1... | collective-permute-start | bytes 110600 | tf_op jit(solution)/shard_map/ppermute | solution.py:21
  69.6 4.6 %collective-permute-start.14 = (f32[72,128]{1,0:T(8,128)S(1)}, f32[72,128]{1,0:T(8,128)S(1)}, u32[]{:S(2)}, u32[]{:S(2)}) collective-permute-start(f32[72,128]{1,0:T(8,128)S(1)} %add.45), channel_id=1, source_target_pairs={{0,4},{4,0},{8,12},{12,8},{1,5},{5,1},{9,13},{13,9},{2,6},{6,2},{1... | collective-permute-start | bytes 110600 | tf_op jit(solution)/shard_map/ppermute | solution.py:21
  74.1 5.0 %collective-permute-start.15 = (f32[72,128]{1,0:T(8,128)S(1)}, f32[72,128]{1,0:T(8,128)S(1)}, u32[]{:S(2)}, u32[]{:S(2)}) collective-permute-start(f32[72,128]{1,0:T(8,128)S(1)} %add.46), channel_id=1, source_target_pairs={{0,12},{4,8},{8,4},{12,0},{1,13},{5,9},{9,5},{13,1},{2,14},{6,10},... | collective-permute-start | bytes 110600 | tf_op jit(solution)/shard_map/ppermute | solution.py:21
  79.1 2.8 %collective-permute-start.16 = (f32[72,128]{1,0:T(8,128)S(1)}, f32[72,128]{1,0:T(8,128)S(1)}, u32[]{:S(2)}, u32[]{:S(2)}) collective-permute-start(f32[72,128]{1,0:T(8,128)S(1)} %add.47), channel_id=1, source_target_pairs={{0,16},{16,0},{32,48},{48,32},{1,17},{17,1},{33,49},{49,33},{2,18}... | collective-permute-start | bytes 110600 | tf_op jit(solution)/shard_map/ppermute | solution.py:21
  81.9 4.0 %collective-permute-start.17 = (f32[72,128]{1,0:T(8,128)S(1)}, f32[72,128]{1,0:T(8,128)S(1)}, u32[]{:S(2)}, u32[]{:S(2)}) collective-permute-start(f32[72,128]{1,0:T(8,128)S(1)} %add.48), channel_id=1, source_target_pairs={{0,48},{16,32},{32,16},{48,0},{1,49},{17,33},{33,17},{49,1},{2,50}... | collective-permute-start | bytes 110600 | tf_op jit(solution)/shard_map/ppermute | solution.py:21
  85.9 2.8 %collective-permute-start.18 = (f32[72,128]{1,0:T(8,128)S(1)}, f32[72,128]{1,0:T(8,128)S(1)}, u32[]{:S(2)}, u32[]{:S(2)}) collective-permute-start(f32[72,128]{1,0:T(8,128)S(1)} %add.49), channel_id=1, source_target_pairs={{0,64},{64,0},{128,192},{192,128},{1,65},{65,1},{129,193},{193,129... | collective-permute-start | bytes 110600 | tf_op jit(solution)/shard_map/ppermute | solution.py:21
  88.8 4.0 %collective-permute-start.19 = (f32[72,128]{1,0:T(8,128)S(1)}, f32[72,128]{1,0:T(8,128)S(1)}, u32[]{:S(2)}, u32[]{:S(2)}) collective-permute-start(f32[72,128]{1,0:T(8,128)S(1)} %add.50), channel_id=1, source_target_pairs={{0,192},{64,128},{128,64},{192,0},{1,193},{65,129},{129,65},{193,1... | collective-permute-start | bytes 110600 | tf_op jit(solution)/shard_map/ppermute | solution.py:21
  92.8 8.6 %collective-permute-start.22 = (f32[72,128]{1,0:T(8,128)S(1)}, f32[72,128]{1,0:T(8,128)S(1)}, u32[]{:S(2)}, u32[]{:S(2)}) collective-permute-start(f32[72,128]{1,0:T(8,128)S(1)} %add.51.refs_1_), channel_id=1, source_target_pairs={{0,3},{1,2},{2,1},{3,0},{4,7},{5,6},{6,5},{7,4},{8,11},{9,10},{10,... | collective-permute-start | bytes 110600 | tf_op jit(solution)/shard_map/ppermute | solution.py:21
  99.8 3.5 %collective-permute-start.21 = (f32[72,128]{1,0:T(8,128)S(1)}, f32[72,128]{1,0:T(8,128)S(1)}, u32[]{:S(2)}, u32[]{:S(2)}) collective-permute-start(f32[72,128]{1,0:T(8,128)S(1)} %add.51.refs_1_), channel_id=1, source_target_pairs={{0,1},{1,0},{2,3},{3,2},{4,5},{5,4},{6,7},{7,6},{8,9},{9,8},{10,11... | collective-permute-start | bytes 110600 | tf_op jit(solution)/shard_map/ppermute | solution.py:21
  100.6 2.7 %collective-permute-start.20 = (f32[72,128]{1,0:T(8,128)S(1)}, f32[72,128]{1,0:T(8,128)S(1)}, u32[]{:S(2)}, u32[]{:S(2)}) collective-permute-start(f32[72,128]{1,0:T(8,128)S(1)} %add.51.refs_1_), channel_id=1, source_target_pairs={{0,2},{2,0},{1,3},{3,1},{4,6},{6,4},{5,7},{7,5},{8,10},{10,8},{9,1... | collective-permute-start | bytes 110600 | tf_op jit(solution)/shard_map/ppermute | solution.py:21
  (6 other events, 184.7 us)

commit v2 on v1

v2 whole, which is shorter than its diff:
```python
import functools
import itertools

import jax
import jax.numpy as jnp
from jax import lax
from jax.experimental import pallas as pl
from jax.experimental.pallas import tpu as pltpu
from jax.sharding import Mesh
from jax.sharding import PartitionSpec as P

ROWS = ("x", "y", "z", "c")
ROWS_REP = ("x", "y", "z", "c", "rep")
GROUP = 8
KINDS = 6
EMPTY = 48

SMEM = pl.BlockSpec(memory_space=pltpu.SMEM)
VMEM = pl.BlockSpec(memory_space=pltpu.VMEM)


def swap(value, axis, step):
    n = lax.axis_size(axis)
    return lax.ppermute(value, axis, [(i, i ^ step) for i in range(n)])


def swap_plane(value, step, last):
    nx, ny = lax.axis_size("x"), lax.axis_size("y")
    pairs = []
    for x, y, c in itertools.product(range(nx), range(ny), range(2)):
        along_x = (c == 1) != last
        x2, y2 = (x ^ step, y) if along_x else (x, y ^ step)
        pairs.append(((x * ny + y) * 2 + c, (x2 * ny + y2) * 2 + c))
    return lax.ppermute(value, ("x", "y", "c"), pairs)


def reorder_kernel(rep, order, features, own):
    half = own.shape[0]
    nodes = features.shape[0]
    wanted = order[pl.ds(rep[0], 1), :] & (nodes - 1)
    pick = (lax.broadcasted_iota(jnp.int32, (nodes, half), 0) == wanted).astype(jnp.bfloat16)
    own[...] = lax.dot_general(
        pick, features[...], (((0,), (0,)), ((), ())), preferred_element_type=jnp.float32
    ).astype(jnp.bfloat16)


def plan_kernel(kind, place, count, order, spot, groups, filled):
    room = order.shape[0] // KINDS
    for n in range(KINDS):
        filled[n] = n * room

    def step(t, carry):
        n = kind[t]
        at = filled[n]
        order[at] = t
        spot[at] = place[t]
        filled[n] = at + 1
        return carry

    lax.fori_loop(0, count[0], step, 0)

    def finish(n, carry):
        end = filled[n]
        for k in range(GROUP):
            order[end + k] = 0
            spot[end + k] = EMPTY
        groups[n] = (end - n * room + GROUP - 1) // GROUP
        return carry

    lax.fori_loop(0, KINDS, finish, 0)


def tiles_kernel(kind, order, spot, groups, tiles, *refs):
    refs, out, sources = refs[:-2], refs[-2], refs[-1]
    size = tiles.shape[1]
    before = None
    if refs[0].shape == out.shape:
        before, refs = refs[0], refs[1:]
    blocks = refs[0].shape[0]
    room = order.shape[0] // KINDS

    def place_block(b, carry):
        for k, piece in enumerate(refs):
            sources[k * blocks + b] = piece[b]
        return carry

    lax.fori_loop(0, blocks, place_block, 0)
    sources[EMPTY] = jnp.zeros((size, size), jnp.bfloat16)

    for r in range(2):
        rows = slice(r * size, (r + 1) * size)

        def step(q, acc):
            at = (kind + r) * room + q * GROUP
            left = jnp.concatenate([tiles[order[at + k]] for k in range(GROUP)], axis=1)
            right = jnp.concatenate([sources[spot[at + k]] for k in range(GROUP)], axis=0)
            return acc + jnp.dot(left, right, preferred_element_type=jnp.float32)

        start = jnp.zeros((size, size), jnp.float32) if before is None else before[rows]
        out[rows] = lax.fori_loop(0, groups[kind + r], step, start)


def dense_kernel(core, rep, order, mine, theirs, weight, bias, cotangent, act, keep, send):
    nodes = mine.shape[0]
    half = weight.shape[1] // 2
    part = weight.shape[0] // 2
    hidden = (mine[...] + theirs[...]).astype(jnp.bfloat16)
    where = jnp.concatenate([order[0:1], order[1:2]], axis=1) & (nodes - 1)
    put = (lax.broadcasted_iota(jnp.int32, (nodes, nodes), 0) == where).astype(jnp.bfloat16)
    hidden = jnp.dot(put, hidden, preferred_element_type=jnp.float32).astype(jnp.bfloat16)
    pre_act = jnp.dot(hidden, weight[...], preferred_element_type=jnp.float32) + bias[...]
    sigma = 1.0 / (1.0 + jnp.exp(-pre_act))
    act[...] = (pre_act * sigma).astype(jnp.bfloat16)
    slope = sigma * (1.0 + pre_act * (1.0 - sigma))
    scaled = (cotangent[...].astype(jnp.float32) * slope).astype(jnp.bfloat16)
    total = lax.dot_general(
        hidden, scaled, (((0,), (0,)), ((), ())), preferred_element_type=jnp.float32
    )
    column = jnp.sum(scaled.astype(jnp.float32), axis=0, keepdims=True)
    upper = rep[0] == 1
    total = jnp.where(upper, total[:, half:], total[:, :half])
    column = jnp.where(upper, column[:, half:], column[:, :half])
    lower = core[0] == 0
    keep[:part] = jnp.where(lower, total[:part], total[part:])
    send[:part] = jnp.where(lower, total[part:], total[:part])
    keep[part:] = jnp.broadcast_to(column, (8, half))
    send[part:] = jnp.broadcast_to(column, (8, half))


def pair_kernel(core, own, other, out):
    part = own.shape[0] - 8
    lower = core[0] == 0
    out[:part] = jnp.where(lower, own[:part], other[:part])
    out[part : 2 * part] = jnp.where(lower, other[:part], own[:part])
    out[2 * part :] = own[part:]


def finish_kernel(scale, rep, own, other, weight_grad, bias_grad):
    width, half = own.shape[0] - 8, own.shape[1]
    left = rep[0] == 0
    for columns, first, second in ((slice(0, half), own, other), (slice(half, 2 * half), other, own)):
        weight_grad[:, columns] = jnp.where(left, first[:width], second[:width]) * scale
        bias_grad[:, columns] = jnp.where(left, first[width : width + 1], second[width : width + 1]) * scale


def kinds_and_places(tile_row, tile_col, me):
    source = tile_col >> 1
    away = source ^ me
    x, y, z, c = (away >> 5) & 3, (away >> 3) & 3, (away >> 1) & 3, away & 1
    flip = (source & 1) == 1
    last, plane = jnp.where(flip, y, x), jnp.where(flip, x, y)
    early = last == 0
    kind = jnp.where(early, 0, 2 + 2 * c) + (tile_row & 1)
    return kind, jnp.where(early, c, last - 1) * 16 + plane * 4 + z


def aggregated(own, me, tile_vals, tile_row, tile_col, tile_count):
    slots, size, _ = tile_vals.shape
    width = own.shape[1]

    def products(kind, before, pieces):
        before = [] if before is None else [before]
        return pl.pallas_call(
            functools.partial(tiles_kernel, kind),
            out_shape=jax.ShapeDtypeStruct((2 * size, width), jnp.float32),
            in_specs=[SMEM] * 3 + [VMEM] * (1 + len(before) + len(pieces)),
            out_specs=VMEM,
            scratch_shapes=[pltpu.VMEM((EMPTY + 1, size, width), jnp.bfloat16)],
            compiler_params=pltpu.CompilerParams(vmem_limit_bytes=8 * 2**20),
            cost_estimate=pl.CostEstimate(
                flops=128 * size**3, bytes_accessed=64 * 2 * size**2, transcendentals=0
            ),
        )(*plan, tile_vals, *before, *pieces)

    line = jnp.concatenate([own[None]] + [swap(own[None], "z", s) for s in (1, 2, 3)])
    line = lax.optimization_barrier(line)
    plane = jnp.concatenate([line] + [swap_plane(line, s, False) for s in (1, 2, 3)])
    plane = lax.optimization_barrier(plane)
    one, two, three = (swap_plane(plane, s, True) for s in (1, 2, 3))
    other = swap(plane, "c", 1)

    row, col, _ = lax.optimization_barrier((tile_row, tile_col, plane))
    kind, place = kinds_and_places(row, col, me)
    entries = jax.ShapeDtypeStruct((KINDS * (slots + GROUP),), jnp.int32)
    plan = pl.pallas_call(
        plan_kernel,
        out_shape=(entries, entries, jax.ShapeDtypeStruct((KINDS,), jnp.int32)),
        in_specs=[SMEM] * 3,
        out_specs=(SMEM,) * 3,
        scratch_shapes=[pltpu.SMEM((KINDS,), jnp.int32)],
        compiler_params=pltpu.CompilerParams(vmem_limit_bytes=4 * 2**20),
    )(kind, place, tile_count)
    total = products(0, None, [plane, other])
    one, two, three, total = lax.optimization_barrier((one, two, three, total))
    others = [swap(p, "c", 1) for p in (one, two, three)]
    total = products(2, total, [one, two, three])
    return products(4, total, others)


def body(features, node_order, tile_vals, tile_row, tile_col, tile_count, weight, bias, cotangent):
    nodes, width = features.shape
    hid = weight.shape[1]
    half, part = hid // 2, width // 2
    me = lax.axis_index(ROWS)
    core = lax.axis_index("c").reshape(1)
    rep = lax.axis_index("rep").reshape(1)
    order = node_order.reshape(2, nodes // 2)
    own = pl.pallas_call(
        reorder_kernel,
        out_shape=jax.ShapeDtypeStruct((nodes // 2, width), jnp.bfloat16),
        in_specs=[SMEM, VMEM, VMEM],
        out_specs=VMEM,
        compiler_params=pltpu.CompilerParams(vmem_limit_bytes=56 * 2**20),
    )(rep, order, features)

    mine = aggregated(own, me, tile_vals, tile_row, tile_col, tile_count)
    theirs = swap(mine, "rep", 1)
    act, keep, send = pl.pallas_call(
        dense_kernel,
        out_shape=(
            jax.ShapeDtypeStruct((nodes, hid), jnp.bfloat16),
            jax.ShapeDtypeStruct((part + 8, half), jnp.float32),
            jax.ShapeDtypeStruct((part + 8, half), jnp.float32),
        ),
        in_specs=[SMEM] * 2 + [VMEM] * 6,
        out_specs=(VMEM,) * 3,
        compiler_params=pltpu.CompilerParams(vmem_limit_bytes=16 * 2**20),
    )(core, rep, order, mine, theirs, weight, bias.reshape(1, hid), cotangent)
    total = keep + swap(send, "c", 1)
    for axis in ("z", "y", "x"):
        one, two, three = (swap(total, axis, step) for step in (1, 2, 3))
        total = (total + one) + (two + three)
    scale = float(nodes * lax.axis_size(ROWS)) ** -0.5
    pair = pl.pallas_call(
        pair_kernel,
        out_shape=jax.ShapeDtypeStruct((width + 8, half), jnp.float32),
        in_specs=[SMEM] + [VMEM] * 2,
        out_specs=VMEM,
        compiler_params=pltpu.CompilerParams(vmem_limit_bytes=4 * 2**20),
    )(core, total, swap(total, "c", 1))
    weight_grad, bias_grad = pl.pallas_call(
        functools.partial(finish_kernel, scale),
        out_shape=(
            jax.ShapeDtypeStruct((width, hid), jnp.float32),
            jax.ShapeDtypeStruct((1, hid), jnp.float32),
        ),
        in_specs=[SMEM] + [VMEM] * 2,
        out_specs=(VMEM,) * 2,
        compiler_params=pltpu.CompilerParams(vmem_limit_bytes=4 * 2**20),
    )(rep, pair, swap(pair, "rep", 1))
    return act, weight_grad, bias_grad.reshape(hid)


def solution(mesh):
    finer = Mesh(mesh.devices.reshape(4, 4, 4, 2, mesh.shape["rep"]), ROWS_REP)
    return jax.shard_map(
        body,
        mesh=finer,
        in_specs=(
            P(ROWS, None),
            P(ROWS),
            P(ROWS_REP, None, None),
            P(ROWS_REP),
            P(ROWS_REP),
            P(ROWS_REP),
            P(),
            P(),
            P(ROWS, None),
        ),
        out_specs=(P(ROWS, None), P(), P()),
        check_vma=False,
    )
```

time: 104 us -> 91.6 us (0.88)
  starting transfers between devices: 48.8 us -> 38.1 us
  waiting for transfers between devices: 40.1 us -> 32.3 us
  Pallas kernels: 8.91 us -> 14.8 us
  local copies, waits for them, and re-layouts: 4.4 us -> 2.81 us
    ppermute x17 -> x20, starting transfers between devices: 41.5 us -> 31.5 us  [swap(): return lax.ppermute(value, axis, [(i, i ^ step) for i in range(n)])]
    pallas_call x2 -> x6, Pallas kernels: 6.58 us -> 12.1 us  [the longest x3 7.82 us: products(): pl.pallas_call(functools.partial(tiles_kernel, kind), out_shape=jax.Shape...]
    ppermute x6, waiting for transfers between devices: 11.2 us -> 7.14 us  [swap_plane(): return lax.ppermute(value, ('x', 'y', 'c'), pairs)]
    ppermute x17 -> x20, waiting for transfers between devices: 28.9 us -> 25.2 us  [swap(): return lax.ppermute(value, axis, [(i, i ^ step) for i in range(n)])]
    unnamed x19 -> x10, local copies, waits for them, and re-layouts: 4.38 us -> 2.81 us
  transfers between devices with their start and end apart: 23 -> 26, of which waited for: 16 -> 16; matrix products, arithmetic and copies ran while one was open for 1% -> 1% of each run, Pallas kernels for 0% -> 9%
where the time goes in v2:
time: 91.6 us; the launch traced here: 91.1 us
  starting transfers between devices  38.1 us (42%)
  waiting for transfers between devices  32.3 us (35%)
  Pallas kernels  14.8 us (16%)
  local copies, waits for them, and re-layouts  2.81 us (3%)
  other arithmetic  1.59 us (2%)
  between operations  1.47 us (2%)
    ppermute x20, starting transfers between devices, swap(): return lax.ppermute(value, axis, [(i, i ^ step) for i in range(n)])  31.5 us
    ppermute x20, waiting for transfers between devices, swap(): return lax.ppermute(value, axis, [(i, i ^ step) for i in range(n)])  25.2 us
    pallas_call x3, Pallas kernels, products(): pl.pallas_call(functools.partial(tiles_kernel, kind), out_shape=jax.Shape...  7.82 us
    ppermute x6, waiting for transfers between devices, swap_plane(): return lax.ppermute(value, ('x', 'y', 'c'), pairs)  7.14 us
    ppermute x6, starting transfers between devices, swap_plane(): return lax.ppermute(value, ('x', 'y', 'c'), pairs)  6.59 us
    pallas_call x1, Pallas kernels, aggregated(): pl.pallas_call(plan_kernel, out_shape=(entries, entries, jax.ShapeDtypeSt...  3.56 us
    unnamed x10, local copies, waits for them, and re-layouts  2.81 us
  transfers between devices with their start and end apart: 26, of which 16 were waited for; matrix products, arithmetic and copies ran while one was open for 1% of the time, Pallas kernels for 9%

profile of v2, /device:TPU:1, one launch (start us, length us, event | category | flops | bytes accessed | tf_op | source)
XLA Modules:
  0.0 91.1 jit_solution(1675999021191216022)
XLA Ops:
  0.6 1.7 %shard_map.112 = bf16[128,128]{1,0:T(8,128)(2,1)} custom-call(s32[1]{0:T(128)} %bitcast.1.rep, s32[2,128]{1,0:T(2,128)} %bitcast.6, bf16[256,128]{1,0:T(8,128)(2,1)} %features.1), custom_call_target="tpu_custom_call" | custom-call | tf_op jit(solution)/shard_map/pallas_call | solution.py:208
  2.3 6.8 %collective-permute-start.2 = (bf16[1,128,128]{2,1,0:T(8,128)(2,1)}, bf16[1,128,128]{2,1,0:T(8,128)(2,1)S(1)}, u32[]{:S(2)}, u32[]{:S(2)}) collective-permute-start(bf16[1,128,128]{2,1,0:T(8,128)(2,1)} %bitcast.9), channel_id=1, source_target_pairs={{0,12},{4,8},{8,4},{12,0},{1,13},{5,9},{9,5},{13,1},{2,14},{6,10},... | collective-permute-start | bytes 98312 | tf_op jit(solution)/shard_map/ppermute | solution.py:24
  11.3 5.0 %collective-permute-done.1 = bf16[1,128,128]{2,1,0:T(8,128)(2,1)S(1)} collective-permute-done((bf16[1,128,128]{2,1,0:T(8,128)(2,1)}, bf16[1,128,128]{2,1,0:T(8,128)(2,1)S(1)}, u32[]{:S(2)}, u32[]{:S(2)}) %collective-permute-start.1) | collective-permute-done | bytes 32800 | tf_op jit(solution)/shard_map/ppermute | solution.py:24
  17.0 2.6 %collective-permute-start.5 = (bf16[4,128,128]{2,1,0:T(8,128)(2,1)S(1)}, bf16[4,128,128]{2,1,0:T(8,128)(2,1)S(1)}, u32[]{:S(2)}, u32[]{:S(2)}) collective-permute-start(bf16[4,128,128]{2,1,0:T(8,128)(2,1)S(1)} %pad_maximum_fusion.1), channel_id=1, source_target_pairs={{0,48},{2,194},{16,32},{18,210},{32,16},{34,226},{48,0},{50,242},{... | collective-permute-start | bytes 393224 | tf_op jit(solution)/shard_map/ppermute | solution.py:34
  20.3 2.5 %collective-permute-done.5 = bf16[4,128,128]{2,1,0:T(8,128)(2,1)S(1)} collective-permute-done((bf16[4,128,128]{2,1,0:T(8,128)(2,1)S(1)}, bf16[4,128,128]{2,1,0:T(8,128)(2,1)S(1)}, u32[]{:S(2)}, u32[]{:S(2)}) %collective-permute-start.5) | collective-permute-done | bytes 131104 | tf_op jit(solution)/shard_map/ppermute | solution.py:34
  22.9 2.0 %collective-permute-done.4 = bf16[4,128,128]{2,1,0:T(8,128)(2,1)S(1)} collective-permute-done((bf16[4,128,128]{2,1,0:T(8,128)(2,1)S(1)}, bf16[4,128,128]{2,1,0:T(8,128)(2,1)S(1)}, u32[]{:S(2)}, u32[]{:S(2)}) %collective-permute-start.4) | collective-permute-done | bytes 131104 | tf_op jit(solution)/shard_map/ppermute | solution.py:34
  25.0 4.1 %collective-permute-start.9 = (bf16[16,128,128]{2,1,0:T(8,128)(2,1)S(1)}, bf16[16,128,128]{2,1,0:T(8,128)(2,1)S(1)}, u32[]{:S(2)}, u32[]{:S(2)}) collective-permute-start(bf16[16,128,128]{2,1,0:T(8,128)(2,1)S(1)} %pad_maximum_fusion.refs_0_), channel_id=1, source_target_pairs={{0,2},{2,0},{1,3},{3,1},{4,6},{6,4},{5,7},{7,5},{8,10},{10,8},{9,1... | collective-permute-start | bytes 1572872 | tf_op jit(solution)/shard_map/ppermute | solution.py:24
  29.0 1.7 %collective-permute-start.8 = (bf16[16,128,128]{2,1,0:T(8,128)(2,1)S(1)}, bf16[16,128,128]{2,1,0:T(8,128)(2,1)S(1)}, u32[]{:S(2)}, u32[]{:S(2)}) collective-permute-start(bf16[16,128,128]{2,1,0:T(8,128)(2,1)S(1)} %pad_maximum_fusion.refs_0_), channel_id=1, source_target_pairs={{0,192},{2,50},{16,208},{18,34},{32,224},{34,18},{48,240},{50,2},{... | collective-permute-start | bytes 1572872 | tf_op jit(solution)/shard_map/ppermute | solution.py:34
  33.6 3.6 %shard_map.113 = (s32[1200]{0:T(1024)S(1)}, s32[1200]{0:T(1024)S(1)}, s32[6]{0:T(128)S(1)}) custom-call(s32[192]{0:T(256)S(1)} %get-tuple-element.32.kind, s32[192]{0:T(256)S(1)} %get-tuple-element.31.place, s32[1]{0:T(128)S(6)} %copy.12.count), custom_call_target="tpu_custom_call" | custom-call | tf_op jit(solution)/shard_map/pallas_call | solution.py:185
  37.2 2.8 %copy-done = bf16[192,128,128]{2,1,0:T(8,128)(2,1)S(1)} copy-done((bf16[192,128,128]{2,1,0:T(8,128)(2,1)S(1)}, bf16[192,128,128]{2,1,0:T(8,128)(2,1)}, u32[]{:S(2)}) %copy-start) | copy-done | bytes 6291480
  40.0 2.1 %shard_map.114.refs_0_ = f32[256,128]{1,0:T(8,128)S(1)} custom-call(s32[1200]{0:T(1024)S(1)} %get-tuple-element.19.order, s32[1200]{0:T(1024)S(1)} %get-tuple-element.20.spot, s32[6]{0:T(128)S(1)} %get-tuple-element.21.groups, bf16[192,128,128]{2,1,0:T(8,128)(2,1)S(1)} %copy-done, bf16[16,128,128]{2,1,0:T(8,128)(2,1)S(1)} %pad_maximum_fusion.refs_0_, ...), custom_call_target="tpu_custom_call" | custom-call | flops 268435456 | bytes 2097152 | tf_op jit(solution)/shard_map/pallas_call | solution.py:163
  42.2 2.0 %collective-permute-done.8.refs_3_ = bf16[16,128,128]{2,1,0:T(8,128)(2,1)S(1)} collective-permute-done((bf16[16,128,128]{2,1,0:T(8,128)(2,1)S(1)}, bf16[16,128,128]{2,1,0:T(8,128)(2,1)S(1)}, u32[]{:S(2)}, u32[]{:S(2)}) %collective-permute-start.8) | collective-permute-done | bytes 524320 | tf_op jit(solution)/shard_map/ppermute | solution.py:34
  46.5 2.8 %shard_map.115.refs_0_ = f32[256,128]{1,0:T(8,128)S(1)} custom-call(s32[1200]{0:T(1024)S(1)} %get-tuple-element.19.order, s32[1200]{0:T(1024)S(1)} %get-tuple-element.20.spot, s32[6]{0:T(128)S(1)} %get-tuple-element.21.groups, bf16[192,128,128]{2,1,0:T(8,128)(2,1)S(1)} %copy-done, f32[256,128]{1,0:T(8,128)S(1)} %shard_map.114.refs_0_, ...), custom_call_target="tpu_custom_call" | custom-call | flops 268435456 | bytes 2097152 | tf_op jit(solution)/shard_map/pallas_call | solution.py:163
  49.4 2.8 %shard_map.116.mine = f32[256,128]{1,0:T(8,128)S(1)} custom-call(s32[1200]{0:T(1024)S(1)} %get-tuple-element.19.order, s32[1200]{0:T(1024)S(1)} %get-tuple-element.20.spot, s32[6]{0:T(128)S(1)} %get-tuple-element.21.groups, bf16[192,128,128]{2,1,0:T(8,128)(2,1)S(1)} %copy-done, f32[256,128]{1,0:T(8,128)S(1)} %shard_map.115.refs_0_, ...), custom_call_target="tpu_custom_call" | custom-call | flops 268435456 | bytes 2097152 | tf_op jit(solution)/shard_map/pallas_call | solution.py:163
  52.4 5.1 %collective-permute-done.13.theirs = f32[256,128]{1,0:T(8,128)S(1)} collective-permute-done((f32[256,128]{1,0:T(8,128)S(1)}, f32[256,128]{1,0:T(8,128)S(1)}, u32[]{:S(2)}, u32[]{:S(2)}) %collective-permute-start.13) | collective-permute-done | bytes 131104 | tf_op jit(solution)/shard_map/ppermute | solution.py:24
  59.9 1.5 %collective-permute-start.17 = (f32[72,128]{1,0:T(8,128)S(1)}, f32[72,128]{1,0:T(8,128)S(1)}, u32[]{:S(2)}, u32[]{:S(2)}) collective-permute-start(f32[72,128]{1,0:T(8,128)S(1)} %add.59), channel_id=1, source_target_pairs={{0,12},{4,8},{8,4},{12,0},{1,13},{5,9},{9,5},{13,1},{2,14},{6,10},... | collective-permute-start | bytes 110600 | tf_op jit(solution)/shard_map/ppermute | solution.py:24
  61.4 3.2 %collective-permute-start.16 = (f32[72,128]{1,0:T(8,128)S(1)}, f32[72,128]{1,0:T(8,128)S(1)}, u32[]{:S(2)}, u32[]{:S(2)}) collective-permute-start(f32[72,128]{1,0:T(8,128)S(1)} %add.59), channel_id=1, source_target_pairs={{0,8},{4,12},{8,0},{12,4},{1,9},{5,13},{9,1},{13,5},{2,10},{6,14},... | collective-permute-start | bytes 110600 | tf_op jit(solution)/shard_map/ppermute | solution.py:24
  65.5 2.7 %collective-permute-done.16 = f32[72,128]{1,0:T(8,128)S(1)} collective-permute-done((f32[72,128]{1,0:T(8,128)S(1)}, f32[72,128]{1,0:T(8,128)S(1)}, u32[]{:S(2)}, u32[]{:S(2)}) %collective-permute-start.16) | collective-permute-done | bytes 36896 | tf_op jit(solution)/shard_map/ppermute | solution.py:24
  68.2 2.1 %collective-permute-done.15 = f32[72,128]{1,0:T(8,128)S(1)} collective-permute-done((f32[72,128]{1,0:T(8,128)S(1)}, f32[72,128]{1,0:T(8,128)S(1)}, u32[]{:S(2)}, u32[]{:S(2)}) %collective-permute-start.15) | collective-permute-done | bytes 36896 | tf_op jit(solution)/shard_map/ppermute | solution.py:24
  70.4 2.1 %collective-permute-start.19 = (f32[72,128]{1,0:T(8,128)S(1)}, f32[72,128]{1,0:T(8,128)S(1)}, u32[]{:S(2)}, u32[]{:S(2)}) collective-permute-start(f32[72,128]{1,0:T(8,128)S(1)} %add_add_fusion.2), channel_id=1, source_target_pairs={{0,32},{16,48},{32,0},{48,16},{1,33},{17,49},{33,1},{49,17},{2,34}... | collective-permute-start | bytes 110600 | tf_op jit(solution)/shard_map/ppermute | solution.py:24
  75.7 2.5 %collective-permute-start.23 = (f32[72,128]{1,0:T(8,128)S(1)}, f32[72,128]{1,0:T(8,128)S(1)}, u32[]{:S(2)}, u32[]{:S(2)}) collective-permute-start(f32[72,128]{1,0:T(8,128)S(1)} %add_add_fusion.1), channel_id=1, source_target_pairs={{0,192},{64,128},{128,64},{192,0},{1,193},{65,129},{129,65},{193,1... | collective-permute-start | bytes 110600 | tf_op jit(solution)/shard_map/ppermute | solution.py:24
  79.8 2.7 %collective-permute-done.22 = f32[72,128]{1,0:T(8,128)S(1)} collective-permute-done((f32[72,128]{1,0:T(8,128)S(1)}, f32[72,128]{1,0:T(8,128)S(1)}, u32[]{:S(2)}, u32[]{:S(2)}) %collective-permute-start.22) | collective-permute-done | bytes 36896 | tf_op jit(solution)/shard_map/ppermute | solution.py:24
  82.5 3.8 %collective-permute-start.24 = (f32[72,128]{1,0:T(8,128)S(1)}, f32[72,128]{1,0:T(8,128)S(1)}, u32[]{:S(2)}, u32[]{:S(2)}) collective-permute-start(f32[72,128]{1,0:T(8,128)S(1)} %add_add_fusion.own), channel_id=1, source_target_pairs={{0,2},{2,0},{1,3},{3,1},{4,6},{6,4},{5,7},{7,5},{8,10},{10,8},{9,1... | collective-permute-start | bytes 110600 | tf_op jit(solution)/shard_map/ppermute | solution.py:24
  87.3 3.1 %collective-permute-done.25.other = f32[136,128]{1,0:T(8,128)S(1)} collective-permute-done((f32[136,128]{1,0:T(8,128)S(1)}, f32[136,128]{1,0:T(8,128)S(1)}, u32[]{:S(2)}, u32[]{:S(2)}) %collective-permute-start.25) | collective-permute-done | bytes 69664 | tf_op jit(solution)/shard_map/ppermute | solution.py:24
  (53 shorter events, 18.3 us)
Async XLA Ops:
  2.3 8.9 %collective-permute-start.2 = (bf16[1,128,128]{2,1,0:T(8,128)(2,1)}, bf16[1,128,128]{2,1,0:T(8,128)(2,1)S(1)}, u32[]{:S(2)}, u32[]{:S(2)}) collective-permute-start(bf16[1,128,128]{2,1,0:T(8,128)(2,1)} %bitcast.9), channel_id=1, source_target_pairs={{0,12},{4,8},{8,4},{12,0},{1,13},{5,9},{9,5},{13,1},{2,14},{6,10},... | collective-permute-start | bytes 98312 | tf_op jit(solution)/shard_map/ppermute | solution.py:24
  9.2 7.1 %collective-permute-start.1 = (bf16[1,128,128]{2,1,0:T(8,128)(2,1)}, bf16[1,128,128]{2,1,0:T(8,128)(2,1)S(1)}, u32[]{:S(2)}, u32[]{:S(2)}) collective-permute-start(bf16[1,128,128]{2,1,0:T(8,128)(2,1)} %bitcast.10), channel_id=1, source_target_pairs={{0,8},{4,12},{8,0},{12,4},{1,9},{5,13},{9,1},{13,5},{2,10},{6,14},... | collective-permute-start | bytes 98312 | tf_op jit(solution)/shard_map/ppermute | solution.py:24
  10.1 6.2 %collective-permute-start = (bf16[1,128,128]{2,1,0:T(8,128)(2,1)}, bf16[1,128,128]{2,1,0:T(8,128)(2,1)S(1)}, u32[]{:S(2)}, u32[]{:S(2)}) collective-permute-start(bf16[1,128,128]{2,1,0:T(8,128)(2,1)} %bitcast.11), channel_id=1, source_target_pairs={{0,4},{4,0},{8,12},{12,8},{1,5},{5,1},{9,13},{13,9},{2,6},{6,2},{1... | collective-permute-start | bytes 98312 | tf_op jit(solution)/shard_map/ppermute | solution.py:24
  17.0 5.9 %collective-permute-start.5 = (bf16[4,128,128]{2,1,0:T(8,128)(2,1)S(1)}, bf16[4,128,128]{2,1,0:T(8,128)(2,1)S(1)}, u32[]{:S(2)}, u32[]{:S(2)}) collective-permute-start(bf16[4,128,128]{2,1,0:T(8,128)(2,1)S(1)} %pad_maximum_fusion.1), channel_id=1, source_target_pairs={{0,48},{2,194},{16,32},{18,210},{32,16},{34,226},{48,0},{50,242},{... | collective-permute-start | bytes 393224 | tf_op jit(solution)/shard_map/ppermute | solution.py:34
  19.6 5.3 %collective-permute-start.4 = (bf16[4,128,128]{2,1,0:T(8,128)(2,1)S(1)}, bf16[4,128,128]{2,1,0:T(8,128)(2,1)S(1)}, u32[]{:S(2)}, u32[]{:S(2)}) collective-permute-start(bf16[4,128,128]{2,1,0:T(8,128)(2,1)S(1)} %pad_maximum_fusion.1), channel_id=1, source_target_pairs={{0,32},{2,130},{16,48},{18,146},{32,0},{34,162},{48,16},{50,178},{... | collective-permute-start | bytes 393224 | tf_op jit(solution)/shard_map/ppermute | solution.py:34
  20.1 4.8 %collective-permute-start.3 = (bf16[4,128,128]{2,1,0:T(8,128)(2,1)S(1)}, bf16[4,128,128]{2,1,0:T(8,128)(2,1)S(1)}, u32[]{:S(2)}, u32[]{:S(2)}) collective-permute-start(bf16[4,128,128]{2,1,0:T(8,128)(2,1)S(1)} %pad_maximum_fusion.1), channel_id=1, source_target_pairs={{0,16},{2,66},{16,0},{18,82},{32,48},{34,98},{48,32},{50,114},{64,... | collective-permute-start | bytes 393224 | tf_op jit(solution)/shard_map/ppermute | solution.py:34
  25.0 12.2 %collective-permute-start.9 = (bf16[16,128,128]{2,1,0:T(8,128)(2,1)S(1)}, bf16[16,128,128]{2,1,0:T(8,128)(2,1)S(1)}, u32[]{:S(2)}, u32[]{:S(2)}) collective-permute-start(bf16[16,128,128]{2,1,0:T(8,128)(2,1)S(1)} %pad_maximum_fusion.refs_0_), channel_id=1, source_target_pairs={{0,2},{2,0},{1,3},{3,1},{4,6},{6,4},{5,7},{7,5},{8,10},{10,8},{9,1... | collective-permute-start | bytes 1572872 | tf_op jit(solution)/shard_map/ppermute | solution.py:24
  29.0 15.2 %collective-permute-start.8 = (bf16[16,128,128]{2,1,0:T(8,128)(2,1)S(1)}, bf16[16,128,128]{2,1,0:T(8,128)(2,1)S(1)}, u32[]{:S(2)}, u32[]{:S(2)}) collective-permute-start(bf16[16,128,128]{2,1,0:T(8,128)(2,1)S(1)} %pad_maximum_fusion.refs_0_), channel_id=1, source_target_pairs={{0,192},{2,50},{16,208},{18,34},{32,224},{34,18},{48,240},{50,2},{... | collective-permute-start | bytes 1572872 | tf_op jit(solution)/shard_map/ppermute | solution.py:34
  30.7 13.5 %collective-permute-start.7 = (bf16[16,128,128]{2,1,0:T(8,128)(2,1)S(1)}, bf16[16,128,128]{2,1,0:T(8,128)(2,1)S(1)}, u32[]{:S(2)}, u32[]{:S(2)}) collective-permute-start(bf16[16,128,128]{2,1,0:T(8,128)(2,1)S(1)} %pad_maximum_fusion.refs_0_), channel_id=1, source_target_pairs={{0,128},{2,34},{16,144},{18,50},{32,160},{34,2},{48,176},{50,18},{... | collective-permute-start | bytes 1572872 | tf_op jit(solution)/shard_map/ppermute | solution.py:34
  31.1 13.7 %collective-permute-start.6 = (bf16[16,128,128]{2,1,0:T(8,128)(2,1)S(1)}, bf16[16,128,128]{2,1,0:T(8,128)(2,1)S(1)}, u32[]{:S(2)}, u32[]{:S(2)}) collective-permute-start(bf16[16,128,128]{2,1,0:T(8,128)(2,1)S(1)} %pad_maximum_fusion.refs_0_), channel_id=1, source_target_pairs={{0,64},{2,18},{16,80},{18,2},{32,96},{34,50},{48,112},{50,34},{64,... | collective-permute-start | bytes 1572872 | tf_op jit(solution)/shard_map/ppermute | solution.py:34
  44.8 4.6 %collective-permute-start.10 = (bf16[16,128,128]{2,1,0:T(8,128)(2,1)S(1)}, bf16[16,128,128]{2,1,0:T(8,128)(2,1)S(1)}, u32[]{:S(2)}, u32[]{:S(2)}) collective-permute-start(bf16[16,128,128]{2,1,0:T(8,128)(2,1)S(1)} %collective-permute-done.6.refs_1_), channel_id=1, source_target_pairs={{0,2},{2,0},{1,3},{3,1},{4,6},{6,4},{5,7},{7,5},{8,10},{10,8},{9,1... | collective-permute-start | bytes 1572872 | tf_op jit(solution)/shard_map/ppermute | solution.py:24
  46.0 3.4 %collective-permute-start.11 = (bf16[16,128,128]{2,1,0:T(8,128)(2,1)S(1)}, bf16[16,128,128]{2,1,0:T(8,128)(2,1)S(1)}, u32[]{:S(2)}, u32[]{:S(2)}) collective-permute-start(bf16[16,128,128]{2,1,0:T(8,128)(2,1)S(1)} %collective-permute-done.7.refs_2_), channel_id=1, source_target_pairs={{0,2},{2,0},{1,3},{3,1},{4,6},{6,4},{5,7},{7,5},{8,10},{10,8},{9,1... | collective-permute-start | bytes 1572872 | tf_op jit(solution)/shard_map/ppermute | solution.py:24
  46.0 3.4 %collective-permute-start.12 = (bf16[16,128,128]{2,1,0:T(8,128)(2,1)S(1)}, bf16[16,128,128]{2,1,0:T(8,128)(2,1)S(1)}, u32[]{:S(2)}, u32[]{:S(2)}) collective-permute-start(bf16[16,128,128]{2,1,0:T(8,128)(2,1)S(1)} %collective-permute-done.8.refs_3_), channel_id=1, source_target_pairs={{0,2},{2,0},{1,3},{3,1},{4,6},{6,4},{5,7},{7,5},{8,10},{10,8},{9,1... | collective-permute-start | bytes 1572872 | tf_op jit(solution)/shard_map/ppermute | solution.py:24
  52.3 5.2 %collective-permute-start.13 = (f32[256,128]{1,0:T(8,128)S(1)}, f32[256,128]{1,0:T(8,128)S(1)}, u32[]{:S(2)}, u32[]{:S(2)}) collective-permute-start(f32[256,128]{1,0:T(8,128)S(1)} %shard_map.116.mine), channel_id=1, source_target_pairs={{0,1},{1,0},{2,3},{3,2},{4,5},{5,4},{6,7},{7,6},{8,9},{9,8},{10,11... | collective-permute-start | bytes 393224 | tf_op jit(solution)/shard_map/ppermute | solution.py:24
  59.9 5.7 %collective-permute-start.17 = (f32[72,128]{1,0:T(8,128)S(1)}, f32[72,128]{1,0:T(8,128)S(1)}, u32[]{:S(2)}, u32[]{:S(2)}) collective-permute-start(f32[72,128]{1,0:T(8,128)S(1)} %add.59), channel_id=1, source_target_pairs={{0,12},{4,8},{8,4},{12,0},{1,13},{5,9},{9,5},{13,1},{2,14},{6,10},... | collective-permute-start | bytes 110600 | tf_op jit(solution)/shard_map/ppermute | solution.py:24
  61.4 6.8 %collective-permute-start.16 = (f32[72,128]{1,0:T(8,128)S(1)}, f32[72,128]{1,0:T(8,128)S(1)}, u32[]{:S(2)}, u32[]{:S(2)}) collective-permute-start(f32[72,128]{1,0:T(8,128)S(1)} %add.59), channel_id=1, source_target_pairs={{0,8},{4,12},{8,0},{12,4},{1,9},{5,13},{9,1},{13,5},{2,10},{6,14},... | collective-permute-start | bytes 110600 | tf_op jit(solution)/shard_map/ppermute | solution.py:24
  64.5 5.7 %collective-permute-start.15 = (f32[72,128]{1,0:T(8,128)S(1)}, f32[72,128]{1,0:T(8,128)S(1)}, u32[]{:S(2)}, u32[]{:S(2)}) collective-permute-start(f32[72,128]{1,0:T(8,128)S(1)} %add.59), channel_id=1, source_target_pairs={{0,4},{4,0},{8,12},{12,8},{1,5},{5,1},{9,13},{13,9},{2,6},{6,2},{1... | collective-permute-start | bytes 110600 | tf_op jit(solution)/shard_map/ppermute | solution.py:24
  70.3 4.1 %collective-permute-start.20 = (f32[72,128]{1,0:T(8,128)S(1)}, f32[72,128]{1,0:T(8,128)S(1)}, u32[]{:S(2)}, u32[]{:S(2)}) collective-permute-start(f32[72,128]{1,0:T(8,128)S(1)} %add_add_fusion.2), channel_id=1, source_target_pairs={{0,48},{16,32},{32,16},{48,0},{1,49},{17,33},{33,17},{49,1},{2,50}... | collective-permute-start | bytes 110600 | tf_op jit(solution)/shard_map/ppermute | solution.py:24
  70.4 4.6 %collective-permute-start.19 = (f32[72,128]{1,0:T(8,128)S(1)}, f32[72,128]{1,0:T(8,128)S(1)}, u32[]{:S(2)}, u32[]{:S(2)}) collective-permute-start(f32[72,128]{1,0:T(8,128)S(1)} %add_add_fusion.2), channel_id=1, source_target_pairs={{0,32},{16,48},{32,0},{48,16},{1,33},{17,49},{33,1},{49,17},{2,34}... | collective-permute-start | bytes 110600 | tf_op jit(solution)/shard_map/ppermute | solution.py:24
  75.7 4.1 %collective-permute-start.23 = (f32[72,128]{1,0:T(8,128)S(1)}, f32[72,128]{1,0:T(8,128)S(1)}, u32[]{:S(2)}, u32[]{:S(2)}) collective-permute-start(f32[72,128]{1,0:T(8,128)S(1)} %add_add_fusion.1), channel_id=1, source_target_pairs={{0,192},{64,128},{128,64},{192,0},{1,193},{65,129},{129,65},{193,1... | collective-permute-start | bytes 110600 | tf_op jit(solution)/shard_map/ppermute | solution.py:24
  78.2 4.3 %collective-permute-start.22 = (f32[72,128]{1,0:T(8,128)S(1)}, f32[72,128]{1,0:T(8,128)S(1)}, u32[]{:S(2)}, u32[]{:S(2)}) collective-permute-start(f32[72,128]{1,0:T(8,128)S(1)} %add_add_fusion.1), channel_id=1, source_target_pairs={{0,128},{64,192},{128,0},{192,64},{1,129},{65,193},{129,1},{193,65... | collective-permute-start | bytes 110600 | tf_op jit(solution)/shard_map/ppermute | solution.py:24
  79.1 3.4 %collective-permute-start.21 = (f32[72,128]{1,0:T(8,128)S(1)}, f32[72,128]{1,0:T(8,128)S(1)}, u32[]{:S(2)}, u32[]{:S(2)}) collective-permute-start(f32[72,128]{1,0:T(8,128)S(1)} %add_add_fusion.1), channel_id=1, source_target_pairs={{0,64},{64,0},{128,192},{192,128},{1,65},{65,1},{129,193},{193,129... | collective-permute-start | bytes 110600 | tf_op jit(solution)/shard_map/ppermute | solution.py:24
  82.5 4.7 %collective-permute-start.24 = (f32[72,128]{1,0:T(8,128)S(1)}, f32[72,128]{1,0:T(8,128)S(1)}, u32[]{:S(2)}, u32[]{:S(2)}) collective-permute-start(f32[72,128]{1,0:T(8,128)S(1)} %add_add_fusion.own), channel_id=1, source_target_pairs={{0,2},{2,0},{1,3},{3,1},{4,6},{6,4},{5,7},{7,5},{8,10},{10,8},{9,1... | collective-permute-start | bytes 110600 | tf_op jit(solution)/shard_map/ppermute | solution.py:24
  87.2 3.2 %collective-permute-start.25 = (f32[136,128]{1,0:T(8,128)S(1)}, f32[136,128]{1,0:T(8,128)S(1)}, u32[]{:S(2)}, u32[]{:S(2)}) collective-permute-start(f32[136,128]{1,0:T(8,128)S(1)} %shard_map.118.own), channel_id=1, source_target_pairs={{0,1},{1,0},{2,3},{3,2},{4,5},{5,4},{6,7},{7,6},{8,9},{9,8},{10,11... | collective-permute-start | bytes 208904 | tf_op jit(solution)/shard_map/ppermute | solution.py:24
  (7 other events, 68.5 us)

commit v3 on v2

--- a/solution.py
+++ b/solution.py
@@ -24,14 +24,17 @@
     return lax.ppermute(value, axis, [(i, i ^ step) for i in range(n)])
 
 
-def swap_plane(value, step, last):
-    nx, ny = lax.axis_size("x"), lax.axis_size("y")
+def swap_by_core(value, axes, step):
+    names = ("x", "y", "z", "c")
+    shape = [lax.axis_size(name) for name in names]
     pairs = []
-    for x, y, c in itertools.product(range(nx), range(ny), range(2)):
-        along_x = (c == 1) != last
-        x2, y2 = (x ^ step, y) if along_x else (x, y ^ step)
-        pairs.append(((x * ny + y) * 2 + c, (x2 * ny + y2) * 2 + c))
-    return lax.ppermute(value, ("x", "y", "c"), pairs)
+    for source, index in enumerate(itertools.product(*map(range, shape))):
+        at = names.index(axes[index[3]])
+        target = 0
+        for place, (size, i) in enumerate(zip(shape, index)):
+            target = target * size + (i ^ step if place == at else i)
+        pairs.append((source, target))
+    return lax.ppermute(value, names, pairs)
 
 
 def reorder_kernel(rep, order, features, own):
@@ -61,7 +64,7 @@
 
     def finish(n, carry):
         end = filled[n]
-        for k in range(GROUP):
+        for k in range(2 * GROUP):
             order[end + k] = 0
             spot[end + k] = EMPTY
         groups[n] = (end - n * room + GROUP - 1) // GROUP
@@ -87,22 +90,27 @@
     lax.fori_loop(0, blocks, place_block, 0)
     sources[EMPTY] = jnp.zeros((size, size), jnp.bfloat16)
 
-    for r in range(2):
-        rows = slice(r * size, (r + 1) * size)
-
-        def step(q, acc):
-            at = (kind + r) * room + q * GROUP
-            left = jnp.concatenate([tiles[order[at + k]] for k in range(GROUP)], axis=1)
-            right = jnp.concatenate([sources[spot[at + k]] for k in range(GROUP)], axis=0)
-            return acc + jnp.dot(left, right, preferred_element_type=jnp.float32)
-
-        start = jnp.zeros((size, size), jnp.float32) if before is None else before[rows]
-        out[rows] = lax.fori_loop(0, groups[kind + r], step, start)
-
-
-def dense_kernel(core, rep, order, mine, theirs, weight, bias, cotangent, act, keep, send):
+    out[...] = jnp.zeros_like(out) if before is None else before[...]
+    first, both = groups[kind], groups[kind] + groups[kind + 1]
+
+    def product(q):
+        r = jnp.where(q < first, 0, 1)
+        at = (kind + r) * room + (q - r * first) * GROUP
+        left = jnp.concatenate([tiles[order[at + k]] for k in range(GROUP)], axis=1)
+        right = jnp.concatenate([sources[spot[at + k]] for k in range(GROUP)], axis=0)
+        rows = pl.ds(pl.multiple_of(r * size, size), size)
+        return rows, jnp.dot(left, right, preferred_element_type=jnp.float32)
+
+    def step(i, carry):
+        for rows, value in [product(2 * i), product(2 * i + 1)]:
+            out[rows] += value
+        return carry
+
+    lax.fori_loop(0, (both + 1) // 2, step, 0)
+
+
+def dense_kernel(core, order, mine, theirs, weight, bias, cotangent, act, keep, send):
     nodes = mine.shape[0]
-    half = weight.shape[1] // 2
     part = weight.shape[0] // 2
     hidden = (mine[...] + theirs[...]).astype(jnp.bfloat16)
     where = jnp.concatenate([order[0:1], order[1:2]], axis=1) & (nodes - 1)
@@ -117,30 +125,19 @@
         hidden, scaled, (((0,), (0,)), ((), ())), preferred_element_type=jnp.float32
     )
     column = jnp.sum(scaled.astype(jnp.float32), axis=0, keepdims=True)
-    upper = rep[0] == 1
-    total = jnp.where(upper, total[:, half:], total[:, :half])
-    column = jnp.where(upper, column[:, half:], column[:, :half])
     lower = core[0] == 0
     keep[:part] = jnp.where(lower, total[:part], total[part:])
     send[:part] = jnp.where(lower, total[part:], total[:part])
-    keep[part:] = jnp.broadcast_to(column, (8, half))
-    send[part:] = jnp.broadcast_to(column, (8, half))
-
-
-def pair_kernel(core, own, other, out):
+    keep[part:] = jnp.broadcast_to(column, (8, total.shape[1]))
+    send[part:] = jnp.broadcast_to(column, (8, total.shape[1]))
+
+
+def finish_kernel(scale, core, own, other, weight_grad, bias_grad):
     part = own.shape[0] - 8
     lower = core[0] == 0
-    out[:part] = jnp.where(lower, own[:part], other[:part])
-    out[part : 2 * part] = jnp.where(lower, other[:part], own[:part])
-    out[2 * part :] = own[part:]
-
-
-def finish_kernel(scale, rep, own, other, weight_grad, bias_grad):
-    width, half = own.shape[0] - 8, own.shape[1]
-    left = rep[0] == 0
-    for columns, first, second in ((slice(0, half), own, other), (slice(half, 2 * half), other, own)):
-        weight_grad[:, columns] = jnp.where(left, first[:width], second[:width]) * scale
-        bias_grad[:, columns] = jnp.where(left, first[width : width + 1], second[width : width + 1]) * scale
+    weight_grad[:part] = jnp.where(lower, own[:part], other[:part]) * scale
+    weight_grad[part:] = jnp.where(lower, other[:part], own[:part]) * scale
+    bias_grad[...] = jnp.where(lower, own[part : part + 1], other[part : part + 1]) * scale
 
 
 def kinds_and_places(tile_row, tile_col, me):
@@ -174,14 +171,14 @@
 
     line = jnp.concatenate([own[None]] + [swap(own[None], "z", s) for s in (1, 2, 3)])
     line = lax.optimization_barrier(line)
-    plane = jnp.concatenate([line] + [swap_plane(line, s, False) for s in (1, 2, 3)])
+    plane = jnp.concatenate([line] + [swap_by_core(line, ("y", "x"), s) for s in (1, 2, 3)])
     plane = lax.optimization_barrier(plane)
-    one, two, three = (swap_plane(plane, s, True) for s in (1, 2, 3))
+    one, two, three = (swap_by_core(plane, ("x", "y"), s) for s in (1, 2, 3))
     other = swap(plane, "c", 1)
 
     row, col, _ = lax.optimization_barrier((tile_row, tile_col, plane))
     kind, place = kinds_and_places(row, col, me)
-    entries = jax.ShapeDtypeStruct((KINDS * (slots + GROUP),), jnp.int32)
+    entries = jax.ShapeDtypeStruct((KINDS * (slots + 2 * GROUP),), jnp.int32)
     plan = pl.pallas_call(
         plan_kernel,
         out_shape=(entries, entries, jax.ShapeDtypeStruct((KINDS,), jnp.int32)),
@@ -200,7 +197,7 @@
 def body(features, node_order, tile_vals, tile_row, tile_col, tile_count, weight, bias, cotangent):
     nodes, width = features.shape
     hid = weight.shape[1]
-    half, part = hid // 2, width // 2
+    part = width // 2
     me = lax.axis_index(ROWS)
     core = lax.axis_index("c").reshape(1)
     rep = lax.axis_index("rep").reshape(1)
@@ -219,25 +216,18 @@
         dense_kernel,
         out_shape=(
             jax.ShapeDtypeStruct((nodes, hid), jnp.bfloat16),
-            jax.ShapeDtypeStruct((part + 8, half), jnp.float32),
-            jax.ShapeDtypeStruct((part + 8, half), jnp.float32),
+            jax.ShapeDtypeStruct((part + 8, hid), jnp.float32),
+            jax.ShapeDtypeStruct((part + 8, hid), jnp.float32),
         ),
-        in_specs=[SMEM] * 2 + [VMEM] * 6,
+        in_specs=[SMEM] + [VMEM] * 6,
         out_specs=(VMEM,) * 3,
         compiler_params=pltpu.CompilerParams(vmem_limit_bytes=16 * 2**20),
-    )(core, rep, order, mine, theirs, weight, bias.reshape(1, hid), cotangent)
+    )(core, order, mine, theirs, weight, bias.reshape(1, hid), cotangent)
     total = keep + swap(send, "c", 1)
-    for axis in ("z", "y", "x"):
-        one, two, three = (swap(total, axis, step) for step in (1, 2, 3))
+    for axes in (("z", "x"), ("y", "z"), ("x", "y")):
+        one, two, three = (swap_by_core(total, axes, step) for step in (1, 2, 3))
         total = (total + one) + (two + three)
     scale = float(nodes * lax.axis_size(ROWS)) ** -0.5
-    pair = pl.pallas_call(
-        pair_kernel,
-        out_shape=jax.ShapeDtypeStruct((width + 8, half), jnp.float32),
-        in_specs=[SMEM] + [VMEM] * 2,
-        out_specs=VMEM,
-        compiler_params=pltpu.CompilerParams(vmem_limit_bytes=4 * 2**20),
-    )(core, total, swap(total, "c", 1))
     weight_grad, bias_grad = pl.pallas_call(
         functools.partial(finish_kernel, scale),
         out_shape=(
@@ -247,7 +237,7 @@
         in_specs=[SMEM] + [VMEM] * 2,
         out_specs=(VMEM,) * 2,
         compiler_params=pltpu.CompilerParams(vmem_limit_bytes=4 * 2**20),
-    )(rep, pair, swap(pair, "rep", 1))
+    )(core, total, swap(total, "c", 1))
     return act, weight_grad, bias_grad.reshape(hid)
 
 

time: 91.6 us -> 89.9 us (0.981)
  Pallas kernels: 14.8 us -> 10.9 us
  starting transfers between devices: 38.1 us -> 41 us
    ppermute x20 -> x10, waiting for transfers between devices: 25.2 us -> 10.9 us  [swap(): return lax.ppermute(value, axis, [(i, i ^ step) for i in range(n)])]
    ppermute x6 -> x15, waiting for transfers between devices: 7.14 us -> 20.9 us  [swap_by_core(): return lax.ppermute(value, names, pairs)]
    ppermute x6 -> x15, starting transfers between devices: 6.59 us -> 19 us  [swap_by_core(): return lax.ppermute(value, names, pairs)]
    ppermute x20 -> x10, starting transfers between devices: 31.5 us -> 22 us  [swap(): return lax.ppermute(value, axis, [(i, i ^ step) for i in range(n)])]
    pallas_call x3, Pallas kernels: 7.82 us -> 4.88 us  [products(): pl.pallas_call(functools.partial(tiles_kernel, kind), out_shape=jax.Shape...]
    pallas_call x1, Pallas kernels: 3.56 us -> 2.56 us  [aggregated(): pl.pallas_call(plan_kernel, out_shape=(entries, entries, jax.ShapeDtypeSt...]
  transfers between devices with their start and end apart: 26 -> 25, of which waited for: 16 -> 15; matrix products, arithmetic and copies ran while one was open for 1% -> 1% of each run, Pallas kernels for 9% -> 6%
where the time goes in v3:
time: 89.9 us; the launch traced here: 89.5 us
  starting transfers between devices  41 us (46%)
  waiting for transfers between devices  31.7 us (35%)
  Pallas kernels  10.9 us (12%)
  local copies, waits for them, and re-layouts  2.81 us (3%)
  other arithmetic  1.63 us (2%)
  between operations  1.43 us (2%)
    ppermute x10, starting transfers between devices, swap(): return lax.ppermute(value, axis, [(i, i ^ step) for i in range(n)])  22 us
    ppermute x15, waiting for transfers between devices, swap_by_core(): return lax.ppermute(value, names, pairs)  20.9 us
    ppermute x15, starting transfers between devices, swap_by_core(): return lax.ppermute(value, names, pairs)  19 us
    ppermute x10, waiting for transfers between devices, swap(): return lax.ppermute(value, axis, [(i, i ^ step) for i in range(n)])  10.9 us
    pallas_call x3, Pallas kernels, products(): pl.pallas_call(functools.partial(tiles_kernel, kind), out_shape=jax.Shape...  4.88 us
    unnamed x10, local copies, waits for them, and re-layouts  2.81 us
    pallas_call x1, Pallas kernels, aggregated(): pl.pallas_call(plan_kernel, out_shape=(entries, entries, jax.ShapeDtypeSt...  2.56 us
  transfers between devices with their start and end apart: 25, of which 15 were waited for; matrix products, arithmetic and copies ran while one was open for 1% of the time, Pallas kernels for 6%

profile of v3, /device:TPU:1, one launch (start us, length us, event | category | flops | bytes accessed | tf_op | source)
XLA Modules:
  0.0 89.5 jit_solution(16339961971094561643)
XLA Ops:
  0.6 1.7 %shard_map.112 = bf16[128,128]{1,0:T(8,128)(2,1)} custom-call(s32[1]{0:T(128)} %bitcast.2.rep, s32[2,128]{1,0:T(2,128)} %bitcast.6, bf16[256,128]{1,0:T(8,128)(2,1)} %features.1), custom_call_target="tpu_custom_call" | custom-call | tf_op jit(solution)/shard_map/pallas_call | solution.py:205
  2.3 6.8 %collective-permute-start.2 = (bf16[1,128,128]{2,1,0:T(8,128)(2,1)}, bf16[1,128,128]{2,1,0:T(8,128)(2,1)S(1)}, u32[]{:S(2)}, u32[]{:S(2)}) collective-permute-start(bf16[1,128,128]{2,1,0:T(8,128)(2,1)} %bitcast.9), channel_id=1, source_target_pairs={{0,12},{4,8},{8,4},{12,0},{1,13},{5,9},{9,5},{13,1},{2,14},{6,10},... | collective-permute-start | bytes 98312 | tf_op jit(solution)/shard_map/ppermute | solution.py:24
  11.3 5.0 %collective-permute-done.1 = bf16[1,128,128]{2,1,0:T(8,128)(2,1)S(1)} collective-permute-done((bf16[1,128,128]{2,1,0:T(8,128)(2,1)}, bf16[1,128,128]{2,1,0:T(8,128)(2,1)S(1)}, u32[]{:S(2)}, u32[]{:S(2)}) %collective-permute-start.1) | collective-permute-done | bytes 32800 | tf_op jit(solution)/shard_map/ppermute | solution.py:24
  17.0 2.6 %collective-permute-start.5 = (bf16[4,128,128]{2,1,0:T(8,128)(2,1)S(1)}, bf16[4,128,128]{2,1,0:T(8,128)(2,1)S(1)}, u32[]{:S(2)}, u32[]{:S(2)}) collective-permute-start(bf16[4,128,128]{2,1,0:T(8,128)(2,1)S(1)} %pad_maximum_fusion.1), channel_id=1, source_target_pairs={{0,48},{2,194},{4,52},{6,198},{8,56},{10,202},{12,60},{14,206},{16... | collective-permute-start | bytes 393224 | tf_op jit(solution)/shard_map/ppermute | solution.py:37
  20.3 2.5 %collective-permute-done.5 = bf16[4,128,128]{2,1,0:T(8,128)(2,1)S(1)} collective-permute-done((bf16[4,128,128]{2,1,0:T(8,128)(2,1)S(1)}, bf16[4,128,128]{2,1,0:T(8,128)(2,1)S(1)}, u32[]{:S(2)}, u32[]{:S(2)}) %collective-permute-start.5) | collective-permute-done | bytes 131104 | tf_op jit(solution)/shard_map/ppermute | solution.py:37
  22.9 2.0 %collective-permute-done.4 = bf16[4,128,128]{2,1,0:T(8,128)(2,1)S(1)} collective-permute-done((bf16[4,128,128]{2,1,0:T(8,128)(2,1)S(1)}, bf16[4,128,128]{2,1,0:T(8,128)(2,1)S(1)}, u32[]{:S(2)}, u32[]{:S(2)}) %collective-permute-start.4) | collective-permute-done | bytes 131104 | tf_op jit(solution)/shard_map/ppermute | solution.py:37
  25.0 4.1 %collective-permute-start.9 = (bf16[16,128,128]{2,1,0:T(8,128)(2,1)S(1)}, bf16[16,128,128]{2,1,0:T(8,128)(2,1)S(1)}, u32[]{:S(2)}, u32[]{:S(2)}) collective-permute-start(bf16[16,128,128]{2,1,0:T(8,128)(2,1)S(1)} %pad_maximum_fusion.refs_0_), channel_id=1, source_target_pairs={{0,2},{2,0},{1,3},{3,1},{4,6},{6,4},{5,7},{7,5},{8,10},{10,8},{9,1... | collective-permute-start | bytes 1572872 | tf_op jit(solution)/shard_map/ppermute | solution.py:24
  29.0 1.7 %collective-permute-start.8 = (bf16[16,128,128]{2,1,0:T(8,128)(2,1)S(1)}, bf16[16,128,128]{2,1,0:T(8,128)(2,1)S(1)}, u32[]{:S(2)}, u32[]{:S(2)}) collective-permute-start(bf16[16,128,128]{2,1,0:T(8,128)(2,1)S(1)} %pad_maximum_fusion.refs_0_), channel_id=1, source_target_pairs={{0,192},{2,50},{4,196},{6,54},{8,200},{10,58},{12,204},{14,62},{16... | collective-permute-start | bytes 1572872 | tf_op jit(solution)/shard_map/ppermute | solution.py:37
  33.6 2.6 %shard_map.113 = (s32[1248]{0:T(1024)S(1)}, s32[1248]{0:T(1024)S(1)}, s32[6]{0:T(128)S(1)}) custom-call(s32[192]{0:T(256)S(1)} %get-tuple-element.32.kind, s32[192]{0:T(256)S(1)} %get-tuple-element.31.place, s32[1]{0:T(128)S(6)} %copy.12.count), custom_call_target="tpu_custom_call" | custom-call | tf_op jit(solution)/shard_map/pallas_call | solution.py:182
  36.2 2.8 %copy-done = bf16[192,128,128]{2,1,0:T(8,128)(2,1)S(1)} copy-done((bf16[192,128,128]{2,1,0:T(8,128)(2,1)S(1)}, bf16[192,128,128]{2,1,0:T(8,128)(2,1)}, u32[]{:S(2)}) %copy-start) | copy-done | bytes 6291480
  40.5 3.7 %collective-permute-done.8.refs_3_ = bf16[16,128,128]{2,1,0:T(8,128)(2,1)S(1)} collective-permute-done((bf16[16,128,128]{2,1,0:T(8,128)(2,1)S(1)}, bf16[16,128,128]{2,1,0:T(8,128)(2,1)S(1)}, u32[]{:S(2)}, u32[]{:S(2)}) %collective-permute-start.8) | collective-permute-done | bytes 524320 | tf_op jit(solution)/shard_map/ppermute | solution.py:37
  46.5 1.7 %shard_map.115.refs_0_ = f32[256,128]{1,0:T(8,128)S(1)} custom-call(s32[1248]{0:T(1024)S(1)} %get-tuple-element.19.order, s32[1248]{0:T(1024)S(1)} %get-tuple-element.20.spot, s32[6]{0:T(128)S(1)} %get-tuple-element.21.groups, bf16[192,128,128]{2,1,0:T(8,128)(2,1)S(1)} %copy-done, f32[256,128]{1,0:T(8,128)S(1)} %shard_map.114.refs_0_, ...), custom_call_target="tpu_custom_call" | custom-call | flops 268435456 | bytes 2097152 | tf_op jit(solution)/shard_map/pallas_call | solution.py:160
  49.1 1.7 %shard_map.116.mine = f32[256,128]{1,0:T(8,128)S(1)} custom-call(s32[1248]{0:T(1024)S(1)} %get-tuple-element.19.order, s32[1248]{0:T(1024)S(1)} %get-tuple-element.20.spot, s32[6]{0:T(128)S(1)} %get-tuple-element.21.groups, bf16[192,128,128]{2,1,0:T(8,128)(2,1)S(1)} %copy-done, f32[256,128]{1,0:T(8,128)S(1)} %shard_map.115.refs_0_, ...), custom_call_target="tpu_custom_call" | custom-call | flops 268435456 | bytes 2097152 | tf_op jit(solution)/shard_map/pallas_call | solution.py:160
  51.4 3.3 %collective-permute-done.13.theirs = f32[256,128]{1,0:T(8,128)S(1)} collective-permute-done((f32[256,128]{1,0:T(8,128)S(1)}, f32[256,128]{1,0:T(8,128)S(1)}, u32[]{:S(2)}, u32[]{:S(2)}) %collective-permute-start.13) | collective-permute-done | bytes 131104 | tf_op jit(solution)/shard_map/ppermute | solution.py:24
  55.8 2.1 %collective-permute-start.14 = (f32[72,256]{1,0:T(8,128)S(1)}, f32[72,256]{1,0:T(8,128)S(1)}, u32[]{:S(2)}, u32[]{:S(2)}) collective-permute-start(f32[72,256]{1,0:T(8,128)S(1)} %get-tuple-element.28), channel_id=1, source_target_pairs={{0,2},{2,0},{1,3},{3,1},{4,6},{6,4},{5,7},{7,5},{8,10},{10,8},{9,1... | collective-permute-start | bytes 221192 | tf_op jit(solution)/shard_map/ppermute | solution.py:24
  58.8 2.3 %collective-permute-start.17 = (f32[72,256]{1,0:T(8,128)S(1)}, f32[72,256]{1,0:T(8,128)S(1)}, u32[]{:S(2)}, u32[]{:S(2)}) collective-permute-start(f32[72,256]{1,0:T(8,128)S(1)} %add.59), channel_id=1, source_target_pairs={{0,12},{2,194},{4,8},{6,198},{8,4},{10,202},{12,0},{14,206},{16,28... | collective-permute-start | bytes 221192 | tf_op jit(solution)/shard_map/ppermute | solution.py:37
  63.3 2.5 %collective-permute-done.16 = f32[72,256]{1,0:T(8,128)S(1)} collective-permute-done((f32[72,256]{1,0:T(8,128)S(1)}, f32[72,256]{1,0:T(8,128)S(1)}, u32[]{:S(2)}, u32[]{:S(2)}) %collective-permute-start.16) | collective-permute-done | bytes 73760 | tf_op jit(solution)/shard_map/ppermute | solution.py:37
  65.8 1.8 %collective-permute-start.20 = (f32[72,256]{1,0:T(8,128)S(1)}, f32[72,256]{1,0:T(8,128)S(1)}, u32[]{:S(2)}, u32[]{:S(2)}) collective-permute-start(f32[72,256]{1,0:T(8,128)S(1)} %add_add_fusion.2), channel_id=1, source_target_pairs={{0,48},{2,14},{4,52},{6,10},{8,56},{10,6},{12,60},{14,2},{16,32},{... | collective-permute-start | bytes 221192 | tf_op jit(solution)/shard_map/ppermute | solution.py:37
  67.6 3.4 %collective-permute-start.19 = (f32[72,256]{1,0:T(8,128)S(1)}, f32[72,256]{1,0:T(8,128)S(1)}, u32[]{:S(2)}, u32[]{:S(2)}) collective-permute-start(f32[72,256]{1,0:T(8,128)S(1)} %add_add_fusion.2), channel_id=1, source_target_pairs={{0,32},{2,10},{4,36},{6,14},{8,40},{10,2},{12,44},{14,6},{16,48},{... | collective-permute-start | bytes 221192 | tf_op jit(solution)/shard_map/ppermute | solution.py:37
  71.6 3.3 %collective-permute-done.19 = f32[72,256]{1,0:T(8,128)S(1)} collective-permute-done((f32[72,256]{1,0:T(8,128)S(1)}, f32[72,256]{1,0:T(8,128)S(1)}, u32[]{:S(2)}, u32[]{:S(2)}) %collective-permute-start.19) | collective-permute-done | bytes 73760 | tf_op jit(solution)/shard_map/ppermute | solution.py:37
  74.9 1.9 %collective-permute-done.18 = f32[72,256]{1,0:T(8,128)S(1)} collective-permute-done((f32[72,256]{1,0:T(8,128)S(1)}, f32[72,256]{1,0:T(8,128)S(1)}, u32[]{:S(2)}, u32[]{:S(2)}) %collective-permute-start.18) | collective-permute-done | bytes 73760 | tf_op jit(solution)/shard_map/ppermute | solution.py:37
  76.8 1.8 %collective-permute-start.23 = (f32[72,256]{1,0:T(8,128)S(1)}, f32[72,256]{1,0:T(8,128)S(1)}, u32[]{:S(2)}, u32[]{:S(2)}) collective-permute-start(f32[72,256]{1,0:T(8,128)S(1)} %add_add_fusion.1), channel_id=1, source_target_pairs={{0,192},{2,50},{4,196},{6,54},{8,200},{10,58},{12,204},{14,62},{16... | collective-permute-start | bytes 221192 | tf_op jit(solution)/shard_map/ppermute | solution.py:37
  81.3 2.0 %collective-permute-done.22 = f32[72,256]{1,0:T(8,128)S(1)} collective-permute-done((f32[72,256]{1,0:T(8,128)S(1)}, f32[72,256]{1,0:T(8,128)S(1)}, u32[]{:S(2)}, u32[]{:S(2)}) %collective-permute-start.22) | collective-permute-done | bytes 73760 | tf_op jit(solution)/shard_map/ppermute | solution.py:37
  83.4 4.6 %collective-permute-start.24 = (f32[72,256]{1,0:T(8,128)S(1)}, f32[72,256]{1,0:T(8,128)S(1)}, u32[]{:S(2)}, u32[]{:S(2)}) collective-permute-start(f32[72,256]{1,0:T(8,128)S(1)} %add_add_fusion.own), channel_id=1, source_target_pairs={{0,2},{2,0},{1,3},{3,1},{4,6},{6,4},{5,7},{7,5},{8,10},{10,8},{9,1... | collective-permute-start | bytes 221192 | tf_op jit(solution)/shard_map/ppermute | solution.py:24
  (50 shorter events, 20.4 us)
Async XLA Ops:
  2.3 8.9 %collective-permute-start.2 = (bf16[1,128,128]{2,1,0:T(8,128)(2,1)}, bf16[1,128,128]{2,1,0:T(8,128)(2,1)S(1)}, u32[]{:S(2)}, u32[]{:S(2)}) collective-permute-start(bf16[1,128,128]{2,1,0:T(8,128)(2,1)} %bitcast.9), channel_id=1, source_target_pairs={{0,12},{4,8},{8,4},{12,0},{1,13},{5,9},{9,5},{13,1},{2,14},{6,10},... | collective-permute-start | bytes 98312 | tf_op jit(solution)/shard_map/ppermute | solution.py:24
  9.2 7.1 %collective-permute-start.1 = (bf16[1,128,128]{2,1,0:T(8,128)(2,1)}, bf16[1,128,128]{2,1,0:T(8,128)(2,1)S(1)}, u32[]{:S(2)}, u32[]{:S(2)}) collective-permute-start(bf16[1,128,128]{2,1,0:T(8,128)(2,1)} %bitcast.10), channel_id=1, source_target_pairs={{0,8},{4,12},{8,0},{12,4},{1,9},{5,13},{9,1},{13,5},{2,10},{6,14},... | collective-permute-start | bytes 98312 | tf_op jit(solution)/shard_map/ppermute | solution.py:24
  10.1 6.2 %collective-permute-start = (bf16[1,128,128]{2,1,0:T(8,128)(2,1)}, bf16[1,128,128]{2,1,0:T(8,128)(2,1)S(1)}, u32[]{:S(2)}, u32[]{:S(2)}) collective-permute-start(bf16[1,128,128]{2,1,0:T(8,128)(2,1)} %bitcast.11), channel_id=1, source_target_pairs={{0,4},{4,0},{8,12},{12,8},{1,5},{5,1},{9,13},{13,9},{2,6},{6,2},{1... | collective-permute-start | bytes 98312 | tf_op jit(solution)/shard_map/ppermute | solution.py:24
  17.0 5.9 %collective-permute-start.5 = (bf16[4,128,128]{2,1,0:T(8,128)(2,1)S(1)}, bf16[4,128,128]{2,1,0:T(8,128)(2,1)S(1)}, u32[]{:S(2)}, u32[]{:S(2)}) collective-permute-start(bf16[4,128,128]{2,1,0:T(8,128)(2,1)S(1)} %pad_maximum_fusion.1), channel_id=1, source_target_pairs={{0,48},{2,194},{4,52},{6,198},{8,56},{10,202},{12,60},{14,206},{16... | collective-permute-start | bytes 393224 | tf_op jit(solution)/shard_map/ppermute | solution.py:37
  19.6 5.3 %collective-permute-start.4 = (bf16[4,128,128]{2,1,0:T(8,128)(2,1)S(1)}, bf16[4,128,128]{2,1,0:T(8,128)(2,1)S(1)}, u32[]{:S(2)}, u32[]{:S(2)}) collective-permute-start(bf16[4,128,128]{2,1,0:T(8,128)(2,1)S(1)} %pad_maximum_fusion.1), channel_id=1, source_target_pairs={{0,32},{2,130},{4,36},{6,134},{8,40},{10,138},{12,44},{14,142},{16... | collective-permute-start | bytes 393224 | tf_op jit(solution)/shard_map/ppermute | solution.py:37
  20.1 4.8 %collective-permute-start.3 = (bf16[4,128,128]{2,1,0:T(8,128)(2,1)S(1)}, bf16[4,128,128]{2,1,0:T(8,128)(2,1)S(1)}, u32[]{:S(2)}, u32[]{:S(2)}) collective-permute-start(bf16[4,128,128]{2,1,0:T(8,128)(2,1)S(1)} %pad_maximum_fusion.1), channel_id=1, source_target_pairs={{0,16},{2,66},{4,20},{6,70},{8,24},{10,74},{12,28},{14,78},{16,0},... | collective-permute-start | bytes 393224 | tf_op jit(solution)/shard_map/ppermute | solution.py:37
  25.0 11.3 %collective-permute-start.9 = (bf16[16,128,128]{2,1,0:T(8,128)(2,1)S(1)}, bf16[16,128,128]{2,1,0:T(8,128)(2,1)S(1)}, u32[]{:S(2)}, u32[]{:S(2)}) collective-permute-start(bf16[16,128,128]{2,1,0:T(8,128)(2,1)S(1)} %pad_maximum_fusion.refs_0_), channel_id=1, source_target_pairs={{0,2},{2,0},{1,3},{3,1},{4,6},{6,4},{5,7},{7,5},{8,10},{10,8},{9,1... | collective-permute-start | bytes 1572872 | tf_op jit(solution)/shard_map/ppermute | solution.py:24
  29.0 15.2 %collective-permute-start.8 = (bf16[16,128,128]{2,1,0:T(8,128)(2,1)S(1)}, bf16[16,128,128]{2,1,0:T(8,128)(2,1)S(1)}, u32[]{:S(2)}, u32[]{:S(2)}) collective-permute-start(bf16[16,128,128]{2,1,0:T(8,128)(2,1)S(1)} %pad_maximum_fusion.refs_0_), channel_id=1, source_target_pairs={{0,192},{2,50},{4,196},{6,54},{8,200},{10,58},{12,204},{14,62},{16... | collective-permute-start | bytes 1572872 | tf_op jit(solution)/shard_map/ppermute | solution.py:37
  30.7 13.5 %collective-permute-start.7 = (bf16[16,128,128]{2,1,0:T(8,128)(2,1)S(1)}, bf16[16,128,128]{2,1,0:T(8,128)(2,1)S(1)}, u32[]{:S(2)}, u32[]{:S(2)}) collective-permute-start(bf16[16,128,128]{2,1,0:T(8,128)(2,1)S(1)} %pad_maximum_fusion.refs_0_), channel_id=1, source_target_pairs={{0,128},{2,34},{4,132},{6,38},{8,136},{10,42},{12,140},{14,46},{16... | collective-permute-start | bytes 1572872 | tf_op jit(solution)/shard_map/ppermute | solution.py:37
  31.1 13.7 %collective-permute-start.6 = (bf16[16,128,128]{2,1,0:T(8,128)(2,1)S(1)}, bf16[16,128,128]{2,1,0:T(8,128)(2,1)S(1)}, u32[]{:S(2)}, u32[]{:S(2)}) collective-permute-start(bf16[16,128,128]{2,1,0:T(8,128)(2,1)S(1)} %pad_maximum_fusion.refs_0_), channel_id=1, source_target_pairs={{0,64},{2,18},{4,68},{6,22},{8,72},{10,26},{12,76},{14,30},{16,80}... | collective-permute-start | bytes 1572872 | tf_op jit(solution)/shard_map/ppermute | solution.py:37
  44.8 3.5 %collective-permute-start.10 = (bf16[16,128,128]{2,1,0:T(8,128)(2,1)S(1)}, bf16[16,128,128]{2,1,0:T(8,128)(2,1)S(1)}, u32[]{:S(2)}, u32[]{:S(2)}) collective-permute-start(bf16[16,128,128]{2,1,0:T(8,128)(2,1)S(1)} %collective-permute-done.6.refs_1_), channel_id=1, source_target_pairs={{0,2},{2,0},{1,3},{3,1},{4,6},{6,4},{5,7},{7,5},{8,10},{10,8},{9,1... | collective-permute-start | bytes 1572872 | tf_op jit(solution)/shard_map/ppermute | solution.py:24
  46.0 3.0 %collective-permute-start.12 = (bf16[16,128,128]{2,1,0:T(8,128)(2,1)S(1)}, bf16[16,128,128]{2,1,0:T(8,128)(2,1)S(1)}, u32[]{:S(2)}, u32[]{:S(2)}) collective-permute-start(bf16[16,128,128]{2,1,0:T(8,128)(2,1)S(1)} %collective-permute-done.8.refs_3_), channel_id=1, source_target_pairs={{0,2},{2,0},{1,3},{3,1},{4,6},{6,4},{5,7},{7,5},{8,10},{10,8},{9,1... | collective-permute-start | bytes 1572872 | tf_op jit(solution)/shard_map/ppermute | solution.py:24
  50.8 3.9 %collective-permute-start.13 = (f32[256,128]{1,0:T(8,128)S(1)}, f32[256,128]{1,0:T(8,128)S(1)}, u32[]{:S(2)}, u32[]{:S(2)}) collective-permute-start(f32[256,128]{1,0:T(8,128)S(1)} %shard_map.116.mine), channel_id=1, source_target_pairs={{0,1},{1,0},{2,3},{3,2},{4,5},{5,4},{6,7},{7,6},{8,9},{9,8},{10,11... | collective-permute-start | bytes 393224 | tf_op jit(solution)/shard_map/ppermute | solution.py:24
  55.8 3.0 %collective-permute-start.14 = (f32[72,256]{1,0:T(8,128)S(1)}, f32[72,256]{1,0:T(8,128)S(1)}, u32[]{:S(2)}, u32[]{:S(2)}) collective-permute-start(f32[72,256]{1,0:T(8,128)S(1)} %get-tuple-element.28), channel_id=1, source_target_pairs={{0,2},{2,0},{1,3},{3,1},{4,6},{6,4},{5,7},{7,5},{8,10},{10,8},{9,1... | collective-permute-start | bytes 221192 | tf_op jit(solution)/shard_map/ppermute | solution.py:24
  58.8 4.5 %collective-permute-start.17 = (f32[72,256]{1,0:T(8,128)S(1)}, f32[72,256]{1,0:T(8,128)S(1)}, u32[]{:S(2)}, u32[]{:S(2)}) collective-permute-start(f32[72,256]{1,0:T(8,128)S(1)} %add.59), channel_id=1, source_target_pairs={{0,12},{2,194},{4,8},{6,198},{8,4},{10,202},{12,0},{14,206},{16,28... | collective-permute-start | bytes 221192 | tf_op jit(solution)/shard_map/ppermute | solution.py:37
  61.1 4.7 %collective-permute-start.16 = (f32[72,256]{1,0:T(8,128)S(1)}, f32[72,256]{1,0:T(8,128)S(1)}, u32[]{:S(2)}, u32[]{:S(2)}) collective-permute-start(f32[72,256]{1,0:T(8,128)S(1)} %add.59), channel_id=1, source_target_pairs={{0,8},{2,130},{4,12},{6,134},{8,0},{10,138},{12,4},{14,142},{16,24... | collective-permute-start | bytes 221192 | tf_op jit(solution)/shard_map/ppermute | solution.py:37
  62.1 3.7 %collective-permute-start.15 = (f32[72,256]{1,0:T(8,128)S(1)}, f32[72,256]{1,0:T(8,128)S(1)}, u32[]{:S(2)}, u32[]{:S(2)}) collective-permute-start(f32[72,256]{1,0:T(8,128)S(1)} %add.59), channel_id=1, source_target_pairs={{0,4},{2,66},{4,0},{6,70},{8,12},{10,74},{12,8},{14,78},{16,20},{1... | collective-permute-start | bytes 221192 | tf_op jit(solution)/shard_map/ppermute | solution.py:37
  65.8 5.7 %collective-permute-start.20 = (f32[72,256]{1,0:T(8,128)S(1)}, f32[72,256]{1,0:T(8,128)S(1)}, u32[]{:S(2)}, u32[]{:S(2)}) collective-permute-start(f32[72,256]{1,0:T(8,128)S(1)} %add_add_fusion.2), channel_id=1, source_target_pairs={{0,48},{2,14},{4,52},{6,10},{8,56},{10,6},{12,60},{14,2},{16,32},{... | collective-permute-start | bytes 221192 | tf_op jit(solution)/shard_map/ppermute | solution.py:37
  67.6 7.3 %collective-permute-start.19 = (f32[72,256]{1,0:T(8,128)S(1)}, f32[72,256]{1,0:T(8,128)S(1)}, u32[]{:S(2)}, u32[]{:S(2)}) collective-permute-start(f32[72,256]{1,0:T(8,128)S(1)} %add_add_fusion.2), channel_id=1, source_target_pairs={{0,32},{2,10},{4,36},{6,14},{8,40},{10,2},{12,44},{14,6},{16,48},{... | collective-permute-start | bytes 221192 | tf_op jit(solution)/shard_map/ppermute | solution.py:37
  71.0 5.8 %collective-permute-start.18 = (f32[72,256]{1,0:T(8,128)S(1)}, f32[72,256]{1,0:T(8,128)S(1)}, u32[]{:S(2)}, u32[]{:S(2)}) collective-permute-start(f32[72,256]{1,0:T(8,128)S(1)} %add_add_fusion.2), channel_id=1, source_target_pairs={{0,16},{2,6},{4,20},{6,2},{8,24},{10,14},{12,28},{14,10},{16,0},{1... | collective-permute-start | bytes 221192 | tf_op jit(solution)/shard_map/ppermute | solution.py:37
  76.8 4.5 %collective-permute-start.23 = (f32[72,256]{1,0:T(8,128)S(1)}, f32[72,256]{1,0:T(8,128)S(1)}, u32[]{:S(2)}, u32[]{:S(2)}) collective-permute-start(f32[72,256]{1,0:T(8,128)S(1)} %add_add_fusion.1), channel_id=1, source_target_pairs={{0,192},{2,50},{4,196},{6,54},{8,200},{10,58},{12,204},{14,62},{16... | collective-permute-start | bytes 221192 | tf_op jit(solution)/shard_map/ppermute | solution.py:37
  78.6 4.7 %collective-permute-start.22 = (f32[72,256]{1,0:T(8,128)S(1)}, f32[72,256]{1,0:T(8,128)S(1)}, u32[]{:S(2)}, u32[]{:S(2)}) collective-permute-start(f32[72,256]{1,0:T(8,128)S(1)} %add_add_fusion.1), channel_id=1, source_target_pairs={{0,128},{2,34},{4,132},{6,38},{8,136},{10,42},{12,140},{14,46},{16... | collective-permute-start | bytes 221192 | tf_op jit(solution)/shard_map/ppermute | solution.py:37
  79.0 4.3 %collective-permute-start.21 = (f32[72,256]{1,0:T(8,128)S(1)}, f32[72,256]{1,0:T(8,128)S(1)}, u32[]{:S(2)}, u32[]{:S(2)}) collective-permute-start(f32[72,256]{1,0:T(8,128)S(1)} %add_add_fusion.1), channel_id=1, source_target_pairs={{0,64},{2,18},{4,68},{6,22},{8,72},{10,26},{12,76},{14,30},{16,80}... | collective-permute-start | bytes 221192 | tf_op jit(solution)/shard_map/ppermute | solution.py:37
  83.4 5.5 %collective-permute-start.24 = (f32[72,256]{1,0:T(8,128)S(1)}, f32[72,256]{1,0:T(8,128)S(1)}, u32[]{:S(2)}, u32[]{:S(2)}) collective-permute-start(f32[72,256]{1,0:T(8,128)S(1)} %add_add_fusion.own), channel_id=1, source_target_pairs={{0,2},{2,0},{1,3},{3,1},{4,6},{6,4},{5,7},{7,5},{8,10},{10,8},{9,1... | collective-permute-start | bytes 221192 | tf_op jit(solution)/shard_map/ppermute | solution.py:24
  (6 other events, 62.2 us)

commit v4 on v3

--- a/solution.py
+++ b/solution.py
@@ -45,6 +45,10 @@
     own[...] = lax.dot_general(
         pick, features[...], (((0,), (0,)), ((), ())), preferred_element_type=jnp.float32
     ).astype(jnp.bfloat16)
+
+
+def copy_kernel(source, target):
+    target[...] = source[...]
 
 
 def plan_kernel(kind, place, count, order, spot, groups, filled):
@@ -169,7 +173,14 @@
             ),
         )(*plan, tile_vals, *before, *pieces)
 
-    line = jnp.concatenate([own[None]] + [swap(own[None], "z", s) for s in (1, 2, 3)])
+    here = pl.pallas_call(
+        copy_kernel,
+        out_shape=jax.ShapeDtypeStruct((1, *own.shape), own.dtype),
+        in_specs=[VMEM],
+        out_specs=VMEM,
+        compiler_params=pltpu.CompilerParams(vmem_limit_bytes=4 * 2**20),
+    )(own[None])
+    line = jnp.concatenate([here] + [swap(own[None], "z", s) for s in (1, 2, 3)])
     line = lax.optimization_barrier(line)
     plane = jnp.concatenate([line] + [swap_by_core(line, ("y", "x"), s) for s in (1, 2, 3)])
     plane = lax.optimization_barrier(plane)
@@ -188,7 +199,7 @@
         compiler_params=pltpu.CompilerParams(vmem_limit_bytes=4 * 2**20),
     )(kind, place, tile_count)
     total = products(0, None, [plane, other])
-    one, two, three, total = lax.optimization_barrier((one, two, three, total))
+    three, total = lax.optimization_barrier((three, total))
     others = [swap(p, "c", 1) for p in (one, two, three)]
     total = products(2, total, [one, two, three])
     return products(4, total, others)

time: 89.9 us -> 90.9 us (1.011)
  starting transfers between devices: 41 us -> 45.6 us
  waiting for transfers between devices: 31.7 us -> 28.5 us
    ppermute x15, starting transfers between devices: 19 us -> 21.4 us  [swap_by_core(): return lax.ppermute(value, names, pairs)]
    ppermute x15, waiting for transfers between devices: 20.9 us -> 18.5 us  [swap_by_core(): return lax.ppermute(value, names, pairs)]
    ppermute x10, starting transfers between devices: 22 us -> 24.1 us  [swap(): return lax.ppermute(value, axis, [(i, i ^ step) for i in range(n)])]
    unnamed x10 -> x12, local copies, waits for them, and re-layouts: 2.81 us -> 3.63 us
  transfers between devices with their start and end apart: 25 -> 25, of which waited for: 15 -> 13; matrix products, arithmetic and copies ran while one was open for 1% -> 1% of each run, Pallas kernels for 6% -> 6%
where the time goes in v4:
time: 90.9 us; the launch traced here: 90.6 us
  starting transfers between devices  45.6 us (50%)
  waiting for transfers between devices  28.5 us (31%)
  Pallas kernels  10.6 us (12%)
  local copies, waits for them, and re-layouts  3.63 us (4%)
  between operations  1.46 us (2%)
    ppermute x10, starting transfers between devices, swap(): return lax.ppermute(value, axis, [(i, i ^ step) for i in range(n)])  24.1 us
    ppermute x15, starting transfers between devices, swap_by_core(): return lax.ppermute(value, names, pairs)  21.4 us
    ppermute x15, waiting for transfers between devices, swap_by_core(): return lax.ppermute(value, names, pairs)  18.5 us
    ppermute x10, waiting for transfers between devices, swap(): return lax.ppermute(value, axis, [(i, i ^ step) for i in range(n)])  9.99 us
    pallas_call x3, Pallas kernels, products(): pl.pallas_call(functools.partial(tiles_kernel, kind), out_shape=jax.Shape...  4.58 us
    unnamed x12, local copies, waits for them, and re-layouts  3.63 us
    pallas_call x1, Pallas kernels, aggregated(): pl.pallas_call(plan_kernel, out_shape=(entries, entries, jax.ShapeDtypeSt...  2.56 us
  transfers between devices with their start and end apart: 25, of which 13 were waited for; matrix products, arithmetic and copies ran while one was open for 1% of the time, Pallas kernels for 6%

profile of v4, /device:TPU:1, one launch (start us, length us, event | category | flops | bytes accessed | tf_op | source)
XLA Modules:
  0.0 90.6 jit_solution(2682720938180066434)
XLA Ops:
  0.6 1.7 %shard_map.112 = bf16[128,128]{1,0:T(8,128)(2,1)} custom-call(s32[1]{0:T(128)} %bitcast.2.rep, s32[2,128]{1,0:T(2,128)} %bitcast.10, bf16[256,128]{1,0:T(8,128)(2,1)} %features.1), custom_call_target="tpu_custom_call" | custom-call | tf_op jit(solution)/shard_map/pallas_call | solution.py:216
  2.3 3.8 %collective-permute-start = (bf16[1,128,128]{2,1,0:T(8,128)(2,1)}, bf16[1,128,128]{2,1,0:T(8,128)(2,1)S(1)}, u32[]{:S(2)}, u32[]{:S(2)}) collective-permute-start(bf16[1,128,128]{2,1,0:T(8,128)(2,1)} %bitcast.6), channel_id=1, source_target_pairs={{0,4},{4,0},{8,12},{12,8},{1,5},{5,1},{9,13},{13,9},{2,6},{6,2},{1... | collective-permute-start | bytes 98312 | tf_op jit(solution)/shard_map/ppermute | solution.py:24
  6.1 5.1 %collective-permute-start.1 = (bf16[1,128,128]{2,1,0:T(8,128)(2,1)}, bf16[1,128,128]{2,1,0:T(8,128)(2,1)S(1)}, u32[]{:S(2)}, u32[]{:S(2)}) collective-permute-start(bf16[1,128,128]{2,1,0:T(8,128)(2,1)} %bitcast.7), channel_id=1, source_target_pairs={{0,8},{4,12},{8,0},{12,4},{1,9},{5,13},{9,1},{13,5},{2,10},{6,14},... | collective-permute-start | bytes 98312 | tf_op jit(solution)/shard_map/ppermute | solution.py:24
  13.1 3.2 %collective-permute-done.2 = bf16[1,128,128]{2,1,0:T(8,128)(2,1)S(1)} collective-permute-done((bf16[1,128,128]{2,1,0:T(8,128)(2,1)}, bf16[1,128,128]{2,1,0:T(8,128)(2,1)S(1)}, u32[]{:S(2)}, u32[]{:S(2)}) %collective-permute-start.2) | collective-permute-done | bytes 32800 | tf_op jit(solution)/shard_map/ppermute | solution.py:24
  17.7 2.4 %collective-permute-start.4 = (bf16[4,128,128]{2,1,0:T(8,128)(2,1)S(1)}, bf16[4,128,128]{2,1,0:T(8,128)(2,1)S(1)}, u32[]{:S(2)}, u32[]{:S(2)}) collective-permute-start(bf16[4,128,128]{2,1,0:T(8,128)(2,1)S(1)} %pad_maximum_fusion.1), channel_id=1, source_target_pairs={{0,32},{2,130},{4,36},{6,134},{8,40},{10,138},{12,44},{14,142},{16... | collective-permute-start | bytes 393224 | tf_op jit(solution)/shard_map/ppermute | solution.py:37
  20.3 3.6 %collective-permute-done.4 = bf16[4,128,128]{2,1,0:T(8,128)(2,1)S(1)} collective-permute-done((bf16[4,128,128]{2,1,0:T(8,128)(2,1)S(1)}, bf16[4,128,128]{2,1,0:T(8,128)(2,1)S(1)}, u32[]{:S(2)}, u32[]{:S(2)}) %collective-permute-start.4) | collective-permute-done | bytes 131104 | tf_op jit(solution)/shard_map/ppermute | solution.py:37
  25.3 4.3 %collective-permute-start.7 = (bf16[16,128,128]{2,1,0:T(8,128)(2,1)S(1)}, bf16[16,128,128]{2,1,0:T(8,128)(2,1)S(1)}, u32[]{:S(2)}, u32[]{:S(2)}) collective-permute-start(bf16[16,128,128]{2,1,0:T(8,128)(2,1)S(1)} %pad_maximum_fusion.refs_0_), channel_id=1, source_target_pairs={{0,2},{2,0},{1,3},{3,1},{4,6},{6,4},{5,7},{7,5},{8,10},{10,8},{9,1... | collective-permute-start | bytes 1572872 | tf_op jit(solution)/shard_map/ppermute | solution.py:24
  30.3 3.2 %collective-permute-start.9 = (bf16[16,128,128]{2,1,0:T(8,128)(2,1)S(1)}, bf16[16,128,128]{2,1,0:T(8,128)(2,1)S(1)}, u32[]{:S(2)}, u32[]{:S(2)}) collective-permute-start(bf16[16,128,128]{2,1,0:T(8,128)(2,1)S(1)} %pad_maximum_fusion.refs_0_), channel_id=1, source_target_pairs={{0,128},{2,34},{4,132},{6,38},{8,136},{10,42},{12,140},{14,46},{16... | collective-permute-start | bytes 1572872 | tf_op jit(solution)/shard_map/ppermute | solution.py:37
  34.9 2.6 %shard_map.114 = (s32[1248]{0:T(1024)S(1)}, s32[1248]{0:T(1024)S(1)}, s32[6]{0:T(128)S(1)}) custom-call(s32[192]{0:T(256)S(1)} %get-tuple-element.28.kind, s32[192]{0:T(256)S(1)} %get-tuple-element.27.place, s32[1]{0:T(128)S(6)} %copy.12.count), custom_call_target="tpu_custom_call" | custom-call | tf_op jit(solution)/shard_map/pallas_call | solution.py:193
  37.5 2.8 %copy-done = bf16[192,128,128]{2,1,0:T(8,128)(2,1)S(1)} copy-done((bf16[192,128,128]{2,1,0:T(8,128)(2,1)S(1)}, bf16[192,128,128]{2,1,0:T(8,128)(2,1)}, u32[]{:S(2)}) %copy-start) | copy-done | bytes 6291480
  42.8 3.2 %collective-permute-done.9.refs_2_ = bf16[16,128,128]{2,1,0:T(8,128)(2,1)S(1)} collective-permute-done((bf16[16,128,128]{2,1,0:T(8,128)(2,1)S(1)}, bf16[16,128,128]{2,1,0:T(8,128)(2,1)S(1)}, u32[]{:S(2)}, u32[]{:S(2)}) %collective-permute-start.9) | collective-permute-done | bytes 524320 | tf_op jit(solution)/shard_map/ppermute | solution.py:37
  47.2 1.7 %shard_map.116.refs_0_ = f32[256,128]{1,0:T(8,128)S(1)} custom-call(s32[1248]{0:T(1024)S(1)} %get-tuple-element.17.order, s32[1248]{0:T(1024)S(1)} %get-tuple-element.18.spot, s32[6]{0:T(128)S(1)} %get-tuple-element.19.groups, bf16[192,128,128]{2,1,0:T(8,128)(2,1)S(1)} %copy-done, f32[256,128]{1,0:T(8,128)S(1)} %shard_map.115.refs_0_, ...), custom_call_target="tpu_custom_call" | custom-call | flops 268435456 | bytes 2097152 | tf_op jit(solution)/shard_map/pallas_call | solution.py:164
  49.0 1.7 %shard_map.117.mine = f32[256,128]{1,0:T(8,128)S(1)} custom-call(s32[1248]{0:T(1024)S(1)} %get-tuple-element.17.order, s32[1248]{0:T(1024)S(1)} %get-tuple-element.18.spot, s32[6]{0:T(128)S(1)} %get-tuple-element.19.groups, bf16[192,128,128]{2,1,0:T(8,128)(2,1)S(1)} %copy-done, f32[256,128]{1,0:T(8,128)S(1)} %shard_map.116.refs_0_, ...), custom_call_target="tpu_custom_call" | custom-call | flops 268435456 | bytes 2097152 | tf_op jit(solution)/shard_map/pallas_call | solution.py:164
  50.7 2.0 %collective-permute-start.13 = (f32[256,128]{1,0:T(8,128)S(1)}, f32[256,128]{1,0:T(8,128)S(1)}, u32[]{:S(2)}, u32[]{:S(2)}) collective-permute-start(f32[256,128]{1,0:T(8,128)S(1)} %shard_map.117.mine), channel_id=1, source_target_pairs={{0,1},{1,0},{2,3},{3,2},{4,5},{5,4},{6,7},{7,6},{8,9},{9,8},{10,11... | collective-permute-start | bytes 393224 | tf_op jit(solution)/shard_map/ppermute | solution.py:24
  52.7 3.9 %collective-permute-done.13.theirs = f32[256,128]{1,0:T(8,128)S(1)} collective-permute-done((f32[256,128]{1,0:T(8,128)S(1)}, f32[256,128]{1,0:T(8,128)S(1)}, u32[]{:S(2)}, u32[]{:S(2)}) %collective-permute-start.13) | collective-permute-done | bytes 131104 | tf_op jit(solution)/shard_map/ppermute | solution.py:24
  59.3 3.2 %collective-permute-start.16 = (f32[72,256]{1,0:T(8,128)S(1)}, f32[72,256]{1,0:T(8,128)S(1)}, u32[]{:S(2)}, u32[]{:S(2)}) collective-permute-start(f32[72,256]{1,0:T(8,128)S(1)} %add.59), channel_id=1, source_target_pairs={{0,8},{2,130},{4,12},{6,134},{8,0},{10,138},{12,4},{14,142},{16,24... | collective-permute-start | bytes 221192 | tf_op jit(solution)/shard_map/ppermute | solution.py:37
  63.1 1.9 %collective-permute-done.16 = f32[72,256]{1,0:T(8,128)S(1)} collective-permute-done((f32[72,256]{1,0:T(8,128)S(1)}, f32[72,256]{1,0:T(8,128)S(1)}, u32[]{:S(2)}, u32[]{:S(2)}) %collective-permute-start.16) | collective-permute-done | bytes 73760 | tf_op jit(solution)/shard_map/ppermute | solution.py:37
  65.0 1.9 %collective-permute-done.17 = f32[72,256]{1,0:T(8,128)S(1)} collective-permute-done((f32[72,256]{1,0:T(8,128)S(1)}, f32[72,256]{1,0:T(8,128)S(1)}, u32[]{:S(2)}, u32[]{:S(2)}) %collective-permute-start.17) | collective-permute-done | bytes 73760 | tf_op jit(solution)/shard_map/ppermute | solution.py:37
  66.9 1.6 %collective-permute-start.18 = (f32[72,256]{1,0:T(8,128)S(1)}, f32[72,256]{1,0:T(8,128)S(1)}, u32[]{:S(2)}, u32[]{:S(2)}) collective-permute-start(f32[72,256]{1,0:T(8,128)S(1)} %add_add_fusion.2), channel_id=1, source_target_pairs={{0,16},{2,6},{4,20},{6,2},{8,24},{10,14},{12,28},{14,10},{16,0},{1... | collective-permute-start | bytes 221192 | tf_op jit(solution)/shard_map/ppermute | solution.py:37
  69.6 3.0 %collective-permute-start.20 = (f32[72,256]{1,0:T(8,128)S(1)}, f32[72,256]{1,0:T(8,128)S(1)}, u32[]{:S(2)}, u32[]{:S(2)}) collective-permute-start(f32[72,256]{1,0:T(8,128)S(1)} %add_add_fusion.2), channel_id=1, source_target_pairs={{0,48},{2,14},{4,52},{6,10},{8,56},{10,6},{12,60},{14,2},{16,32},{... | collective-permute-start | bytes 221192 | tf_op jit(solution)/shard_map/ppermute | solution.py:37
  72.7 3.7 %collective-permute-done.19 = f32[72,256]{1,0:T(8,128)S(1)} collective-permute-done((f32[72,256]{1,0:T(8,128)S(1)}, f32[72,256]{1,0:T(8,128)S(1)}, u32[]{:S(2)}, u32[]{:S(2)}) %collective-permute-start.19) | collective-permute-done | bytes 73760 | tf_op jit(solution)/shard_map/ppermute | solution.py:37
  76.5 2.3 %collective-permute-start.22 = (f32[72,256]{1,0:T(8,128)S(1)}, f32[72,256]{1,0:T(8,128)S(1)}, u32[]{:S(2)}, u32[]{:S(2)}) collective-permute-start(f32[72,256]{1,0:T(8,128)S(1)} %add_add_fusion.1), channel_id=1, source_target_pairs={{0,128},{2,34},{4,132},{6,38},{8,136},{10,42},{12,140},{14,46},{16... | collective-permute-start | bytes 221192 | tf_op jit(solution)/shard_map/ppermute | solution.py:37
  81.3 1.9 %collective-permute-done.23 = f32[72,256]{1,0:T(8,128)S(1)} collective-permute-done((f32[72,256]{1,0:T(8,128)S(1)}, f32[72,256]{1,0:T(8,128)S(1)}, u32[]{:S(2)}, u32[]{:S(2)}) %collective-permute-start.23) | collective-permute-done | bytes 73760 | tf_op jit(solution)/shard_map/ppermute | solution.py:37
  83.3 5.7 %collective-permute-start.24 = (f32[72,256]{1,0:T(8,128)S(1)}, f32[72,256]{1,0:T(8,128)S(1)}, u32[]{:S(2)}, u32[]{:S(2)}) collective-permute-start(f32[72,256]{1,0:T(8,128)S(1)} %add_add_fusion.own), channel_id=1, source_target_pairs={{0,2},{2,0},{1,3},{3,1},{4,6},{6,4},{5,7},{7,5},{8,10},{10,8},{9,1... | collective-permute-start | bytes 221192 | tf_op jit(solution)/shard_map/ppermute | solution.py:24
  (53 shorter events, 18.7 us)
Async XLA Ops:
  2.3 9.8 %collective-permute-start = (bf16[1,128,128]{2,1,0:T(8,128)(2,1)}, bf16[1,128,128]{2,1,0:T(8,128)(2,1)S(1)}, u32[]{:S(2)}, u32[]{:S(2)}) collective-permute-start(bf16[1,128,128]{2,1,0:T(8,128)(2,1)} %bitcast.6), channel_id=1, source_target_pairs={{0,4},{4,0},{8,12},{12,8},{1,5},{5,1},{9,13},{13,9},{2,6},{6,2},{1... | collective-permute-start | bytes 98312 | tf_op jit(solution)/shard_map/ppermute | solution.py:24
  6.1 7.0 %collective-permute-start.1 = (bf16[1,128,128]{2,1,0:T(8,128)(2,1)}, bf16[1,128,128]{2,1,0:T(8,128)(2,1)S(1)}, u32[]{:S(2)}, u32[]{:S(2)}) collective-permute-start(bf16[1,128,128]{2,1,0:T(8,128)(2,1)} %bitcast.7), channel_id=1, source_target_pairs={{0,8},{4,12},{8,0},{12,4},{1,9},{5,13},{9,1},{13,5},{2,10},{6,14},... | collective-permute-start | bytes 98312 | tf_op jit(solution)/shard_map/ppermute | solution.py:24
  11.2 5.1 %collective-permute-start.2 = (bf16[1,128,128]{2,1,0:T(8,128)(2,1)}, bf16[1,128,128]{2,1,0:T(8,128)(2,1)S(1)}, u32[]{:S(2)}, u32[]{:S(2)}) collective-permute-start(bf16[1,128,128]{2,1,0:T(8,128)(2,1)} %bitcast.8), channel_id=1, source_target_pairs={{0,12},{4,8},{8,4},{12,0},{1,13},{5,9},{9,5},{13,1},{2,14},{6,10},... | collective-permute-start | bytes 98312 | tf_op jit(solution)/shard_map/ppermute | solution.py:24
  16.4 3.9 %collective-permute-start.3 = (bf16[4,128,128]{2,1,0:T(8,128)(2,1)S(1)}, bf16[4,128,128]{2,1,0:T(8,128)(2,1)S(1)}, u32[]{:S(2)}, u32[]{:S(2)}) collective-permute-start(bf16[4,128,128]{2,1,0:T(8,128)(2,1)S(1)} %pad_maximum_fusion.1), channel_id=1, source_target_pairs={{0,16},{2,66},{4,20},{6,70},{8,24},{10,74},{12,28},{14,78},{16,0},... | collective-permute-start | bytes 393224 | tf_op jit(solution)/shard_map/ppermute | solution.py:37
  17.7 6.2 %collective-permute-start.4 = (bf16[4,128,128]{2,1,0:T(8,128)(2,1)S(1)}, bf16[4,128,128]{2,1,0:T(8,128)(2,1)S(1)}, u32[]{:S(2)}, u32[]{:S(2)}) collective-permute-start(bf16[4,128,128]{2,1,0:T(8,128)(2,1)S(1)} %pad_maximum_fusion.1), channel_id=1, source_target_pairs={{0,32},{2,130},{4,36},{6,134},{8,40},{10,138},{12,44},{14,142},{16... | collective-permute-start | bytes 393224 | tf_op jit(solution)/shard_map/ppermute | solution.py:37
  20.1 5.2 %collective-permute-start.5 = (bf16[4,128,128]{2,1,0:T(8,128)(2,1)S(1)}, bf16[4,128,128]{2,1,0:T(8,128)(2,1)S(1)}, u32[]{:S(2)}, u32[]{:S(2)}) collective-permute-start(bf16[4,128,128]{2,1,0:T(8,128)(2,1)S(1)} %pad_maximum_fusion.1), channel_id=1, source_target_pairs={{0,48},{2,194},{4,52},{6,198},{8,56},{10,202},{12,60},{14,206},{16... | collective-permute-start | bytes 393224 | tf_op jit(solution)/shard_map/ppermute | solution.py:37
  25.3 12.1 %collective-permute-start.7 = (bf16[16,128,128]{2,1,0:T(8,128)(2,1)S(1)}, bf16[16,128,128]{2,1,0:T(8,128)(2,1)S(1)}, u32[]{:S(2)}, u32[]{:S(2)}) collective-permute-start(bf16[16,128,128]{2,1,0:T(8,128)(2,1)S(1)} %pad_maximum_fusion.refs_0_), channel_id=1, source_target_pairs={{0,2},{2,0},{1,3},{3,1},{4,6},{6,4},{5,7},{7,5},{8,10},{10,8},{9,1... | collective-permute-start | bytes 1572872 | tf_op jit(solution)/shard_map/ppermute | solution.py:24
  29.6 11.8 %collective-permute-start.6 = (bf16[16,128,128]{2,1,0:T(8,128)(2,1)S(1)}, bf16[16,128,128]{2,1,0:T(8,128)(2,1)S(1)}, u32[]{:S(2)}, u32[]{:S(2)}) collective-permute-start(bf16[16,128,128]{2,1,0:T(8,128)(2,1)S(1)} %pad_maximum_fusion.refs_0_), channel_id=1, source_target_pairs={{0,192},{2,50},{4,196},{6,54},{8,200},{10,58},{12,204},{14,62},{16... | collective-permute-start | bytes 1572872 | tf_op jit(solution)/shard_map/ppermute | solution.py:37
  30.3 12.4 %collective-permute-start.8 = (bf16[16,128,128]{2,1,0:T(8,128)(2,1)S(1)}, bf16[16,128,128]{2,1,0:T(8,128)(2,1)S(1)}, u32[]{:S(2)}, u32[]{:S(2)}) collective-permute-start(bf16[16,128,128]{2,1,0:T(8,128)(2,1)S(1)} %pad_maximum_fusion.refs_0_), channel_id=1, source_target_pairs={{0,64},{2,18},{4,68},{6,22},{8,72},{10,26},{12,76},{14,30},{16,80}... | collective-permute-start | bytes 1572872 | tf_op jit(solution)/shard_map/ppermute | solution.py:37
  30.3 15.6 %collective-permute-start.9 = (bf16[16,128,128]{2,1,0:T(8,128)(2,1)S(1)}, bf16[16,128,128]{2,1,0:T(8,128)(2,1)S(1)}, u32[]{:S(2)}, u32[]{:S(2)}) collective-permute-start(bf16[16,128,128]{2,1,0:T(8,128)(2,1)S(1)} %pad_maximum_fusion.refs_0_), channel_id=1, source_target_pairs={{0,128},{2,34},{4,132},{6,38},{8,136},{10,42},{12,140},{14,46},{16... | collective-permute-start | bytes 1572872 | tf_op jit(solution)/shard_map/ppermute | solution.py:37
  41.4 7.5 %collective-permute-start.12 = (bf16[16,128,128]{2,1,0:T(8,128)(2,1)S(1)}, bf16[16,128,128]{2,1,0:T(8,128)(2,1)S(1)}, u32[]{:S(2)}, u32[]{:S(2)}) collective-permute-start(bf16[16,128,128]{2,1,0:T(8,128)(2,1)S(1)} %collective-permute-done.6.refs_3_), channel_id=1, source_target_pairs={{0,2},{2,0},{1,3},{3,1},{4,6},{6,4},{5,7},{7,5},{8,10},{10,8},{9,1... | collective-permute-start | bytes 1572872 | tf_op jit(solution)/shard_map/ppermute | solution.py:24
  42.7 6.3 %collective-permute-start.10 = (bf16[16,128,128]{2,1,0:T(8,128)(2,1)S(1)}, bf16[16,128,128]{2,1,0:T(8,128)(2,1)S(1)}, u32[]{:S(2)}, u32[]{:S(2)}) collective-permute-start(bf16[16,128,128]{2,1,0:T(8,128)(2,1)S(1)} %collective-permute-done.8.refs_1_), channel_id=1, source_target_pairs={{0,2},{2,0},{1,3},{3,1},{4,6},{6,4},{5,7},{7,5},{8,10},{10,8},{9,1... | collective-permute-start | bytes 1572872 | tf_op jit(solution)/shard_map/ppermute | solution.py:24
  46.0 3.0 %collective-permute-start.11 = (bf16[16,128,128]{2,1,0:T(8,128)(2,1)S(1)}, bf16[16,128,128]{2,1,0:T(8,128)(2,1)S(1)}, u32[]{:S(2)}, u32[]{:S(2)}) collective-permute-start(bf16[16,128,128]{2,1,0:T(8,128)(2,1)S(1)} %collective-permute-done.9.refs_2_), channel_id=1, source_target_pairs={{0,2},{2,0},{1,3},{3,1},{4,6},{6,4},{5,7},{7,5},{8,10},{10,8},{9,1... | collective-permute-start | bytes 1572872 | tf_op jit(solution)/shard_map/ppermute | solution.py:24
  50.7 5.9 %collective-permute-start.13 = (f32[256,128]{1,0:T(8,128)S(1)}, f32[256,128]{1,0:T(8,128)S(1)}, u32[]{:S(2)}, u32[]{:S(2)}) collective-permute-start(f32[256,128]{1,0:T(8,128)S(1)} %shard_map.117.mine), channel_id=1, source_target_pairs={{0,1},{1,0},{2,3},{3,2},{4,5},{5,4},{6,7},{7,6},{8,9},{9,8},{10,11... | collective-permute-start | bytes 393224 | tf_op jit(solution)/shard_map/ppermute | solution.py:24
  59.2 4.0 %collective-permute-start.15 = (f32[72,256]{1,0:T(8,128)S(1)}, f32[72,256]{1,0:T(8,128)S(1)}, u32[]{:S(2)}, u32[]{:S(2)}) collective-permute-start(f32[72,256]{1,0:T(8,128)S(1)} %add.59), channel_id=1, source_target_pairs={{0,4},{2,66},{4,0},{6,70},{8,12},{10,74},{12,8},{14,78},{16,20},{1... | collective-permute-start | bytes 221192 | tf_op jit(solution)/shard_map/ppermute | solution.py:37
  59.3 5.7 %collective-permute-start.16 = (f32[72,256]{1,0:T(8,128)S(1)}, f32[72,256]{1,0:T(8,128)S(1)}, u32[]{:S(2)}, u32[]{:S(2)}) collective-permute-start(f32[72,256]{1,0:T(8,128)S(1)} %add.59), channel_id=1, source_target_pairs={{0,8},{2,130},{4,12},{6,134},{8,0},{10,138},{12,4},{14,142},{16,24... | collective-permute-start | bytes 221192 | tf_op jit(solution)/shard_map/ppermute | solution.py:37
  62.5 4.4 %collective-permute-start.17 = (f32[72,256]{1,0:T(8,128)S(1)}, f32[72,256]{1,0:T(8,128)S(1)}, u32[]{:S(2)}, u32[]{:S(2)}) collective-permute-start(f32[72,256]{1,0:T(8,128)S(1)} %add.59), channel_id=1, source_target_pairs={{0,12},{2,194},{4,8},{6,198},{8,4},{10,202},{12,0},{14,206},{16,28... | collective-permute-start | bytes 221192 | tf_op jit(solution)/shard_map/ppermute | solution.py:37
  66.9 5.7 %collective-permute-start.18 = (f32[72,256]{1,0:T(8,128)S(1)}, f32[72,256]{1,0:T(8,128)S(1)}, u32[]{:S(2)}, u32[]{:S(2)}) collective-permute-start(f32[72,256]{1,0:T(8,128)S(1)} %add_add_fusion.2), channel_id=1, source_target_pairs={{0,16},{2,6},{4,20},{6,2},{8,24},{10,14},{12,28},{14,10},{16,0},{1... | collective-permute-start | bytes 221192 | tf_op jit(solution)/shard_map/ppermute | solution.py:37
  68.5 7.9 %collective-permute-start.19 = (f32[72,256]{1,0:T(8,128)S(1)}, f32[72,256]{1,0:T(8,128)S(1)}, u32[]{:S(2)}, u32[]{:S(2)}) collective-permute-start(f32[72,256]{1,0:T(8,128)S(1)} %add_add_fusion.2), channel_id=1, source_target_pairs={{0,32},{2,10},{4,36},{6,14},{8,40},{10,2},{12,44},{14,6},{16,48},{... | collective-permute-start | bytes 221192 | tf_op jit(solution)/shard_map/ppermute | solution.py:37
  69.6 6.8 %collective-permute-start.20 = (f32[72,256]{1,0:T(8,128)S(1)}, f32[72,256]{1,0:T(8,128)S(1)}, u32[]{:S(2)}, u32[]{:S(2)}) collective-permute-start(f32[72,256]{1,0:T(8,128)S(1)} %add_add_fusion.2), channel_id=1, source_target_pairs={{0,48},{2,14},{4,52},{6,10},{8,56},{10,6},{12,60},{14,2},{16,32},{... | collective-permute-start | bytes 221192 | tf_op jit(solution)/shard_map/ppermute | solution.py:37
  76.4 3.9 %collective-permute-start.21 = (f32[72,256]{1,0:T(8,128)S(1)}, f32[72,256]{1,0:T(8,128)S(1)}, u32[]{:S(2)}, u32[]{:S(2)}) collective-permute-start(f32[72,256]{1,0:T(8,128)S(1)} %add_add_fusion.1), channel_id=1, source_target_pairs={{0,64},{2,18},{4,68},{6,22},{8,72},{10,26},{12,76},{14,30},{16,80}... | collective-permute-start | bytes 221192 | tf_op jit(solution)/shard_map/ppermute | solution.py:37
  76.5 4.8 %collective-permute-start.22 = (f32[72,256]{1,0:T(8,128)S(1)}, f32[72,256]{1,0:T(8,128)S(1)}, u32[]{:S(2)}, u32[]{:S(2)}) collective-permute-start(f32[72,256]{1,0:T(8,128)S(1)} %add_add_fusion.1), channel_id=1, source_target_pairs={{0,128},{2,34},{4,132},{6,38},{8,136},{10,42},{12,140},{14,46},{16... | collective-permute-start | bytes 221192 | tf_op jit(solution)/shard_map/ppermute | solution.py:37
  78.8 4.4 %collective-permute-start.23 = (f32[72,256]{1,0:T(8,128)S(1)}, f32[72,256]{1,0:T(8,128)S(1)}, u32[]{:S(2)}, u32[]{:S(2)}) collective-permute-start(f32[72,256]{1,0:T(8,128)S(1)} %add_add_fusion.1), channel_id=1, source_target_pairs={{0,192},{2,50},{4,196},{6,54},{8,200},{10,58},{12,204},{14,62},{16... | collective-permute-start | bytes 221192 | tf_op jit(solution)/shard_map/ppermute | solution.py:37
  83.3 6.6 %collective-permute-start.24 = (f32[72,256]{1,0:T(8,128)S(1)}, f32[72,256]{1,0:T(8,128)S(1)}, u32[]{:S(2)}, u32[]{:S(2)}) collective-permute-start(f32[72,256]{1,0:T(8,128)S(1)} %add_add_fusion.own), channel_id=1, source_target_pairs={{0,2},{2,0},{1,3},{3,1},{4,6},{6,4},{5,7},{7,5},{8,10},{10,8},{9,1... | collective-permute-start | bytes 221192 | tf_op jit(solution)/shard_map/ppermute | solution.py:24
  (7 other events, 66.2 us)

commit v5 on v4

--- a/solution.py
+++ b/solution.py
@@ -37,10 +37,10 @@
     return lax.ppermute(value, names, pairs)
 
 
-def reorder_kernel(rep, order, features, own):
+def reorder_kernel(order, features, own):
     half = own.shape[0]
     nodes = features.shape[0]
-    wanted = order[pl.ds(rep[0], 1), :] & (nodes - 1)
+    wanted = order[pl.ds(lax.axis_index("rep"), 1), :] & (nodes - 1)
     pick = (lax.broadcasted_iota(jnp.int32, (nodes, half), 0) == wanted).astype(jnp.bfloat16)
     own[...] = lax.dot_general(
         pick, features[...], (((0,), (0,)), ((), ())), preferred_element_type=jnp.float32
@@ -211,15 +211,14 @@
     part = width // 2
     me = lax.axis_index(ROWS)
     core = lax.axis_index("c").reshape(1)
-    rep = lax.axis_index("rep").reshape(1)
     order = node_order.reshape(2, nodes // 2)
     own = pl.pallas_call(
         reorder_kernel,
         out_shape=jax.ShapeDtypeStruct((nodes // 2, width), jnp.bfloat16),
-        in_specs=[SMEM, VMEM, VMEM],
+        in_specs=[VMEM, VMEM],
         out_specs=VMEM,
         compiler_params=pltpu.CompilerParams(vmem_limit_bytes=56 * 2**20),
-    )(rep, order, features)
+    )(order, features)
 
     mine = aggregated(own, me, tile_vals, tile_row, tile_col, tile_count)
     theirs = swap(mine, "rep", 1)

time: 90.9 us -> 89.9 us (0.989)
  starting transfers between devices: 45.6 us -> 42.4 us
  Pallas kernels: 10.6 us -> 13.5 us
    ppermute x10, starting transfers between devices: 24.1 us -> 20.9 us  [swap(): return lax.ppermute(value, axis, [(i, i ^ step) for i in range(n)])]
    pallas_call x3, Pallas kernels: 4.58 us -> 6.35 us  [products(): pl.pallas_call(functools.partial(tiles_kernel, kind), out_shape=jax.Shape...]
    pallas_call x1, Pallas kernels: 2.56 us -> 3.7 us  [aggregated(): pl.pallas_call(plan_kernel, out_shape=(entries, entries, jax.ShapeDtypeSt...]
    ppermute x15, waiting for transfers between devices: 18.5 us -> 17.4 us  [swap_by_core(): return lax.ppermute(value, names, pairs)]
  transfers between devices with their start and end apart: 25 -> 25, of which waited for: 13 -> 13; matrix products, arithmetic and copies ran while one was open for 1% -> 1% of each run, Pallas kernels for 6% -> 8%
where the time goes in v5:
time: 89.9 us; the launch traced here: 90.1 us
  starting transfers between devices  42.4 us (47%)
  waiting for transfers between devices  28.3 us (31%)
  Pallas kernels  13.5 us (15%)
  local copies, waits for them, and re-layouts  3.63 us (4%)
  between operations  1.47 us (2%)
    ppermute x15, starting transfers between devices, swap_by_core(): return lax.ppermute(value, names, pairs)  21.4 us
    ppermute x10, starting transfers between devices, swap(): return lax.ppermute(value, axis, [(i, i ^ step) for i in range(n)])  20.9 us
    ppermute x15, waiting for transfers between devices, swap_by_core(): return lax.ppermute(value, names, pairs)  17.4 us
    ppermute x10, waiting for transfers between devices, swap(): return lax.ppermute(value, axis, [(i, i ^ step) for i in range(n)])  10.9 us
    pallas_call x3, Pallas kernels, products(): pl.pallas_call(functools.partial(tiles_kernel, kind), out_shape=jax.Shape...  6.35 us
    pallas_call x1, Pallas kernels, aggregated(): pl.pallas_call(plan_kernel, out_shape=(entries, entries, jax.ShapeDtypeSt...  3.7 us
    unnamed x12, local copies, waits for them, and re-layouts  3.63 us
  transfers between devices with their start and end apart: 25, of which 13 were waited for; matrix products, arithmetic and copies ran while one was open for 1% of the time, Pallas kernels for 8%

profile of v5, /device:TPU:1, one launch (start us, length us, event | category | flops | bytes accessed | tf_op | source)
XLA Modules:
  0.0 90.1 jit_solution(16344595142302440118)
XLA Ops:
  0.6 1.7 %shard_map.112 = bf16[128,128]{1,0:T(8,128)(2,1)} custom-call(s32[2,128]{1,0:T(2,128)} %bitcast.9, bf16[256,128]{1,0:T(8,128)(2,1)} %features.1), custom_call_target="tpu_custom_call" | custom-call | tf_op jit(solution)/shard_map/pallas_call | solution.py:215
  2.3 3.8 %collective-permute-start = (bf16[1,128,128]{2,1,0:T(8,128)(2,1)}, bf16[1,128,128]{2,1,0:T(8,128)(2,1)S(1)}, u32[]{:S(2)}, u32[]{:S(2)}) collective-permute-start(bf16[1,128,128]{2,1,0:T(8,128)(2,1)} %bitcast.5), channel_id=1, source_target_pairs={{0,4},{4,0},{8,12},{12,8},{1,5},{5,1},{9,13},{13,9},{2,6},{6,2},{1... | collective-permute-start | bytes 98312 | tf_op jit(solution)/shard_map/ppermute | solution.py:24
  6.1 5.1 %collective-permute-start.1 = (bf16[1,128,128]{2,1,0:T(8,128)(2,1)}, bf16[1,128,128]{2,1,0:T(8,128)(2,1)S(1)}, u32[]{:S(2)}, u32[]{:S(2)}) collective-permute-start(bf16[1,128,128]{2,1,0:T(8,128)(2,1)} %bitcast.6), channel_id=1, source_target_pairs={{0,8},{4,12},{8,0},{12,4},{1,9},{5,13},{9,1},{13,5},{2,10},{6,14},... | collective-permute-start | bytes 98312 | tf_op jit(solution)/shard_map/ppermute | solution.py:24
  13.1 3.2 %collective-permute-done.2 = bf16[1,128,128]{2,1,0:T(8,128)(2,1)S(1)} collective-permute-done((bf16[1,128,128]{2,1,0:T(8,128)(2,1)}, bf16[1,128,128]{2,1,0:T(8,128)(2,1)S(1)}, u32[]{:S(2)}, u32[]{:S(2)}) %collective-permute-start.2) | collective-permute-done | bytes 32800 | tf_op jit(solution)/shard_map/ppermute | solution.py:24
  17.7 2.4 %collective-permute-start.4 = (bf16[4,128,128]{2,1,0:T(8,128)(2,1)S(1)}, bf16[4,128,128]{2,1,0:T(8,128)(2,1)S(1)}, u32[]{:S(2)}, u32[]{:S(2)}) collective-permute-start(bf16[4,128,128]{2,1,0:T(8,128)(2,1)S(1)} %pad_maximum_fusion.1), channel_id=1, source_target_pairs={{0,32},{2,130},{4,36},{6,134},{8,40},{10,138},{12,44},{14,142},{16... | collective-permute-start | bytes 393224 | tf_op jit(solution)/shard_map/ppermute | solution.py:37
  20.3 3.6 %collective-permute-done.4 = bf16[4,128,128]{2,1,0:T(8,128)(2,1)S(1)} collective-permute-done((bf16[4,128,128]{2,1,0:T(8,128)(2,1)S(1)}, bf16[4,128,128]{2,1,0:T(8,128)(2,1)S(1)}, u32[]{:S(2)}, u32[]{:S(2)}) %collective-permute-start.4) | collective-permute-done | bytes 131104 | tf_op jit(solution)/shard_map/ppermute | solution.py:37
  25.3 4.3 %collective-permute-start.7 = (bf16[16,128,128]{2,1,0:T(8,128)(2,1)S(1)}, bf16[16,128,128]{2,1,0:T(8,128)(2,1)S(1)}, u32[]{:S(2)}, u32[]{:S(2)}) collective-permute-start(bf16[16,128,128]{2,1,0:T(8,128)(2,1)S(1)} %pad_maximum_fusion.refs_0_), channel_id=1, source_target_pairs={{0,2},{2,0},{1,3},{3,1},{4,6},{6,4},{5,7},{7,5},{8,10},{10,8},{9,1... | collective-permute-start | bytes 1572872 | tf_op jit(solution)/shard_map/ppermute | solution.py:24
  30.3 3.2 %collective-permute-start.9 = (bf16[16,128,128]{2,1,0:T(8,128)(2,1)S(1)}, bf16[16,128,128]{2,1,0:T(8,128)(2,1)S(1)}, u32[]{:S(2)}, u32[]{:S(2)}) collective-permute-start(bf16[16,128,128]{2,1,0:T(8,128)(2,1)S(1)} %pad_maximum_fusion.refs_0_), channel_id=1, source_target_pairs={{0,128},{2,34},{4,132},{6,38},{8,136},{10,42},{12,140},{14,46},{16... | collective-permute-start | bytes 1572872 | tf_op jit(solution)/shard_map/ppermute | solution.py:37
  34.9 3.7 %shard_map.114 = (s32[1248]{0:T(1024)S(1)}, s32[1248]{0:T(1024)S(1)}, s32[6]{0:T(128)S(1)}) custom-call(s32[192]{0:T(256)S(1)} %get-tuple-element.28.kind, s32[192]{0:T(256)S(1)} %get-tuple-element.27.place, s32[1]{0:T(128)S(6)} %copy.12.count), custom_call_target="tpu_custom_call" | custom-call | tf_op jit(solution)/shard_map/pallas_call | solution.py:193
  38.6 2.8 %copy-done = bf16[192,128,128]{2,1,0:T(8,128)(2,1)S(1)} copy-done((bf16[192,128,128]{2,1,0:T(8,128)(2,1)S(1)}, bf16[192,128,128]{2,1,0:T(8,128)(2,1)}, u32[]{:S(2)}) %copy-start) | copy-done | bytes 6291480
  41.4 1.7 %shard_map.115.refs_0_ = f32[256,128]{1,0:T(8,128)S(1)} custom-call(s32[1248]{0:T(1024)S(1)} %get-tuple-element.17.order, s32[1248]{0:T(1024)S(1)} %get-tuple-element.18.spot, s32[6]{0:T(128)S(1)} %get-tuple-element.19.groups, bf16[192,128,128]{2,1,0:T(8,128)(2,1)S(1)} %copy-done, bf16[16,128,128]{2,1,0:T(8,128)(2,1)S(1)} %pad_maximum_fusion.refs_0_, ...), custom_call_target="tpu_custom_call" | custom-call | flops 268435456 | bytes 2097152 | tf_op jit(solution)/shard_map/pallas_call | solution.py:164
  43.7 2.2 %collective-permute-done.9.refs_2_ = bf16[16,128,128]{2,1,0:T(8,128)(2,1)S(1)} collective-permute-done((bf16[16,128,128]{2,1,0:T(8,128)(2,1)S(1)}, bf16[16,128,128]{2,1,0:T(8,128)(2,1)S(1)}, u32[]{:S(2)}, u32[]{:S(2)}) %collective-permute-start.9) | collective-permute-done | bytes 524320 | tf_op jit(solution)/shard_map/ppermute | solution.py:37
  47.2 2.0 %shard_map.116.refs_0_ = f32[256,128]{1,0:T(8,128)S(1)} custom-call(s32[1248]{0:T(1024)S(1)} %get-tuple-element.17.order, s32[1248]{0:T(1024)S(1)} %get-tuple-element.18.spot, s32[6]{0:T(128)S(1)} %get-tuple-element.19.groups, bf16[192,128,128]{2,1,0:T(8,128)(2,1)S(1)} %copy-done, f32[256,128]{1,0:T(8,128)S(1)} %shard_map.115.refs_0_, ...), custom_call_target="tpu_custom_call" | custom-call | flops 268435456 | bytes 2097152 | tf_op jit(solution)/shard_map/pallas_call | solution.py:164
  49.3 2.6 %shard_map.117.mine = f32[256,128]{1,0:T(8,128)S(1)} custom-call(s32[1248]{0:T(1024)S(1)} %get-tuple-element.17.order, s32[1248]{0:T(1024)S(1)} %get-tuple-element.18.spot, s32[6]{0:T(128)S(1)} %get-tuple-element.19.groups, bf16[192,128,128]{2,1,0:T(8,128)(2,1)S(1)} %copy-done, f32[256,128]{1,0:T(8,128)S(1)} %shard_map.116.refs_0_, ...), custom_call_target="tpu_custom_call" | custom-call | flops 268435456 | bytes 2097152 | tf_op jit(solution)/shard_map/pallas_call | solution.py:164
  52.1 4.8 %collective-permute-done.13.theirs = f32[256,128]{1,0:T(8,128)S(1)} collective-permute-done((f32[256,128]{1,0:T(8,128)S(1)}, f32[256,128]{1,0:T(8,128)S(1)}, u32[]{:S(2)}, u32[]{:S(2)}) %collective-permute-start.13) | collective-permute-done | bytes 131104 | tf_op jit(solution)/shard_map/ppermute | solution.py:24
  59.4 3.0 %collective-permute-start.16 = (f32[72,256]{1,0:T(8,128)S(1)}, f32[72,256]{1,0:T(8,128)S(1)}, u32[]{:S(2)}, u32[]{:S(2)}) collective-permute-start(f32[72,256]{1,0:T(8,128)S(1)} %add.59), channel_id=1, source_target_pairs={{0,8},{2,130},{4,12},{6,134},{8,0},{10,138},{12,4},{14,142},{16,24... | collective-permute-start | bytes 221192 | tf_op jit(solution)/shard_map/ppermute | solution.py:37
  63.3 1.7 %collective-permute-done.16 = f32[72,256]{1,0:T(8,128)S(1)} collective-permute-done((f32[72,256]{1,0:T(8,128)S(1)}, f32[72,256]{1,0:T(8,128)S(1)}, u32[]{:S(2)}, u32[]{:S(2)}) %collective-permute-start.16) | collective-permute-done | bytes 73760 | tf_op jit(solution)/shard_map/ppermute | solution.py:37
  65.0 1.9 %collective-permute-done.17 = f32[72,256]{1,0:T(8,128)S(1)} collective-permute-done((f32[72,256]{1,0:T(8,128)S(1)}, f32[72,256]{1,0:T(8,128)S(1)}, u32[]{:S(2)}, u32[]{:S(2)}) %collective-permute-start.17) | collective-permute-done | bytes 73760 | tf_op jit(solution)/shard_map/ppermute | solution.py:37
  66.9 2.2 %collective-permute-start.18 = (f32[72,256]{1,0:T(8,128)S(1)}, f32[72,256]{1,0:T(8,128)S(1)}, u32[]{:S(2)}, u32[]{:S(2)}) collective-permute-start(f32[72,256]{1,0:T(8,128)S(1)} %add_add_fusion.2), channel_id=1, source_target_pairs={{0,16},{2,6},{4,20},{6,2},{8,24},{10,14},{12,28},{14,10},{16,0},{1... | collective-permute-start | bytes 221192 | tf_op jit(solution)/shard_map/ppermute | solution.py:37
  69.6 3.0 %collective-permute-start.20 = (f32[72,256]{1,0:T(8,128)S(1)}, f32[72,256]{1,0:T(8,128)S(1)}, u32[]{:S(2)}, u32[]{:S(2)}) collective-permute-start(f32[72,256]{1,0:T(8,128)S(1)} %add_add_fusion.2), channel_id=1, source_target_pairs={{0,48},{2,14},{4,52},{6,10},{8,56},{10,6},{12,60},{14,2},{16,32},{... | collective-permute-start | bytes 221192 | tf_op jit(solution)/shard_map/ppermute | solution.py:37
  72.6 4.1 %collective-permute-done.19 = f32[72,256]{1,0:T(8,128)S(1)} collective-permute-done((f32[72,256]{1,0:T(8,128)S(1)}, f32[72,256]{1,0:T(8,128)S(1)}, u32[]{:S(2)}, u32[]{:S(2)}) %collective-permute-start.19) | collective-permute-done | bytes 73760 | tf_op jit(solution)/shard_map/ppermute | solution.py:37
  76.8 2.0 %collective-permute-start.22 = (f32[72,256]{1,0:T(8,128)S(1)}, f32[72,256]{1,0:T(8,128)S(1)}, u32[]{:S(2)}, u32[]{:S(2)}) collective-permute-start(f32[72,256]{1,0:T(8,128)S(1)} %add_add_fusion.1), channel_id=1, source_target_pairs={{0,128},{2,34},{4,132},{6,38},{8,136},{10,42},{12,140},{14,46},{16... | collective-permute-start | bytes 221192 | tf_op jit(solution)/shard_map/ppermute | solution.py:37
  78.8 1.8 %collective-permute-start.23 = (f32[72,256]{1,0:T(8,128)S(1)}, f32[72,256]{1,0:T(8,128)S(1)}, u32[]{:S(2)}, u32[]{:S(2)}) collective-permute-start(f32[72,256]{1,0:T(8,128)S(1)} %add_add_fusion.1), channel_id=1, source_target_pairs={{0,192},{2,50},{4,196},{6,54},{8,200},{10,58},{12,204},{14,62},{16... | collective-permute-start | bytes 221192 | tf_op jit(solution)/shard_map/ppermute | solution.py:37
  83.3 5.2 %collective-permute-start.24 = (f32[72,256]{1,0:T(8,128)S(1)}, f32[72,256]{1,0:T(8,128)S(1)}, u32[]{:S(2)}, u32[]{:S(2)}) collective-permute-start(f32[72,256]{1,0:T(8,128)S(1)} %add_add_fusion.own), channel_id=1, source_target_pairs={{0,2},{2,0},{1,3},{3,1},{4,6},{6,4},{5,7},{7,5},{8,10},{10,8},{9,1... | collective-permute-start | bytes 221192 | tf_op jit(solution)/shard_map/ppermute | solution.py:24
  (53 shorter events, 16.5 us)
Async XLA Ops:
  2.3 9.8 %collective-permute-start = (bf16[1,128,128]{2,1,0:T(8,128)(2,1)}, bf16[1,128,128]{2,1,0:T(8,128)(2,1)S(1)}, u32[]{:S(2)}, u32[]{:S(2)}) collective-permute-start(bf16[1,128,128]{2,1,0:T(8,128)(2,1)} %bitcast.5), channel_id=1, source_target_pairs={{0,4},{4,0},{8,12},{12,8},{1,5},{5,1},{9,13},{13,9},{2,6},{6,2},{1... | collective-permute-start | bytes 98312 | tf_op jit(solution)/shard_map/ppermute | solution.py:24
  6.1 7.0 %collective-permute-start.1 = (bf16[1,128,128]{2,1,0:T(8,128)(2,1)}, bf16[1,128,128]{2,1,0:T(8,128)(2,1)S(1)}, u32[]{:S(2)}, u32[]{:S(2)}) collective-permute-start(bf16[1,128,128]{2,1,0:T(8,128)(2,1)} %bitcast.6), channel_id=1, source_target_pairs={{0,8},{4,12},{8,0},{12,4},{1,9},{5,13},{9,1},{13,5},{2,10},{6,14},... | collective-permute-start | bytes 98312 | tf_op jit(solution)/shard_map/ppermute | solution.py:24
  11.2 5.1 %collective-permute-start.2 = (bf16[1,128,128]{2,1,0:T(8,128)(2,1)}, bf16[1,128,128]{2,1,0:T(8,128)(2,1)S(1)}, u32[]{:S(2)}, u32[]{:S(2)}) collective-permute-start(bf16[1,128,128]{2,1,0:T(8,128)(2,1)} %bitcast.7), channel_id=1, source_target_pairs={{0,12},{4,8},{8,4},{12,0},{1,13},{5,9},{9,5},{13,1},{2,14},{6,10},... | collective-permute-start | bytes 98312 | tf_op jit(solution)/shard_map/ppermute | solution.py:24
  16.4 3.9 %collective-permute-start.3 = (bf16[4,128,128]{2,1,0:T(8,128)(2,1)S(1)}, bf16[4,128,128]{2,1,0:T(8,128)(2,1)S(1)}, u32[]{:S(2)}, u32[]{:S(2)}) collective-permute-start(bf16[4,128,128]{2,1,0:T(8,128)(2,1)S(1)} %pad_maximum_fusion.1), channel_id=1, source_target_pairs={{0,16},{2,66},{4,20},{6,70},{8,24},{10,74},{12,28},{14,78},{16,0},... | collective-permute-start | bytes 393224 | tf_op jit(solution)/shard_map/ppermute | solution.py:37
  17.7 6.2 %collective-permute-start.4 = (bf16[4,128,128]{2,1,0:T(8,128)(2,1)S(1)}, bf16[4,128,128]{2,1,0:T(8,128)(2,1)S(1)}, u32[]{:S(2)}, u32[]{:S(2)}) collective-permute-start(bf16[4,128,128]{2,1,0:T(8,128)(2,1)S(1)} %pad_maximum_fusion.1), channel_id=1, source_target_pairs={{0,32},{2,130},{4,36},{6,134},{8,40},{10,138},{12,44},{14,142},{16... | collective-permute-start | bytes 393224 | tf_op jit(solution)/shard_map/ppermute | solution.py:37
  20.1 5.2 %collective-permute-start.5 = (bf16[4,128,128]{2,1,0:T(8,128)(2,1)S(1)}, bf16[4,128,128]{2,1,0:T(8,128)(2,1)S(1)}, u32[]{:S(2)}, u32[]{:S(2)}) collective-permute-start(bf16[4,128,128]{2,1,0:T(8,128)(2,1)S(1)} %pad_maximum_fusion.1), channel_id=1, source_target_pairs={{0,48},{2,194},{4,52},{6,198},{8,56},{10,202},{12,60},{14,206},{16... | collective-permute-start | bytes 393224 | tf_op jit(solution)/shard_map/ppermute | solution.py:37
  25.3 13.2 %collective-permute-start.7 = (bf16[16,128,128]{2,1,0:T(8,128)(2,1)S(1)}, bf16[16,128,128]{2,1,0:T(8,128)(2,1)S(1)}, u32[]{:S(2)}, u32[]{:S(2)}) collective-permute-start(bf16[16,128,128]{2,1,0:T(8,128)(2,1)S(1)} %pad_maximum_fusion.refs_0_), channel_id=1, source_target_pairs={{0,2},{2,0},{1,3},{3,1},{4,6},{6,4},{5,7},{7,5},{8,10},{10,8},{9,1... | collective-permute-start | bytes 1572872 | tf_op jit(solution)/shard_map/ppermute | solution.py:24
  29.6 13.5 %collective-permute-start.6 = (bf16[16,128,128]{2,1,0:T(8,128)(2,1)S(1)}, bf16[16,128,128]{2,1,0:T(8,128)(2,1)S(1)}, u32[]{:S(2)}, u32[]{:S(2)}) collective-permute-start(bf16[16,128,128]{2,1,0:T(8,128)(2,1)S(1)} %pad_maximum_fusion.refs_0_), channel_id=1, source_target_pairs={{0,192},{2,50},{4,196},{6,54},{8,200},{10,58},{12,204},{14,62},{16... | collective-permute-start | bytes 1572872 | tf_op jit(solution)/shard_map/ppermute | solution.py:37
  30.3 12.9 %collective-permute-start.8 = (bf16[16,128,128]{2,1,0:T(8,128)(2,1)S(1)}, bf16[16,128,128]{2,1,0:T(8,128)(2,1)S(1)}, u32[]{:S(2)}, u32[]{:S(2)}) collective-permute-start(bf16[16,128,128]{2,1,0:T(8,128)(2,1)S(1)} %pad_maximum_fusion.refs_0_), channel_id=1, source_target_pairs={{0,64},{2,18},{4,68},{6,22},{8,72},{10,26},{12,76},{14,30},{16,80}... | collective-permute-start | bytes 1572872 | tf_op jit(solution)/shard_map/ppermute | solution.py:37
  30.3 15.6 %collective-permute-start.9 = (bf16[16,128,128]{2,1,0:T(8,128)(2,1)S(1)}, bf16[16,128,128]{2,1,0:T(8,128)(2,1)S(1)}, u32[]{:S(2)}, u32[]{:S(2)}) collective-permute-start(bf16[16,128,128]{2,1,0:T(8,128)(2,1)S(1)} %pad_maximum_fusion.refs_0_), channel_id=1, source_target_pairs={{0,128},{2,34},{4,132},{6,38},{8,136},{10,42},{12,140},{14,46},{16... | collective-permute-start | bytes 1572872 | tf_op jit(solution)/shard_map/ppermute | solution.py:37
  43.1 6.1 %collective-permute-start.12 = (bf16[16,128,128]{2,1,0:T(8,128)(2,1)S(1)}, bf16[16,128,128]{2,1,0:T(8,128)(2,1)S(1)}, u32[]{:S(2)}, u32[]{:S(2)}) collective-permute-start(bf16[16,128,128]{2,1,0:T(8,128)(2,1)S(1)} %collective-permute-done.6.refs_3_), channel_id=1, source_target_pairs={{0,2},{2,0},{1,3},{3,1},{4,6},{6,4},{5,7},{7,5},{8,10},{10,8},{9,1... | collective-permute-start | bytes 1572872 | tf_op jit(solution)/shard_map/ppermute | solution.py:24
  43.3 6.0 %collective-permute-start.10 = (bf16[16,128,128]{2,1,0:T(8,128)(2,1)S(1)}, bf16[16,128,128]{2,1,0:T(8,128)(2,1)S(1)}, u32[]{:S(2)}, u32[]{:S(2)}) collective-permute-start(bf16[16,128,128]{2,1,0:T(8,128)(2,1)S(1)} %collective-permute-done.8.refs_1_), channel_id=1, source_target_pairs={{0,2},{2,0},{1,3},{3,1},{4,6},{6,4},{5,7},{7,5},{8,10},{10,8},{9,1... | collective-permute-start | bytes 1572872 | tf_op jit(solution)/shard_map/ppermute | solution.py:24
  46.0 3.3 %collective-permute-start.11 = (bf16[16,128,128]{2,1,0:T(8,128)(2,1)S(1)}, bf16[16,128,128]{2,1,0:T(8,128)(2,1)S(1)}, u32[]{:S(2)}, u32[]{:S(2)}) collective-permute-start(bf16[16,128,128]{2,1,0:T(8,128)(2,1)S(1)} %collective-permute-done.9.refs_2_), channel_id=1, source_target_pairs={{0,2},{2,0},{1,3},{3,1},{4,6},{6,4},{5,7},{7,5},{8,10},{10,8},{9,1... | collective-permute-start | bytes 1572872 | tf_op jit(solution)/shard_map/ppermute | solution.py:24
  51.9 5.0 %collective-permute-start.13 = (f32[256,128]{1,0:T(8,128)S(1)}, f32[256,128]{1,0:T(8,128)S(1)}, u32[]{:S(2)}, u32[]{:S(2)}) collective-permute-start(f32[256,128]{1,0:T(8,128)S(1)} %shard_map.117.mine), channel_id=1, source_target_pairs={{0,1},{1,0},{2,3},{3,2},{4,5},{5,4},{6,7},{7,6},{8,9},{9,8},{10,11... | collective-permute-start | bytes 393224 | tf_op jit(solution)/shard_map/ppermute | solution.py:24
  59.3 4.0 %collective-permute-start.15 = (f32[72,256]{1,0:T(8,128)S(1)}, f32[72,256]{1,0:T(8,128)S(1)}, u32[]{:S(2)}, u32[]{:S(2)}) collective-permute-start(f32[72,256]{1,0:T(8,128)S(1)} %add.59), channel_id=1, source_target_pairs={{0,4},{2,66},{4,0},{6,70},{8,12},{10,74},{12,8},{14,78},{16,20},{1... | collective-permute-start | bytes 221192 | tf_op jit(solution)/shard_map/ppermute | solution.py:37
  59.4 5.5 %collective-permute-start.16 = (f32[72,256]{1,0:T(8,128)S(1)}, f32[72,256]{1,0:T(8,128)S(1)}, u32[]{:S(2)}, u32[]{:S(2)}) collective-permute-start(f32[72,256]{1,0:T(8,128)S(1)} %add.59), channel_id=1, source_target_pairs={{0,8},{2,130},{4,12},{6,134},{8,0},{10,138},{12,4},{14,142},{16,24... | collective-permute-start | bytes 221192 | tf_op jit(solution)/shard_map/ppermute | solution.py:37
  62.5 4.4 %collective-permute-start.17 = (f32[72,256]{1,0:T(8,128)S(1)}, f32[72,256]{1,0:T(8,128)S(1)}, u32[]{:S(2)}, u32[]{:S(2)}) collective-permute-start(f32[72,256]{1,0:T(8,128)S(1)} %add.59), channel_id=1, source_target_pairs={{0,12},{2,194},{4,8},{6,198},{8,4},{10,202},{12,0},{14,206},{16,28... | collective-permute-start | bytes 221192 | tf_op jit(solution)/shard_map/ppermute | solution.py:37
  66.9 5.8 %collective-permute-start.18 = (f32[72,256]{1,0:T(8,128)S(1)}, f32[72,256]{1,0:T(8,128)S(1)}, u32[]{:S(2)}, u32[]{:S(2)}) collective-permute-start(f32[72,256]{1,0:T(8,128)S(1)} %add_add_fusion.2), channel_id=1, source_target_pairs={{0,16},{2,6},{4,20},{6,2},{8,24},{10,14},{12,28},{14,10},{16,0},{1... | collective-permute-start | bytes 221192 | tf_op jit(solution)/shard_map/ppermute | solution.py:37
  69.1 7.6 %collective-permute-start.19 = (f32[72,256]{1,0:T(8,128)S(1)}, f32[72,256]{1,0:T(8,128)S(1)}, u32[]{:S(2)}, u32[]{:S(2)}) collective-permute-start(f32[72,256]{1,0:T(8,128)S(1)} %add_add_fusion.2), channel_id=1, source_target_pairs={{0,32},{2,10},{4,36},{6,14},{8,40},{10,2},{12,44},{14,6},{16,48},{... | collective-permute-start | bytes 221192 | tf_op jit(solution)/shard_map/ppermute | solution.py:37
  69.6 7.1 %collective-permute-start.20 = (f32[72,256]{1,0:T(8,128)S(1)}, f32[72,256]{1,0:T(8,128)S(1)}, u32[]{:S(2)}, u32[]{:S(2)}) collective-permute-start(f32[72,256]{1,0:T(8,128)S(1)} %add_add_fusion.2), channel_id=1, source_target_pairs={{0,48},{2,14},{4,52},{6,10},{8,56},{10,6},{12,60},{14,2},{16,32},{... | collective-permute-start | bytes 221192 | tf_op jit(solution)/shard_map/ppermute | solution.py:37
  76.7 3.9 %collective-permute-start.21 = (f32[72,256]{1,0:T(8,128)S(1)}, f32[72,256]{1,0:T(8,128)S(1)}, u32[]{:S(2)}, u32[]{:S(2)}) collective-permute-start(f32[72,256]{1,0:T(8,128)S(1)} %add_add_fusion.1), channel_id=1, source_target_pairs={{0,64},{2,18},{4,68},{6,22},{8,72},{10,26},{12,76},{14,30},{16,80}... | collective-permute-start | bytes 221192 | tf_op jit(solution)/shard_map/ppermute | solution.py:37
  76.8 4.8 %collective-permute-start.22 = (f32[72,256]{1,0:T(8,128)S(1)}, f32[72,256]{1,0:T(8,128)S(1)}, u32[]{:S(2)}, u32[]{:S(2)}) collective-permute-start(f32[72,256]{1,0:T(8,128)S(1)} %add_add_fusion.1), channel_id=1, source_target_pairs={{0,128},{2,34},{4,132},{6,38},{8,136},{10,42},{12,140},{14,46},{16... | collective-permute-start | bytes 221192 | tf_op jit(solution)/shard_map/ppermute | solution.py:37
  78.8 4.4 %collective-permute-start.23 = (f32[72,256]{1,0:T(8,128)S(1)}, f32[72,256]{1,0:T(8,128)S(1)}, u32[]{:S(2)}, u32[]{:S(2)}) collective-permute-start(f32[72,256]{1,0:T(8,128)S(1)} %add_add_fusion.1), channel_id=1, source_target_pairs={{0,192},{2,50},{4,196},{6,54},{8,200},{10,58},{12,204},{14,62},{16... | collective-permute-start | bytes 221192 | tf_op jit(solution)/shard_map/ppermute | solution.py:37
  83.3 6.1 %collective-permute-start.24 = (f32[72,256]{1,0:T(8,128)S(1)}, f32[72,256]{1,0:T(8,128)S(1)}, u32[]{:S(2)}, u32[]{:S(2)}) collective-permute-start(f32[72,256]{1,0:T(8,128)S(1)} %add_add_fusion.own), channel_id=1, source_target_pairs={{0,2},{2,0},{1,3},{3,1},{4,6},{6,4},{5,7},{7,5},{8,10},{10,8},{9,1... | collective-permute-start | bytes 221192 | tf_op jit(solution)/shard_map/ppermute | solution.py:24
  (7 other events, 60.3 us)
